TPU v7x, 32 devices: a whole 2x2x4 slice. The times are simulated.
32 devices in a mesh: dp: 8 (over z, y), mp: 4 (over x, core).
Axes of the slice: x: 2, y: 2, z: 4, core: 2. Of those that a mesh axis runs over, the one named last changes fastest.
Arguments:
- tokens: bfloat16 [32768, 512], P(('dp', 'mp')), may hold values from -6 to 6
- sentence_ids: int32 [32768], P(('dp', 'mp')), may hold values from 0 to 2047, as said below
- validity: int32 [32768], P(('dp', 'mp')), may hold values from 0 to 1, as said below
- expert_ids: int32 [32768, 2], P(('dp', 'mp')), may hold values from 0 to 7, all different within a row
- cotangent: bfloat16 [32768, 512], P(('dp', 'mp')), may hold values from -6 to 6
- first_gain: bfloat16 [512], replicated, may hold values from 0.5 to 1.5
- first_shift: bfloat16 [512], replicated, may hold values from -1.5 to 1.5
- router: bfloat16 [512, 8], replicated, may hold values from -0.25 to 0.25
- query_weight: bfloat16 [512, 512], replicated, may hold values from -0.25 to 0.25
- output_weight: bfloat16 [512, 512], replicated, may hold values from -6 to 6
- keyval_weight: bfloat16 [512, 128], replicated, may hold values from -0.25 to 0.25
- second_gain: bfloat16 [512], replicated, may hold values from 0.5 to 1.5
- second_shift: bfloat16 [512], replicated, may hold values from -1.5 to 1.5
- expand_weight: bfloat16 [512, 2048], P(None, 'mp'), may hold values from -0.25 to 0.25
- expand_bias: bfloat16 [2048], P('mp'), may hold values from -1.5 to 1.5
- contract_weight: bfloat16 [2048, 512], P('mp'), may hold values from -0.125 to 0.125
- contract_bias: bfloat16 [512], replicated, may hold values from -1.5 to 1.5
Outputs:
- layer_output: bfloat16 [32768, 512], P(('dp', 'mp'))
- tokens_gradient: bfloat16 [32768, 512], P(('dp', 'mp'))
- first_gain_grad: float32 [512], replicated
- first_shift_grad: float32 [512], replicated
- router_grad: float32 [512, 8], replicated
- query_grad: float32 [512, 512], replicated
- output_grad: float32 [512, 512], replicated
- keyval_grad: float32 [512, 128], replicated
- second_gain_grad: float32 [512], replicated
- second_shift_grad: float32 [512], replicated
- expand_grad: float32 [512, 2048], P(None, 'mp')
- expand_bias_grad: float32 [2048], P('mp')
- contract_grad: float32 [2048, 512], P('mp')
- contract_bias_grad: float32 [512], replicated
Inputs may be any that keep to these rules, and one draw needn't show every extreme that they name: `sentence_ids`: each aligned block of 1024 rows holds whole sentences one after another, each with its own id, of 16 to 128 tokens (where a block has no padding its last sentence may be shorter), followed by padding; a padding token's id is 1024 plus its place in the block and equals no other id of the block. Ids are compared only within a block. `validity`: 1 on the sentences' tokens, 0 on padding; in every draw some block of 1024 rows is all 1. `expert_ids`: each token names 2 different experts.
All inputs are finite; a program needn't handle non-finite values.
Results may differ from a plain program's by a relative error of at most 0.015.
Values may be sent and summed in bfloat16 or wider, within the bound.
No kernel may reach another device: no remote copies, remote signals or barrier semaphores. Data moves between devices by JAX's collectives and lax.ppermute only.
A program may use at most 192 MiB of HBM per device.

v0:
```python
import math

import jax
import jax.numpy as jnp
from jax import lax
from jax.sharding import PartitionSpec as P

epsilon = 1e-05


def product(left, right):
    return jnp.dot(left, right, preferred_element_type=jnp.float32)


def across_rows(left, right):
    return lax.dot_general(
        left, right, (((0,), (0,)), ((), ())), preferred_element_type=jnp.float32
    )


def against(left, right):
    return lax.dot_general(
        left, right, (((1,), (1,)), ((), ())), preferred_element_type=jnp.float32
    )


def gelu_slope(values):
    cumulative = 0.5 * (1.0 + jax.scipy.special.erf(values * (1.0 / math.sqrt(2.0))))
    return cumulative + values * jnp.exp(-0.5 * values * values) * (1.0 / math.sqrt(2.0 * math.pi))


def normalize(rows_in, gain, shift):
    middle = jnp.mean(rows_in, axis=-1, keepdims=True)
    center = rows_in - middle
    inverse = lax.rsqrt(jnp.mean(center * center, axis=-1, keepdims=True) + epsilon)
    normed_hat = center * inverse
    return (normed_hat * gain + shift, normed_hat, inverse)


def norm_back(grad_normed, gain, normed_hat, inverse):
    scaled = grad_normed * gain
    mean_one = jnp.mean(scaled, axis=-1, keepdims=True)
    mean_two = jnp.mean(scaled * normed_hat, axis=-1, keepdims=True)
    grad_rows = inverse * (scaled - mean_one - normed_hat * mean_two)
    return (grad_rows, jnp.sum(grad_normed * normed_hat, axis=0), jnp.sum(grad_normed, axis=0))


def masked_scores(query_block, key_rows, block_ids, idents, score_scale):
    raw_scores = jnp.einsum(
        "qeh,kh->eqk", query_block, key_rows, preferred_element_type=jnp.float32
    )
    same = block_ids[:, None] == idents[None, :]
    return jnp.where(same[None], raw_scores * score_scale, -1e30)


def attend_forward(query_rows, key_rows, value_rows, idents, score_scale):
    row_total = query_rows.shape[0]
    block_size = min(512, row_total)
    pieces = []
    totals = []
    for offset in range(0, row_total, block_size):
        scores = masked_scores(
            query_rows[offset : offset + block_size],
            key_rows,
            idents[offset : offset + block_size],
            idents,
            score_scale,
        )
        topmost = jnp.max(scores, axis=-1, keepdims=True)
        weights = jnp.exp(scores - topmost)
        summed = jnp.sum(weights, axis=-1, keepdims=True)
        chances = (weights / summed).astype(jnp.bfloat16)
        totals.append((topmost + jnp.log(summed))[:, :, 0])
        pieces.append(
            jnp.einsum("eqk,kh->qeh", chances, value_rows, preferred_element_type=jnp.float32)
        )
    return (jnp.concatenate(pieces, axis=0), jnp.concatenate(totals, axis=1))


def attend_back(query_rows, key_rows, value_rows, idents, log_totals, grad_context, score_scale):
    row_total = query_rows.shape[0]
    block_size = min(512, row_total)
    pieces = []
    key_sum = jnp.zeros(key_rows.shape, jnp.float32)
    value_sum = jnp.zeros(value_rows.shape, jnp.float32)
    for offset in range(0, row_total, block_size):
        query_block = query_rows[offset : offset + block_size]
        grad_block = grad_context[offset : offset + block_size]
        scores = masked_scores(
            query_block, key_rows, idents[offset : offset + block_size], idents, score_scale
        )
        chances = jnp.exp(scores - log_totals[:, offset : offset + block_size, None])
        chances_low = chances.astype(jnp.bfloat16)
        grad_chances = jnp.einsum(
            "qeh,kh->eqk", grad_block, value_rows, preferred_element_type=jnp.float32
        )
        row_dot = jnp.sum(chances * grad_chances, axis=-1, keepdims=True)
        grad_raw = (chances * (grad_chances - row_dot) * score_scale).astype(jnp.bfloat16)
        pieces.append(
            jnp.einsum("eqk,kh->qeh", grad_raw, key_rows, preferred_element_type=jnp.float32)
        )
        key_sum = key_sum + jnp.einsum(
            "eqk,qeh->kh", grad_raw, query_block, preferred_element_type=jnp.float32
        )
        value_sum = value_sum + jnp.einsum(
            "eqk,qeh->kh", chances_low, grad_block, preferred_element_type=jnp.float32
        )
    return (jnp.concatenate(pieces, axis=0), key_sum, value_sum)


def shards(
    tokens,
    sentence_ids,
    validity,
    expert_ids,
    cotangent,
    first_gain,
    first_shift,
    router,
    query_weight,
    output_weight,
    keyval_weight,
    second_gain,
    second_shift,
    expand_weight,
    expand_bias,
    contract_weight,
    contract_bias,
):
    local_rows = tokens.shape[0]
    experts = router.shape[1]
    head_size = keyval_weight.shape[1] // 2
    score_scale = head_size ** (-0.5)
    inputs = tokens.astype(jnp.float32)
    gain_one = first_gain.astype(jnp.float32)
    gain_two = second_gain.astype(jnp.float32)
    first_out, first_hat, first_inverse = normalize(
        inputs, gain_one, first_shift.astype(jnp.float32)
    )
    first_low = first_out.astype(jnp.bfloat16)
    logits = product(first_low, router)
    chosen = (expert_ids[:, :, None] == jnp.arange(experts, dtype=jnp.int32)[None, None, :]).astype(
        jnp.float32
    )
    picked = jnp.sum(chosen * logits[:, None, :], axis=-1)
    paired = jax.nn.softmax(picked, axis=-1)
    gating = jnp.sum(paired[:, :, None] * chosen, axis=1)
    queries = product(first_low, query_weight).astype(jnp.bfloat16)
    keyval = product(first_low, keyval_weight).astype(jnp.bfloat16)
    key_rows = keyval[:, :head_size]
    value_rows = keyval[:, head_size:]
    query_rows = queries.reshape(local_rows, experts, head_size)
    context, log_totals = attend_forward(
        query_rows, key_rows, value_rows, sentence_ids, score_scale
    )
    context = context.reshape(local_rows, experts * head_size)
    gate_wide = jnp.repeat(gating, head_size, axis=1)
    mixed_low = (context * gate_wide).astype(jnp.bfloat16)
    residual = inputs + product(mixed_low, output_weight)
    second_out, second_hat, second_inverse = normalize(
        residual, gain_two, second_shift.astype(jnp.float32)
    )
    second_low = second_out.astype(jnp.bfloat16)
    grad_out = cotangent.astype(jnp.float32) * validity.astype(jnp.float32)[:, None]
    grad_low = grad_out.astype(jnp.bfloat16)
    group_rows = lax.all_gather(second_low, "mp", axis=0, tiled=True)
    preact = product(group_rows, expand_weight) + expand_bias.astype(jnp.float32)
    hidden = jax.nn.gelu(preact, approximate=False).astype(jnp.bfloat16)
    ffn_value = lax.psum_scatter(
        product(hidden, contract_weight).astype(jnp.bfloat16), "mp", scatter_dimension=0, tiled=True
    ).astype(jnp.float32)
    group_grad = lax.all_gather(grad_low, "mp", axis=0, tiled=True)
    grad_hidden = against(group_grad, contract_weight)
    grad_preact = (grad_hidden * gelu_slope(preact)).astype(jnp.bfloat16)
    contract_part = across_rows(hidden, group_grad)
    expand_part = across_rows(group_rows, grad_preact)
    bias_part = jnp.sum(grad_preact.astype(jnp.float32), axis=0)
    grad_second = lax.psum_scatter(
        against(grad_preact, expand_weight).astype(jnp.bfloat16),
        "mp",
        scatter_dimension=0,
        tiled=True,
    ).astype(jnp.float32)
    layer_output = (residual + ffn_value + contract_bias.astype(jnp.float32)).astype(jnp.bfloat16)
    expand_grad, expand_bias_grad, contract_grad = (
        lax.psum(expand_part.astype(jnp.bfloat16), "dp").astype(jnp.float32),
        lax.psum(bias_part.astype(jnp.bfloat16), "dp").astype(jnp.float32),
        lax.psum(contract_part.astype(jnp.bfloat16), "dp").astype(jnp.float32),
    )
    grad_norm_two, gain_two_grad, shift_two_grad = norm_back(
        grad_second, gain_two, second_hat, second_inverse
    )
    grad_residual = grad_out + grad_norm_two
    contract_bias_local = jnp.sum(grad_out, axis=0)
    grad_attn = grad_residual.astype(jnp.bfloat16)
    output_local = across_rows(mixed_low, grad_attn)
    grad_mixed = against(grad_attn, output_weight)
    grad_gating = jnp.sum((grad_mixed * context).reshape(local_rows, experts, head_size), axis=-1)
    grad_context = (grad_mixed * gate_wide).astype(jnp.bfloat16)
    grad_query_rows, key_sum, value_sum = attend_back(
        query_rows,
        key_rows,
        value_rows,
        sentence_ids,
        log_totals,
        grad_context.reshape(local_rows, experts, head_size),
        score_scale,
    )
    grad_queries = grad_query_rows.reshape(local_rows, experts * head_size).astype(jnp.bfloat16)
    grad_keyval = jnp.concatenate([key_sum, value_sum], axis=1).astype(jnp.bfloat16)
    grad_paired = jnp.sum(chosen * grad_gating[:, None, :], axis=-1)
    grad_picked = paired * (grad_paired - jnp.sum(paired * grad_paired, axis=-1, keepdims=True))
    grad_logits = jnp.sum(grad_picked[:, :, None] * chosen, axis=1).astype(jnp.bfloat16)
    query_local = across_rows(first_low, grad_queries)
    keyval_local = across_rows(first_low, grad_keyval)
    router_local = across_rows(first_low, grad_logits)
    grad_first = (
        against(grad_queries, query_weight)
        + against(grad_keyval, keyval_weight)
        + against(grad_logits, router)
    )
    grad_norm_one, gain_one_grad, shift_one_grad = norm_back(
        grad_first, gain_one, first_hat, first_inverse
    )
    tokens_gradient = (grad_residual + grad_norm_one).astype(jnp.bfloat16)
    summed_grads = lax.psum(
        (
            gain_one_grad,
            shift_one_grad,
            router_local,
            query_local,
            output_local,
            keyval_local,
            gain_two_grad,
            shift_two_grad,
            contract_bias_local,
        ),
        ("dp", "mp"),
    )
    return (
        layer_output,
        tokens_gradient,
        summed_grads[0],
        summed_grads[1],
        summed_grads[2],
        summed_grads[3],
        summed_grads[4],
        summed_grads[5],
        summed_grads[6],
        summed_grads[7],
        expand_grad,
        expand_bias_grad,
        contract_grad,
        summed_grads[8],
    )


def solution(mesh):
    placed = (
        P(("dp", "mp"), None),
        P(("dp", "mp")),
        P(("dp", "mp")),
        P(("dp", "mp"), None),
        P(("dp", "mp"), None),
        P(),
        P(),
        P(),
        P(),
        P(),
        P(),
        P(),
        P(),
        P(None, "mp"),
        P("mp"),
        P("mp", None),
        P(),
    )
    return jax.shard_map(
        shards,
        mesh=mesh,
        in_specs=placed,
        out_specs=(
            P(("dp", "mp"), None),
            P(("dp", "mp"), None),
            P(),
            P(),
            P(),
            P(),
            P(),
            P(),
            P(),
            P(),
            P(None, "mp"),
            P("mp"),
            P("mp", None),
            P(),
        ),
        check_vma=False,
    )
```

profile of v0, /device:TPU:0, one launch (start us, length us, event | category | flops | bytes accessed | tf_op | source)
XLA Modules:
  0.0 632.8 jit_solution(12547167245357376705)
XLA Ops:
  15.2 7.3 %fusion.121 = (f32[8,512]{1,0:T(8,128)S(1)}, f32[8,512,1024]{1,2,0:T(8,128)}) fusion(bf16[512,8,64]{0,2,1:T(8,128)(2,1)S(1)} %bitcast.185, bf16[1024,128]{0,1:T(8,128)(2,1)S(1)} %convolution_convert_fusion.5, pred[512,1024]{0,1:T(8,128)(4,1)S(1)} %get-tuple-element.82), kind=kOutput, calls=%fused_computation.181 | convolution fusion | flops 549449728 | bytes 17973248 | tf_op jit(solution)/shard_map/qeh,kh->eqk/dot_general | solution.py:49
  22.5 8.0 %fusion.8 = f32[8,512]{1,0:T(8,128)S(1)} fusion(f32[8,512,1024]{1,2,0:T(8,128)} %get-tuple-element.89, f32[8,512]{1,0:T(8,128)S(1)} %get-tuple-element.88), kind=kLoop, calls=%fused_computation.20 | loop fusion | flops 8384512 | bytes 16809984 | tf_op jit(solution)/shard_map/reduce_sum | solution.py:71
  30.5 7.3 %fusion.72 = f32[512,8,64]{0,2,1:T(8,128)S(1)} fusion(f32[8,512,1024]{1,2,0:T(8,128)} %get-tuple-element.89, f32[8,512]{1,0:T(8,128)S(1)} %fusion.8, f32[8,512]{1,0:T(8,128)S(1)} %get-tuple-element.88, bf16[1024,128]{0,1:T(8,128)(2,1)S(1)} %convolution_convert_fusion.5), kind=kOutput, calls=%fused_computation.113 | convolution fusion | flops 549453824 | bytes 17989632 | tf_op jit(solution)/shard_map/eqk,kh->qeh/dot_general | solution.py:75
  37.9 7.3 %fusion.120 = (f32[8,512]{1,0:T(8,128)S(1)}, f32[8,512,1024]{1,2,0:T(8,128)}) fusion(bf16[512,8,64]{0,2,1:T(8,128)(2,1)S(1)} %bitcast.183, bf16[1024,128]{0,1:T(8,128)(2,1)S(1)} %convolution_convert_fusion.5, pred[512,1024]{0,1:T(8,128)(4,1)S(1)} %get-tuple-element.83), kind=kOutput, calls=%fused_computation.180 | convolution fusion | flops 549449728 | bytes 17973248 | tf_op jit(solution)/shard_map/qeh,kh->eqk/dot_general | solution.py:49
  45.2 8.0 %fusion.9 = f32[8,512]{1,0:T(8,128)S(1)} fusion(f32[8,512,1024]{1,2,0:T(8,128)} %get-tuple-element.87, f32[8,512]{1,0:T(8,128)S(1)} %get-tuple-element.86), kind=kLoop, calls=%fused_computation.21 | loop fusion | flops 8384512 | bytes 16809984 | tf_op jit(solution)/shard_map/reduce_sum | solution.py:71
  53.2 7.6 %fusion.71 = f32[512,8,64]{0,2,1:T(8,128)S(1)} fusion(f32[8,512,1024]{1,2,0:T(8,128)} %get-tuple-element.87, f32[8,512]{1,0:T(8,128)S(1)} %fusion.9, f32[8,512]{1,0:T(8,128)S(1)} %get-tuple-element.86, bf16[1024,128]{0,1:T(8,128)(2,1)S(1)} %convolution_convert_fusion.5), kind=kOutput, calls=%fused_computation.112 | convolution fusion | flops 549453824 | bytes 17989632 | tf_op jit(solution)/shard_map/eqk,kh->qeh/dot_general | solution.py:75
  73.7 32.5 %all-gather.3.cloned.1.call-done = bf16[4096,512]{0,1:T(8,128)(2,1)} async-done(((bf16[1024,512]{0,1:T(8,128)(2,1)}), bf16[4096,512]{0,1:T(8,128)(2,1)}) %all-gather.3.cloned.1.call-update) | async-done | bytes 4194320 | tf_op jit(solution)/shard_map/all_gather | solution.py:166
  106.2 22.7 %fusion.14 = (bf16[4096,512]{1,0:T(8,128)(2,1)}, f32[4096,512]{1,0:T(8,128)}) fusion(f32[512]{0:T(512)S(1)} %convert_element_type.131, bf16[4096,512]{0,1:T(8,128)(2,1)} %all-gather.3.cloned.1.call-done, bf16[512,512]{1,0:T(8,128)(2,1)S(1)} %copy-done), kind=kOutput, calls=%fused_computation.28 | convolution fusion | flops 2285895680 | bytes 17303552 | tf_op jit(solution)/shard_map/dot_general | solution.py:12
  128.9 13.9 %all-gather.5.cloned.1.call-done = bf16[4096,512]{0,1:T(8,128)(2,1)} async-done(((bf16[1024,512]{0,1:T(8,128)(2,1)}), bf16[4096,512]{0,1:T(8,128)(2,1)}) %all-gather.5.cloned.1.call-update) | async-done | bytes 4194320 | tf_op jit(solution)/shard_map/all_gather | solution.py:172
  142.8 8.9 %fusion.123 = (bf16[512]{0:T(512)(128)(2,1)S(1)}, bf16[4096,512]{1,0:T(8,128)(2,1)S(1)}) fusion(f32[4096,512]{1,0:T(8,128)} %get-tuple-element.93, f32[512]{0:T(512)S(1)} %convert_element_type.131, bf16[4096,512]{0,1:T(8,128)(2,1)} %all-gather.5.cloned.1.call-done, bf16[512,512]{1,0:T(8,128)(2,1)} %param.32), kind=kOutput, calls=%fused_computation.183 | convolution fusion | flops 2172648960 | bytes 17304576 | tf_op jit(solution)/shard_map/dot_general | solution.py:22
  151.8 3.1 convolution_convert_fusion.4
  156.9 3.2 convolution_convert_fusion.3
  160.1 9.9 %reduce-scatter.5.cloned.1.call-start = ((), (), s32[]{:S(2)}) async-start(), calls=%async_computation.5 | async-start | bytes 5242880 | tf_op jit(solution)/shard_map/reduce_scatter | solution.py:178
  170.0 6.6 %convolution_convert_fusion = bf16[4096,512]{0,1:T(8,128)(2,1)} fusion(bf16[4096,512]{1,0:T(8,128)(2,1)} %copy-done.46, bf16[512,512]{1,0:T(8,128)(2,1)S(1)} %copy-done), kind=kOutput, calls=%fused_computation.62 | convolution fusion | flops 2149580800 | bytes 8912896 | tf_op jit(solution)/shard_map/dot_general | solution.py:22
  176.8 6.7 %convolution_convert_fusion.1 = bf16[4096,512]{0,1:T(8,128)(2,1)} fusion(bf16[4096,512]{1,0:T(8,128)(2,1)} %get-tuple-element.92, bf16[512,512]{1,0:T(8,128)(2,1)} %param.32), kind=kOutput, calls=%fused_computation.63 | convolution fusion | flops 2149580800 | bytes 8912896 | tf_op jit(solution)/shard_map/dot_general | solution.py:12
  183.6 21.4 %psum.93 = bf16[512]{0:T(512)(128)(2,1)S(1)} all-reduce(bf16[512]{0:T(512)(128)(2,1)S(1)} %get-tuple-element.97), channel_id=1, replica_groups=mesh['dp'=8,'mp'=4] {'dp'}, use_global_device_ids=true, to_apply=%region_38.39 | all-reduce | flops 512 | bytes 2048 | tf_op jit(solution)/shard_map/psum | solution.py:187
  205.5 33.2 %all-reduce.8.cloned.1.call-done = (bf16[512,512]{1,0:T(8,128)(2,1)}, bf16[512,512]{1,0:T(8,128)(2,1)}) async-done(((bf16[512,512]{1,0:T(8,128)(2,1)}, bf16[512,512]{1,0:T(8,128)(2,1)}), (bf16[512,512]{1,0:T(8,128)(2,1)}, bf16[512,512]{1,0:T(8,128)(2,1)})) %all-reduce.8.cloned.1.call-update) | async-done | bytes 1048592 | tf_op jit(solution)/shard_map/psum | solution.py:186
  243.0 42.3 %reduce-scatter.5.cloned.1.call-done = bf16[1024,512]{0,1:T(8,128)(2,1)} async-done(((bf16[4096,512]{0,1:T(8,128)(2,1)}), bf16[1024,512]{0,1:T(8,128)(2,1)}) %reduce-scatter.5.cloned.1.call-update) | async-done | bytes 1048592 | tf_op jit(solution)/shard_map/reduce_scatter | solution.py:178
  287.4 44.8 %reduce-scatter.3.cloned.1.call-done = bf16[1024,512]{0,1:T(8,128)(2,1)} async-done(((bf16[4096,512]{0,1:T(8,128)(2,1)}), bf16[1024,512]{0,1:T(8,128)(2,1)}) %reduce-scatter.3.cloned.1.call-update) | async-done | bytes 1048592 | tf_op jit(solution)/shard_map/reduce_scatter | solution.py:169
  332.2 4.3 fusion.64
  338.2 10.4 %fusion.100 = f32[1024,512,8]{1,0,2:T(8,128)} fusion(bf16[512,8,64]{0,2,1:T(8,128)(2,1)S(1)} %bitcast.179, bf16[1024,128]{0,1:T(8,128)(2,1)S(1)} %convolution_convert_fusion.5), kind=kOutput, calls=%fused_computation.147 | convolution fusion | flops 536870912 | bytes 17432576 | tf_op jit(solution)/shard_map/qeh,kh->eqk/dot_general | solution.py:94
  349.0 3.4 fusion.79
  352.4 23.2 %fusion.77 = f32[1024,64]{0,1:T(8,128)} fusion(bf16[512,8,64]{0,2,1:T(8,128)(2,1)S(1)} %bitcast.186, f32[1024,512,8]{1,0,2:T(8,128)} %fusion.100, f32[8,512,1024]{1,2,0:T(8,128)} %get-tuple-element.89, f32[8,512]{1,0:T(8,128)S(1)} %log_add_fusion.1), kind=kOutput, calls=%fused_computation.121 | convolution fusion | flops 566236160 | bytes 34357248 | tf_op jit(solution)/shard_map/eqk,qeh->kh/dot_general | solution.py:102
  375.5 28.5 %fusion.76 = bf16[512,8,64]{0,2,1:T(8,128)(2,1)} fusion(f32[1024,512,8]{1,0,2:T(8,128)} %fusion.100, f32[8,512,1024]{1,2,0:T(8,128)} %get-tuple-element.89, f32[8,512]{1,0:T(8,128)S(1)} %log_add_fusion.1, bf16[1024,128]{0,1:T(8,128)(2,1)S(1)} %convolution_convert_fusion.5), kind=kOutput, calls=%fused_computation.119 | convolution fusion | flops 566498304 | bytes 67796992 | tf_op jit(solution)/shard_map/eqk,kh->qeh/dot_general | solution.py:100
  404.0 3.0 fusion.93
  406.9 8.1 %fusion.99 = f32[1024,512,8]{1,0,2:T(8,128)} fusion(bf16[512,8,64]{0,2,1:T(8,128)(2,1)S(1)} %bitcast.177, bf16[1024,128]{0,1:T(8,128)(2,1)S(1)} %convolution_convert_fusion.5), kind=kOutput, calls=%fused_computation.146 | convolution fusion | flops 536870912 | bytes 17432576 | tf_op jit(solution)/shard_map/qeh,kh->eqk/dot_general | solution.py:94
  415.0 28.3 %fusion.75 = bf16[512,8,64]{0,2,1:T(8,128)(2,1)} fusion(f32[1024,512,8]{1,0,2:T(8,128)} %fusion.99, f32[8,512,1024]{1,2,0:T(8,128)} %get-tuple-element.87, f32[8,512]{1,0:T(8,128)S(1)} %log_add_fusion, bf16[1024,128]{0,1:T(8,128)(2,1)S(1)} %convolution_convert_fusion.5), kind=kOutput, calls=%fused_computation.118 | convolution fusion | flops 566498304 | bytes 67796992 | tf_op jit(solution)/shard_map/eqk,kh->qeh/dot_general | solution.py:100
  443.3 22.8 %fusion.89 = bf16[1024,64]{0,1:T(8,128)(2,1)S(1)} fusion(f32[1024,64]{0,1:T(8,128)S(1)} %copy-done.48, bf16[512,8,64]{0,2,1:T(8,128)(2,1)S(1)} %bitcast.184, f32[1024,512,8]{1,0,2:T(8,128)} %fusion.99, f32[8,512,1024]{1,2,0:T(8,128)} %get-tuple-element.87, f32[8,512]{1,0:T(8,128)S(1)} %log_add_fusion), kind=kOutput, calls=%fused_computation.127 | convolution fusion | flops 566367232 | bytes 34488320 | tf_op jit(solution)/shard_map/eqk,qeh->kh/dot_general | solution.py:102
  466.2 8.6 %fusion.90 = bf16[1024,64]{0,1:T(8,128)(2,1)S(1)} fusion(f32[1024,64]{0,1:T(8,128)S(1)} %copy-done.17, bf16[512,8,64]{0,2,1:T(8,128)(2,1)S(1)} %bitcast.178, f32[8,512,1024]{1,2,0:T(8,128)} %get-tuple-element.87, f32[8,512]{1,0:T(8,128)S(1)} %log_add_fusion), kind=kOutput, calls=%fused_computation.128 | convolution fusion | flops 545390592 | bytes 17711104 | tf_op jit(solution)/shard_map/eqk,qeh->kh/dot_general | solution.py:105
  482.8 4.1 fusion.60
  493.5 40.1 %all-reduce = (f32[512]{0:T(512)}, f32[512]{0:T(512)}, f32[512,8]{0,1:T(8,128)}, f32[512]{0:T(512)}, f32[512]{0:T(512)}, /*index=5*/f32[512]{0:T(512)}) all-reduce(f32[512]{0:T(512)S(1)} %get-tuple-element.58, f32[512]{0:T(512)S(1)} %get-tuple-element.61, f32[512,8]{0,1:T(8,128)S(1)} %fusion.126, ...), channel_id=1, replica_groups=mesh['dp'=8,'mp'=4] {'dp','mp'}, use_global_device_ids=true, to_apply=%region_25.26 | all-reduce | flops 6656 | bytes 53248 | tf_op jit(solution)/shard_map/psum | solution.py:226
  533.5 85.8 %all-reduce.6.cloned.1.call-done = (f32[512,512]{1,0:T(8,128)}, f32[512,512]{1,0:T(8,128)}, f32[512,128]{1,0:T(8,128)}) async-done(((f32[512,512]{1,0:T(8,128)}, f32[512,512]{1,0:T(8,128)}, f32[512,128]{1,0:T(8,128)}), (f32[512,512]{1,0:T(8,128)}, f32[512,512]{1,0:T(8,128)}, f32[512,128]{1,0:T(8,128)})) %all-reduce.6.cloned.1.call-update) | async-done | bytes 2359312 | tf_op jit(solution)/shard_map/psum | solution.py:226
  (179 shorter events, 52.2 us)
Async XLA Ops:
  7.2 99.0 %copy-start = (bf16[512,512]{1,0:T(8,128)(2,1)S(1)}, bf16[512,512]{1,0:T(8,128)(2,1)}, u32[]{:S(2)}) copy-start(bf16[512,512]{1,0:T(8,128)(2,1)} %param.30) | copy-start | bytes 1572868
  7.2 99.0 %all-gather.3.cloned.1.call-start = ((), (), s32[]{:S(2)}) async-start(), calls=%async_computation.2 | async-start | bytes 5242880 | tf_op jit(solution)/shard_map/all_gather | solution.py:166
  8.8 13.7 %copy-start.1 = (bf16[1024,512]{0,1:T(8,128)(2,1)}, bf16[1024,512]{0,1:T(8,128)(2,1)S(1)}, u32[]{:S(2)}) copy-start(bf16[1024,512]{0,1:T(8,128)(2,1)S(1)} %copy.70) | copy-start | bytes 3145732
  11.2 49.7 %copy-start.6 = (bf16[1024,512]{0,1:T(8,128)(2,1)}, bf16[1024,512]{0,1:T(8,128)(2,1)S(1)}, u32[]{:S(2)}) copy-start(bf16[1024,512]{0,1:T(8,128)(2,1)S(1)} %fusion.54) | copy-start | bytes 3145732
  14.5 8.0 %copy-start.14 = (bf16[512,512]{0,1:T(8,128)(2,1)}, bf16[512,512]{0,1:T(8,128)(2,1)S(1)}, u32[]{:S(2)}) copy-start(bf16[512,512]{0,1:T(8,128)(2,1)S(1)} %get-tuple-element.80) | copy-start | bytes 1572868
  14.5 23.4 %copy-start.12 = (bf16[512,512]{0,1:T(8,128)(2,1)}, bf16[512,512]{0,1:T(8,128)(2,1)S(1)}, u32[]{:S(2)}) copy-start(bf16[512,512]{0,1:T(8,128)(2,1)S(1)} %get-tuple-element.81) | copy-start | bytes 1572868
  53.2 7.6 %copy-start.34 = (bf16[512,8]{0,1:T(8,128)(2,1)S(1)}, bf16[512,8]{0,1:T(8,128)(2,1)}, u32[]{:S(2)}) copy-start(bf16[512,8]{0,1:T(8,128)(2,1)} %param.24) | copy-start | bytes 24580
  53.2 7.9 %copy-start.24 = (s32[1024,2]{0,1:T(2,128)S(1)}, s32[1024,2]{0,1:T(2,128)}, u32[]{:S(2)}) copy-start(s32[1024,2]{0,1:T(2,128)} %param.20) | copy-start | bytes 24580
  65.1 8.6 %copy-start.42 = (bf16[512]{0:T(512)(128)(2,1)S(1)}, bf16[512]{0:T(512)(128)(2,1)}, u32[]{:S(2)}) copy-start(bf16[512]{0:T(512)(128)(2,1)} %param.31) | copy-start | bytes 3076
  68.8 74.0 %all-gather.5.cloned.1.call-start = ((), (), s32[]{:S(2)}) async-start(), calls=%async_computation.4 | async-start | bytes 5242880 | tf_op jit(solution)/shard_map/all_gather | solution.py:172
  73.6 165.1 %all-reduce.8.cloned.1.call-start = ((), (), s32[]{:S(2)}) async-start(), calls=%async_computation.7 | async-start | bytes 2097152 | tf_op jit(solution)/shard_map/psum | solution.py:186
  142.8 8.9 %copy-start.44 = (bf16[4096,512]{0,1:T(8,128)(2,1)S(1)}, bf16[4096,512]{0,1:T(8,128)(2,1)}, u32[]{:S(2)}) copy-start(bf16[4096,512]{0,1:T(8,128)(2,1)} %all-gather.3.cloned.1.call-done) | copy-start | bytes 12582916
  160.1 125.2 %reduce-scatter.5.cloned.1.call-start = ((), (), s32[]{:S(2)}) async-start(), calls=%async_computation.5 | async-start | bytes 5242880 | tf_op jit(solution)/shard_map/reduce_scatter | solution.py:178
  176.7 155.5 %reduce-scatter.3.cloned.1.call-start = ((), (), s32[]{:S(2)}) async-start(), calls=%async_computation.3 | async-start | bytes 5242880 | tf_op jit(solution)/shard_map/reduce_scatter | solution.py:169
  183.5 435.9 %all-reduce.6.cloned.1.call-start = ((), (), s32[]{:S(2)}) async-start(), calls=%async_computation.6 | async-start | bytes 4718592 | tf_op jit(solution)/shard_map/psum | solution.py:226
  337.8 10.8 %slice-start = ((s8[16777216]{0:T(1024)(128)(4,1)}), s8[4194304]{0:T(1024)(128)(4,1)S(1)}, s32[]{:S(2)}) async-start(s8[16777216]{0:T(1024)(128)(4,1)} %bitcast.175), calls=%async_computation.8 | async-start | bytes 8388608
  338.2 10.5 %slice-start.1 = ((s8[16777216]{0:T(1024)(128)(4,1)}), s8[4194304]{0:T(1024)(128)(4,1)S(1)}, s32[]{:S(2)}) async-start(s8[16777216]{0:T(1024)(128)(4,1)} %bitcast.175), calls=%async_computation.9 | async-start | bytes 8388608
  338.2 10.5 %slice-start.2 = ((s8[16777216]{0:T(1024)(128)(4,1)}), s8[4194304]{0:T(1024)(128)(4,1)S(1)}, s32[]{:S(2)}) async-start(s8[16777216]{0:T(1024)(128)(4,1)} %bitcast.175), calls=%async_computation.10 | async-start | bytes 8388608
  338.2 10.8 %slice-start.3 = ((s8[16777216]{0:T(1024)(128)(4,1)}), s8[4194304]{0:T(1024)(128)(4,1)S(1)}, s32[]{:S(2)}) async-start(s8[16777216]{0:T(1024)(128)(4,1)} %bitcast.175), calls=%async_computation.11 | async-start | bytes 8388608
  375.5 28.5 %copy-start.4 = (f32[1024,512]{0,1:T(8,128)S(1)}, f32[1024,512]{0,1:T(8,128)}, u32[]{:S(2)}) copy-start(f32[1024,512]{0,1:T(8,128)} %copy-done.3) | copy-start | bytes 6291460
  415.0 28.3 %copy-start.13 = (bf16[512,512]{0,1:T(8,128)(2,1)S(1)}, bf16[512,512]{0,1:T(8,128)(2,1)}, u32[]{:S(2)}) copy-start(bf16[512,512]{0,1:T(8,128)(2,1)} %copy-done.12) | copy-start | bytes 1572868
  415.0 28.3 %copy-start.48 = (f32[1024,64]{0,1:T(8,128)S(1)}, f32[1024,64]{0,1:T(8,128)}, u32[]{:S(2)}) copy-start(f32[1024,64]{0,1:T(8,128)} %fusion.77) | copy-start | bytes 786436
  443.3 22.8 %copy-start.17 = (f32[1024,64]{0,1:T(8,128)S(1)}, f32[1024,64]{0,1:T(8,128)}, u32[]{:S(2)}) copy-start(f32[1024,64]{0,1:T(8,128)} %fusion.79) | copy-start | bytes 786436
  466.1 8.6 %copy-start.7 = (bf16[1024,512]{0,1:T(8,128)(2,1)S(1)}, bf16[1024,512]{0,1:T(8,128)(2,1)}, u32[]{:S(2)}) copy-start(bf16[1024,512]{0,1:T(8,128)(2,1)} %copy-done.6) | copy-start | bytes 3145732
  466.2 9.9 %copy-start.21 = (bf16[512,128]{1,0:T(8,128)(2,1)S(1)}, bf16[512,128]{1,0:T(8,128)(2,1)}, u32[]{:S(2)}) copy-start(bf16[512,128]{1,0:T(8,128)(2,1)} %param.27) | copy-start | bytes 393220
  466.2 11.7 %copy-start.19 = (bf16[512,8,64]{0,2,1:T(8,128)(2,1)S(1)}, bf16[512,8,64]{0,2,1:T(8,128)(2,1)}, u32[]{:S(2)}) copy-start(bf16[512,8,64]{0,2,1:T(8,128)(2,1)} %fusion.76) | copy-start | bytes 1572868
  466.2 11.7 %copy-start.20 = (bf16[512,8,64]{0,2,1:T(8,128)(2,1)S(1)}, bf16[512,8,64]{0,2,1:T(8,128)(2,1)}, u32[]{:S(2)}) copy-start(bf16[512,8,64]{0,2,1:T(8,128)(2,1)} %fusion.75) | copy-start | bytes 1572868
  474.9 7.8 %copy-start.2 = (bf16[1024,512]{0,1:T(8,128)(2,1)S(1)}, bf16[1024,512]{0,1:T(8,128)(2,1)}, u32[]{:S(2)}) copy-start(bf16[1024,512]{0,1:T(8,128)(2,1)} %copy-done.1) | copy-start | bytes 3145732
  474.9 7.8 %copy-start.18 = (bf16[512,512]{1,0:T(8,128)(2,1)S(1)}, bf16[512,512]{1,0:T(8,128)(2,1)}, u32[]{:S(2)}) copy-start(bf16[512,512]{1,0:T(8,128)(2,1)} %param.25) | copy-start | bytes 1572868
  474.9 7.8 %copy-start.29 = (f32[1024]{0:T(1024)S(1)}, f32[1024]{0:T(1024)}, u32[]{:S(2)}) copy-start(f32[1024]{0:T(1024)} %copy-done.28) | copy-start | bytes 12292
  474.9 7.8 %copy-start.33 = (f32[1024]{0:T(1024)S(1)}, f32[1024]{0:T(1024)}, u32[]{:S(2)}) copy-start(f32[1024]{0:T(1024)} %copy-done.32) | copy-start | bytes 12292
  474.9 7.8 %copy-start.37 = (f32[512]{0:T(512)S(1)}, f32[512]{0:T(512)}, u32[]{:S(2)}) copy-start(f32[512]{0:T(512)} %copy-done.36) | copy-start | bytes 6148
  (27 other events, 104.2 us)
Sparse Core Ops, SparseCore 0:
  69.0 37.1 all-gather.2
  108.3 34.4 all-gather.4
  160.2 78.4 all-reduce.7
  241.2 44.0 reduce-scatter.4
  287.7 44.5 reduce-scatter.2
  482.8 136.4 all-reduce.5
where the time goes:
time: 642 us; the launch traced here: 633 us
  waiting for transfers between devices  253 us (39%)
  matrix products  234 us (36%)
  blocking collectives  61.4 us (10%)
  other arithmetic  37 us (6%)
  local copies, waits for them, and re-layouts  22.2 us (3%)
  between operations  15.4 us (2%)
  starting transfers between devices  10.1 us (2%)
    psum x1, waiting for transfers between devices, shards(): lax.psum((gain_one_grad, shift_one_grad, router_local, query_local, outpu...  85.8 us
    dot_general x2, matrix products, attend_back(): jnp.einsum('eqk,kh->qeh', grad_raw, key_rows, preferred_element_type=jnp....  56.8 us
    dot_general x2, matrix products, attend_back(): jnp.einsum('eqk,qeh->kh', grad_raw, query_block, preferred_element_type=j...  46 us
    reduce_scatter x1, waiting for transfers between devices, shards(): lax.psum_scatter(product(hidden, contract_weight).astype(jnp.bfloat16), '...  44.8 us
    reduce_scatter x1, waiting for transfers between devices, shards(): lax.psum_scatter(against(grad_preact, expand_weight).astype(jnp.bfloat16)...  42.3 us
    psum x1, blocking collectives, shards(): lax.psum((gain_one_grad, shift_one_grad, router_local, query_local, outpu...  40.1 us
    dot_general x6, matrix products, product(): return jnp.dot(left, right, preferred_element_type=jnp.float32)  34.8 us
    psum x1, waiting for transfers between devices, shards(): lax.psum(expand_part.astype(jnp.bfloat16), 'dp').astype(jnp.float32)  33.2 us
  transfers between devices with their start and end apart: 6, of which 6 were waited for; matrix products, arithmetic and copies ran while one was open for 9% of the time, Pallas kernels for 0%

commit v1 on v0

v1 whole, which is shorter than its diff:
```python
import functools
import math

import jax
import jax.numpy as jnp
from jax import lax
from jax.experimental import pallas as pl
from jax.experimental.pallas import tpu as pltpu
from jax.sharding import PartitionSpec as P

F32 = jnp.float32
BF16 = jnp.bfloat16
epsilon = 1e-05
AXES = ("dp", "mp")
TILE = 128
VMEM_LIMIT = 56 << 20
LANES = 128
VECTOR_ROW = 8


def dot(left, right):
    return lax.dot_general(left, right, (((1,), (0,)), ((), ())), preferred_element_type=F32)


def dot_nt(left, right):
    return lax.dot_general(left, right, (((1,), (1,)), ((), ())), preferred_element_type=F32)


def dot_tn(left, right):
    return lax.dot_general(left, right, (((0,), (0,)), ((), ())), preferred_element_type=F32)


def normed(rows_in):
    middle = jnp.mean(rows_in, axis=-1, keepdims=True)
    center = rows_in - middle
    inverse = lax.rsqrt(jnp.mean(center * center, axis=-1, keepdims=True) + epsilon)
    return center * inverse, inverse


def norm_back(grad_normed, gain, normed_hat, inverse):
    scaled = grad_normed * gain
    mean_one = jnp.mean(scaled, axis=-1, keepdims=True)
    mean_two = jnp.mean(scaled * normed_hat, axis=-1, keepdims=True)
    return inverse * (scaled - mean_one - normed_hat * mean_two)


def row_sum(values):
    return jnp.sum(values, axis=0, keepdims=True)


def pair_masks(first_id, second_id, pairs):
    half = (lax.broadcasted_iota(jnp.int32, (TILE, LANES), 1) >= LANES // 2).astype(F32)
    low = first_id - half
    high = second_id - half
    return [(low == 2.0 * pair, high == 2.0 * pair) for pair in range(pairs)]


def window_of(tile, tiles):
    width = min(3, tiles)
    return min(max(tile - 1, 0), tiles - width) * TILE, width * TILE


def attend_kernel(
    tok, sent, valid, expert, cot, gain1, shift1, router, wq, wkv, wo, gain2, shift2,
    res, low2, glow, low1, mixed, qsel, kv, chance, ctx, cols,
    queries, logits,
):
    rows, width = tok.shape
    tiles = rows // TILE
    pairs = width // LANES
    big = 256
    scale = (wkv.shape[1] // 2) ** -0.5
    half_lane = lax.broadcasted_iota(jnp.int32, (big, LANES), 1) < LANES // 2
    for at in range(0, rows, big):
        span = pl.ds(at, big)
        hat, _ = normed(tok[span, :].astype(F32))
        low = (hat * gain1[...].astype(F32) + shift1[...].astype(F32)).astype(BF16)
        low1[span, :] = low
        queries[span, :] = dot(low, wq[...]).astype(BF16)
        logits[span, :] = dot(low, router[...])
        both = dot(low, wkv[...])
        turned = pltpu.roll(both, LANES // 2, 1)
        kv[span, :LANES] = jnp.where(half_lane, both, turned).astype(BF16)
        kv[span, LANES:] = jnp.where(half_lane, turned, both).astype(BF16)
    for tile in range(tiles):
        at = tile * TILE
        span = pl.ds(at, TILE)
        meta = jnp.concatenate(
            [
                sent[:, at : at + TILE],
                valid[:, at : at + TILE],
                expert[:, at : at + TILE],
                jnp.zeros((4, TILE), jnp.int32),
            ],
            axis=0,
        ).astype(F32)
        column = jnp.transpose(meta)
        own_sent, own_valid = column[:, 0:1], column[:, 1:2]
        first_id, second_id = column[:, 2:3], column[:, 3:4]
        glow[span, :] = jnp.where(own_valid > 0.5, cot[span, :].astype(F32), 0.0).astype(BF16)
        scored = logits[span, :]
        slot = lax.broadcasted_iota(jnp.int32, scored.shape, 1).astype(F32)
        pick0 = jnp.sum(jnp.where(slot == first_id, scored, 0.0), axis=-1, keepdims=True)
        pick1 = jnp.sum(jnp.where(slot == second_id, scored, 0.0), axis=-1, keepdims=True)
        most = jnp.maximum(pick0, pick1)
        raise0, raise1 = jnp.exp(pick0 - most), jnp.exp(pick1 - most)
        gate0 = raise0 / (raise0 + raise1)
        gate1 = raise1 / (raise0 + raise1)
        lane = lax.broadcasted_iota(jnp.int32, (TILE, 8), 1)
        cols[span, :] = jnp.where(
            lane == 0, gate0, jnp.where(lane == 1, gate1, jnp.where(lane == 2, first_id, second_id))
        )
        masks = pair_masks(first_id, second_id, pairs)
        q0 = jnp.zeros((TILE, LANES), F32)
        q1 = jnp.zeros((TILE, LANES), F32)
        for pair in range(pairs):
            block = queries[span, pair * LANES : (pair + 1) * LANES].astype(F32)
            q0 = jnp.where(masks[pair][0], block, q0)
            q1 = jnp.where(masks[pair][1], block, q1)
        picked = (jnp.concatenate([q0, q1], axis=0) * scale).astype(BF16)
        qsel[tile] = picked
        start, extent = window_of(tile, tiles)
        near = pl.ds(start, extent)
        scores = dot_nt(picked, kv[near, :LANES])
        same = own_sent == sent[:, start : start + extent].astype(F32)
        same = jnp.concatenate([same, same], axis=0)
        scores = jnp.where(same, scores, -1e30)
        weights = jnp.exp(scores - jnp.max(scores, axis=-1, keepdims=True))
        share = (weights * (1.0 / jnp.sum(weights, axis=-1, keepdims=True))).astype(BF16)
        chance[tile] = share
        context = dot(share, kv[near, LANES:])
        ctx[tile] = context
        part0 = context[:TILE] * gate0
        part1 = context[TILE:] * gate1
        for pair in range(pairs):
            mixed[span, pair * LANES : (pair + 1) * LANES] = jnp.where(
                masks[pair][0], part0, jnp.where(masks[pair][1], part1, 0.0)
            ).astype(BF16)
    for at in range(0, rows, big):
        span = pl.ds(at, big)
        total = tok[span, :].astype(F32) + dot(mixed[span, :], wo[...])
        res[span, :] = total
        hat, _ = normed(total)
        low2[span, :] = (hat * gain2[...].astype(F32) + shift2[...].astype(F32)).astype(BF16)


def ffn_kernel(*refs, more, last, steps):
    low2, glow, expand, contract, bias = refs[:5]
    at = 5
    if "rows" in more:
        out_in, second_in = refs[at : at + 2]
        at += 2
    if "weights" in more:
        contract_in, expand_in, bias_in = refs[at : at + 3]
        at += 3
    out, second, contract_out, expand_out, bias_out, contract_sum, expand_sum, bias_sum = refs[at:]
    step = pl.program_id(0)

    @pl.when(step == 0)
    def _():
        if "weights" in more:
            contract_sum[...] = contract_in[...]
            expand_sum[...] = expand_in[...]
            bias_sum[...] = bias_in[...]
        else:
            contract_sum[...] = jnp.zeros_like(contract_sum)
            expand_sum[...] = jnp.zeros_like(expand_sum)
            bias_sum[...] = jnp.zeros_like(bias_sum)

    rows, grads = low2[...], glow[...]
    preact = dot(rows, expand[...]) + bias[...].astype(F32)
    cumulative = 0.5 * (1.0 + lax.erf(preact * (1.0 / math.sqrt(2.0))))
    bell = jnp.exp(-0.5 * preact * preact) * (1.0 / math.sqrt(2.0 * math.pi))
    hidden = (preact * cumulative).astype(BF16)
    grad = (dot_nt(grads, contract[...]) * (cumulative + preact * bell)).astype(BF16)
    bias_sum[...] += row_sum(grad.astype(F32))
    out_part = dot(hidden, contract[...])
    second_part = dot_nt(grad, expand[...])
    if "rows" in more:
        out_part += out_in[...]
        second_part += second_in[...]
    out[...] = out_part.astype(out.dtype)
    second[...] = second_part.astype(second.dtype)
    contract_sum[...] += dot_tn(hidden, grads)
    expand_sum[...] += dot_tn(rows, grad)

    @pl.when(step == steps - 1)
    def _():
        contract_out[...] = contract_sum[...].astype(contract_out.dtype)
        expand_out[...] = expand_sum[...].astype(expand_out.dtype)
        bias_out[...] = bias_sum[...]


def ffn(low2, glow, weights, rows_in=None, weights_in=None, rows_dtype=F32, weights_dtype=F32):
    expand, contract, bias = weights
    rows, width = low2.shape
    units = expand.shape[1]
    step_rows = min(256, rows)
    steps = rows // step_rows
    more = []
    row_spec = pl.BlockSpec((step_rows, width), lambda i: (i, 0))

    def whole(*shape):
        return pl.BlockSpec(shape, lambda i: (0, 0))

    operands = [low2, glow, expand, contract, bias]
    in_specs = [row_spec, row_spec, whole(width, units), whole(units, width), whole(1, units)]
    if rows_in is not None:
        more.append("rows")
        operands += rows_in
        in_specs += [row_spec, row_spec]
    if weights_in is not None:
        more.append("weights")
        operands += weights_in
        in_specs += [whole(units, width), whole(width, units), whole(1, units)]
    outs = pl.pallas_call(
        functools.partial(ffn_kernel, more=tuple(more), last=True, steps=steps),
        grid=(steps,),
        in_specs=in_specs,
        out_specs=[
            row_spec, row_spec, whole(units, width), whole(width, units), whole(1, units)
        ],
        out_shape=[
            jax.ShapeDtypeStruct((rows, width), rows_dtype),
            jax.ShapeDtypeStruct((rows, width), rows_dtype),
            jax.ShapeDtypeStruct((units, width), weights_dtype),
            jax.ShapeDtypeStruct((width, units), weights_dtype),
            jax.ShapeDtypeStruct((1, units), F32),
        ],
        scratch_shapes=[
            pltpu.VMEM((units, width), F32),
            pltpu.VMEM((width, units), F32),
            pltpu.VMEM((1, units), F32),
        ],
        compiler_params=pltpu.CompilerParams(vmem_limit_bytes=VMEM_LIMIT),
        name="ffn",
    )(*operands)
    return list(outs[:2]), list(outs[2:])


def back_kernel(
    out_own, out_got, second_own, second_got, res, tok, glow, low1, mixed, qsel, kv, chance, ctx,
    cols, gain1, gain2, contract_bias, router, wq, wkv, wo, unit_bias,
    layer, tok_grad, packed,
    grad_res, grad_mixed, grad_q, grad_log, key_sum, value_sum, vectors,
):
    rows, width = tok.shape
    tiles = rows // TILE
    pairs = width // LANES
    big = 256
    scale = (wkv.shape[1] // 2) ** -0.5
    experts = router.shape[1]
    gain_one, gain_two = gain1[...].astype(F32), gain2[...].astype(F32)
    gain2_sum = shift2_sum = bias_sum = jnp.zeros((1, width), F32)
    for at in range(0, rows, big):
        span = pl.ds(at, big)
        total = res[span, :]
        layer[span, :] = (
            total + out_own[span, :] + out_got[span, :].astype(F32) + contract_bias[...].astype(F32)
        ).astype(BF16)
        hat, inverse = normed(total)
        second = second_own[span, :] + second_got[span, :].astype(F32)
        gain2_sum += row_sum(second * hat)
        shift2_sum += row_sum(second)
        outer = glow[span, :].astype(F32)
        bias_sum += row_sum(outer)
        grad = outer + norm_back(second, gain_two, hat, inverse)
        grad_res[span, :] = grad
        grad_mixed[span, :] = dot_nt(grad.astype(BF16), wo[...])
    packed[:, width : 2 * width] = dot_tn(mixed[...], grad_res[...].astype(BF16)).astype(BF16)
    key_sum[...] = jnp.zeros_like(key_sum)
    value_sum[...] = jnp.zeros_like(value_sum)
    for tile in range(tiles):
        at = tile * TILE
        span = pl.ds(at, TILE)
        gate0, gate1 = cols[span, 0:1], cols[span, 1:2]
        first_id, second_id = cols[span, 2:3], cols[span, 3:4]
        masks = pair_masks(first_id, second_id, pairs)
        g0 = jnp.zeros((TILE, LANES), F32)
        g1 = jnp.zeros((TILE, LANES), F32)
        for pair in range(pairs):
            block = grad_mixed[span, pair * LANES : (pair + 1) * LANES]
            g0 = jnp.where(masks[pair][0], block, g0)
            g1 = jnp.where(masks[pair][1], block, g1)
        context = ctx[tile]
        use0 = jnp.sum(g0 * context[:TILE], axis=-1, keepdims=True)
        use1 = jnp.sum(g1 * context[TILE:], axis=-1, keepdims=True)
        usual = gate0 * use0 + gate1 * use1
        lane = lax.broadcasted_iota(jnp.int32, (TILE, LANES), 1).astype(F32)
        grad_log[span, :] = jnp.where(
            lane == first_id,
            gate0 * (use0 - usual),
            jnp.where(lane == second_id, gate1 * (use1 - usual), 0.0),
        ).astype(BF16)
        grad_ctx = jnp.concatenate([g0 * gate0, g1 * gate1], axis=0).astype(BF16)
        delta = jnp.sum(grad_ctx.astype(F32) * context, axis=-1, keepdims=True)
        start, extent = window_of(tile, tiles)
        near = pl.ds(start, extent)
        grad_share = dot_nt(grad_ctx, kv[near, LANES:])
        share = chance[tile]
        raw = (share.astype(F32) * (grad_share - delta)).astype(BF16)
        grad_query = dot(raw, kv[near, :LANES]) * scale
        for pair in range(pairs):
            grad_q[span, pair * LANES : (pair + 1) * LANES] = jnp.where(
                masks[pair][0],
                grad_query[:TILE],
                jnp.where(masks[pair][1], grad_query[TILE:], 0.0),
            ).astype(BF16)
        key_sum[near, :] += dot_tn(raw, qsel[tile])
        value_sum[near, :] += dot_tn(share, grad_ctx)
    keys, values = key_sum[...], value_sum[...]
    keys = keys + pltpu.roll(keys, LANES // 2, 1)
    values = values + pltpu.roll(values, LANES // 2, 1)
    half_lane = lax.broadcasted_iota(jnp.int32, (rows, LANES), 1) < LANES // 2
    grad_kv = jnp.where(half_lane, keys, values).astype(BF16)
    gain1_sum = shift1_sum = jnp.zeros((1, width), F32)
    for at in range(0, rows, big):
        span = pl.ds(at, big)
        hat, inverse = normed(tok[span, :].astype(F32))
        grad = (
            dot_nt(grad_q[span, :], wq[...])
            + dot_nt(grad_kv[at : at + big], wkv[...])
            + dot_nt(grad_log[span, :experts], router[...])
        )
        gain1_sum += row_sum(grad * hat)
        shift1_sum += row_sum(grad)
        tok_grad[span, :] = (grad_res[span, :] + norm_back(grad, gain_one, hat, inverse)).astype(
            BF16
        )
    packed[:, :width] = dot_tn(low1[...], grad_q[...]).astype(BF16)
    packed[:, 2 * width : 2 * width + LANES] = dot_tn(low1[...], grad_kv).astype(BF16)
    vectors[...] = jnp.zeros_like(vectors)
    sums = (gain1_sum, shift1_sum, gain2_sum, shift2_sum, bias_sum)
    for place, values in enumerate(sums):
        vectors[VECTOR_ROW + place : VECTOR_ROW + place + 1, :] = values
    first = VECTOR_ROW + len(sums)
    count, units = unit_bias.shape
    vectors[first : first + count, :units] = unit_bias[...]
    packed[:, 2 * width + LANES :] = (
        dot_tn(low1[...], grad_log[...]) + jnp.transpose(vectors[...])
    ).astype(BF16)


def vmem_call(kernel, name, operands, out_shape, scratch):
    return pl.pallas_call(
        kernel,
        out_shape=out_shape,
        in_specs=[pl.BlockSpec(memory_space=pltpu.VMEM)] * len(operands),
        out_specs=[pl.BlockSpec(memory_space=pltpu.VMEM)] * len(out_shape),
        scratch_shapes=scratch,
        compiler_params=pltpu.CompilerParams(vmem_limit_bytes=VMEM_LIMIT),
        name=name,
    )(*operands)


def swap(values, bit, devices):
    return lax.ppermute(values, AXES, [(at, at ^ bit) for at in range(devices)])


def halves(values, mine):
    size = values.shape[0] // 2
    keep = lax.dynamic_slice_in_dim(values, mine * size, size, 0)
    send = lax.dynamic_slice_in_dim(values, (1 - mine) * size, size, 0)
    return keep, send


def scatter_sum(values, bits, place, devices):
    for bit in bits:
        mine = (place // bit) % 2
        keep, send = halves(values, mine)
        got = swap(send, bit, devices)
        values = (keep.astype(F32) + got.astype(F32)).astype(BF16)
    return values


def gather(values, bits, place, devices):
    for bit in reversed(bits):
        mine = (place // bit) % 2
        got = swap(values, bit, devices)
        values = jnp.where(
            mine == 0,
            jnp.concatenate([values, got], axis=0),
            jnp.concatenate([got, values], axis=0),
        )
    return values


def shards(
    n_dp,
    n_mp,
    tokens,
    sentence_ids,
    validity,
    expert_ids,
    cotangent,
    first_gain,
    first_shift,
    router,
    query_weight,
    output_weight,
    keyval_weight,
    second_gain,
    second_shift,
    expand_weight,
    expand_bias,
    contract_weight,
    contract_bias,
):
    devices = n_dp * n_mp
    rows, width = tokens.shape
    units = expand_weight.shape[1]
    tiles = rows // TILE
    _, extent = window_of(0, tiles)
    place = lax.axis_index(AXES)
    mp_place = lax.axis_index("mp")

    def row(vector):
        return vector.reshape(1, -1)

    def shape(*dims, dtype=BF16):
        return jax.ShapeDtypeStruct(dims, dtype)

    bias_row = row(expand_bias)
    own = (expand_weight, contract_weight, bias_row)
    chips = n_mp // 2
    others = [
        tuple(swap(item, 2 * step, devices) for item in own) for step in range(1, chips)
    ]
    operands = [
        tokens, row(sentence_ids), row(validity), expert_ids.T, cotangent, row(first_gain),
        row(first_shift), router, query_weight, keyval_weight, output_weight, row(second_gain),
        row(second_shift),
    ]
    res, low2, glow, low1, mixed, qsel, kv, chance, ctx, cols = vmem_call(
        attend_kernel,
        "attend",
        operands,
        [
            shape(rows, width, dtype=F32),
            shape(rows, width),
            shape(rows, width),
            shape(rows, width),
            shape(rows, width),
            shape(tiles, 2 * TILE, LANES),
            shape(rows, 2 * LANES),
            shape(tiles, 2 * TILE, extent),
            shape(tiles, 2 * TILE, LANES, dtype=F32),
            shape(rows, 8, dtype=F32),
        ],
        [pltpu.VMEM((rows, width), BF16), pltpu.VMEM((rows, router.shape[1]), F32)],
    )
    low2_pair = swap(low2, 1, devices)
    glow_pair = swap(glow, 1, devices)
    rows_own, grads_own = ffn(low2, glow, own)
    rows_pair, grads_own = ffn(
        low2_pair, glow_pair, own, weights_in=grads_own, weights_dtype=BF16
    )
    contract_sum, expand_sum = grads_own[0], grads_own[1]
    unit_rows = jnp.arange(n_mp, dtype=jnp.int32)[:, None]
    unit_bias = jnp.where(unit_rows == mp_place, grads_own[2], 0.0)
    for step in range(1, chips):
        final = step == chips - 1
        rows_pair, grads = ffn(
            low2_pair,
            glow_pair,
            others[step - 1],
            rows_in=rows_pair,
            rows_dtype=BF16 if final else F32,
        )
        if final:
            out_got, second_got = (swap(item, 1, devices) for item in rows_pair)
        rows_own, grads = ffn(
            low2,
            glow,
            others[step - 1],
            rows_in=rows_own,
            weights_in=grads,
            weights_dtype=BF16,
        )
        unit_bias += jnp.where(unit_rows == (mp_place ^ (2 * step)), grads[2], 0.0)
        contract_got = swap(grads[0], 2 * step, devices)
        expand_got = swap(grads[1], 2 * step, devices)
        contract_sum = (contract_sum.astype(F32) + contract_got.astype(F32)).astype(BF16)
        expand_sum = (expand_sum.astype(F32) + expand_got.astype(F32)).astype(BF16)
    layer, tok_grad, packed = vmem_call(
        back_kernel,
        "back",
        [
            rows_own[0], out_got, rows_own[1], second_got, res, tokens, glow, low1, mixed, qsel,
            kv, chance, ctx, cols, row(first_gain), row(second_gain), row(contract_bias), router,
            query_weight, keyval_weight, output_weight, unit_bias,
        ],
        [shape(rows, width), shape(rows, width), shape(width, 2 * width + 2 * LANES)],
        [
            pltpu.VMEM((rows, width), F32),
            pltpu.VMEM((rows, width), F32),
            pltpu.VMEM((rows, width), BF16),
            pltpu.VMEM((rows, LANES), BF16),
            pltpu.VMEM((rows, LANES), F32),
            pltpu.VMEM((rows, LANES), F32),
            pltpu.VMEM((LANES, width), F32),
        ],
    )
    dp_bits = [n_mp << at for at in range(n_dp.bit_length() - 1)]
    turned = dp_bits[1:] + dp_bits[:1]
    mp_bits = [1 << at for at in range(n_mp.bit_length() - 1)]
    contract_grad = gather(
        scatter_sum(contract_sum, dp_bits, place, devices), dp_bits, place, devices
    ).astype(F32)
    expand_grad = gather(
        scatter_sum(expand_sum, turned, place, devices), turned, place, devices
    ).astype(F32)
    every = mp_bits + dp_bits
    packed = gather(scatter_sum(packed, every, place, devices), every, place, devices).astype(F32)
    vectors = packed[:, 2 * width + LANES :].T
    first = VECTOR_ROW + 5
    unit_grad = lax.dynamic_slice_in_dim(vectors, first + mp_place, 1, 0)[0, :units]
    return (
        layer,
        tok_grad,
        vectors[VECTOR_ROW],
        vectors[VECTOR_ROW + 1],
        packed[:, 2 * width + LANES : 2 * width + LANES + router.shape[1]],
        packed[:, :width],
        packed[:, width : 2 * width],
        packed[:, 2 * width : 2 * width + LANES],
        vectors[VECTOR_ROW + 2],
        vectors[VECTOR_ROW + 3],
        expand_grad,
        unit_grad,
        contract_grad,
        vectors[VECTOR_ROW + 4],
    )


def solution(mesh):
    tokens_spec = P(AXES, None)
    placed = (
        tokens_spec,
        P(AXES),
        P(AXES),
        tokens_spec,
        tokens_spec,
        P(),
        P(),
        P(),
        P(),
        P(),
        P(),
        P(),
        P(),
        P(None, "mp"),
        P("mp"),
        P("mp", None),
        P(),
    )
    return jax.shard_map(
        functools.partial(shards, mesh.shape["dp"], mesh.shape["mp"]),
        mesh=mesh,
        in_specs=placed,
        out_specs=(
            tokens_spec,
            tokens_spec,
            P(),
            P(),
            P(),
            P(),
            P(),
            P(),
            P(),
            P(),
            P(None, "mp"),
            P("mp"),
            P("mp", None),
            P(),
        ),
        check_vma=False,
    )
```

time: 642 us -> 162 us (0.25); the launches traced: 633 us -> 161 us
  matrix products: 234 us -> 0 us
  waiting for transfers between devices: 253 us -> 36.6 us
  Pallas kernels: 0 us -> 63.1 us
  blocking collectives: 61.4 us -> 0 us
  other arithmetic: 37 us -> 6.53 us
  starting transfers between devices: 10.1 us -> 36.8 us
  between operations: 15.4 us -> 1.02 us
    dot_general x30 -> x0, matrix products: 234 us -> none  [the longest x2 56.8 us: attend_back(): jnp.einsum('eqk,kh->qeh', grad_raw, key_rows, preferred_element_type=jnp....]
    psum x2 -> x0, waiting for transfers between devices: 119 us -> none  [the longest x1 85.8 us: shards(): lax.psum((gain_one_grad, shift_one_grad, router_local, query_local, outpu...]
    reduce_scatter x2 -> x0, waiting for transfers between devices: 87.1 us -> none  [the longest x1 44.8 us: shards(): lax.psum_scatter(product(hidden, contract_weight).astype(jnp.bfloat16), '...]
    pallas_call x0 -> x6, Pallas kernels: none -> 63.1 us  [the longest x4 34.3 us: ffn(): pl.pallas_call(functools.partial(ffn_kernel, more=tuple(more), last=True,...]
    psum x2 -> x0, blocking collectives: 61.4 us -> none  [the longest x1 40.1 us: shards(): lax.psum((gain_one_grad, shift_one_grad, router_local, query_local, outpu...]
    all_gather x2 -> x0, waiting for transfers between devices: 46.4 us -> none  [the longest x1 32.5 us: shards(): group_rows = lax.all_gather(second_low, 'mp', axis=0, tiled=True)]
    ppermute x0 -> x31, starting transfers between devices: none -> 36.8 us  [swap(): return lax.ppermute(values, AXES, [(at, at ^ bit) for at in range(devices)])]
    ppermute x0 -> x31, waiting for transfers between devices: none -> 36.6 us  [swap(): return lax.ppermute(values, AXES, [(at, at ^ bit) for at in range(devices)])]
  transfers between devices with their start and end apart: 6 -> 31, of which waited for: 6 -> 13; matrix products, arithmetic and copies ran while one was open for 9% -> 4% of each run, Pallas kernels for 0% -> 27%
where the time goes in v1:
time: 162 us; the launch traced here: 161 us
  Pallas kernels  63.1 us (39%)
  starting transfers between devices  36.8 us (23%)
  waiting for transfers between devices  36.6 us (23%)
  local copies, waits for them, and re-layouts  17.5 us (11%)
  other arithmetic  6.53 us (4%)
    ppermute x31, starting transfers between devices, swap(): return lax.ppermute(values, AXES, [(at, at ^ bit) for at in range(devices)])  36.8 us
    ppermute x31, waiting for transfers between devices, swap(): return lax.ppermute(values, AXES, [(at, at ^ bit) for at in range(devices)])  36.6 us
    pallas_call x4, Pallas kernels, ffn(): pl.pallas_call(functools.partial(ffn_kernel, more=tuple(more), last=True,...  34.3 us
    pallas_call x2, Pallas kernels, vmem_call(): pl.pallas_call(kernel, out_shape=out_shape, in_specs=[pl.BlockSpec(memory...  28.8 us
    unnamed x36, local copies, waits for them, and re-layouts  5.78 us
    reshape x6, local copies, waits for them, and re-layouts, row(): return vector.reshape(1, -1)  5.62 us
  transfers between devices with their start and end apart: 31, of which 13 were waited for; matrix products, arithmetic and copies ran while one was open for 4% of the time, Pallas kernels for 27%

profile of v1, /device:TPU:0, one launch (start us, length us, event | category | flops | bytes accessed | tf_op | source)
XLA Modules:
  0.0 161.5 jit_solution(14276600276489998652)
XLA Ops:
  7.2 11.3 %attend.1 = (f32[1024,512]{1,0:T(8,128)}, bf16[1024,512]{1,0:T(8,128)(2,1)}, bf16[1024,512]{1,0:T(8,128)(2,1)}, bf16[1024,512]{1,0:T(8,128)(2,1)}, bf16[1024,512...) custom-call(bf16[1024,512]{1,0:T(8,128)(2,1)} %tok.3, ...), custom_call_target="tpu_custom_call" | custom-call | tf_op jit(solution)/shard_map/attend/pallas_call | solution.py:345
  19.0 2.9 %collective-permute-start = (bf16[512,512]{1,0:T(8,128)(2,1)S(1)}, bf16[512,512]{1,0:T(8,128)(2,1)S(1)}, u32[]{:S(2)}, u32[]{:S(2)}) collective-permute-start(bf16[512,512]{1,0:T(8,128)(2,1)S(1)} %copy-done.3), channel_id=1, source_target_pairs={{0,2},{1,3},{2,0},{3,1},{4,6},{5,7},{6,4},{7,5},{8,10},{9,11},{10,... | collective-permute-start | bytes 1572872 | tf_op jit(solution)/shard_map/ppermute | solution.py:357
  22.1 2.0 %collective-permute-start.2 = (bf16[1,512]{1,0:T(2,128)(2,1)S(1)}, bf16[1,512]{1,0:T(2,128)(2,1)S(1)}, u32[]{:S(2)}, u32[]{:S(2)}) collective-permute-start(bf16[1,512]{1,0:T(2,128)(2,1)S(1)} %reshape.72.refs_4_), channel_id=1, source_target_pairs={{0,2},{1,3},{2,0},{3,1},{4,6},{5,7},{6,4},{7,5},{8,10},{9,11},{10,... | collective-permute-start | bytes 3080 | tf_op jit(solution)/shard_map/ppermute | solution.py:357
  24.1 8.2 %ffn.4 = (f32[1024,512]{1,0:T(8,128)}, f32[1024,512]{1,0:T(8,128)}, f32[512,512]{1,0:T(8,128)}, f32[512,512]{1,0:T(8,128)}, f32[1,512]{1,0:T(1,128)}) custom-call(bf16[1024,512]{1,0:T(8,128)(2,1)} %get-tuple-element.47.refs_0_, bf16[1024,512]{1,0:T(8,128)(2,1)} %get-tuple-element.48.refs_1_.glow, bf16[512,512]{1,0:T(8,128)(2,1)} %refs_2_.3, ...), custom_call_target="tpu_custom_call" | custom-call | tf_op jit(solution)/shard_map/ffn/pallas_call | solution.py:216
  33.6 8.4 %ffn.5 = (f32[1024,512]{1,0:T(8,128)}, f32[1024,512]{1,0:T(8,128)}, bf16[512,512]{1,0:T(8,128)(2,1)}, bf16[512,512]{1,0:T(8,128)(2,1)}, f32[1,512]{1,0:T(1,128)}) custom-call(bf16[1024,512]{1,0:T(8,128)(2,1)} %copy-done.1, bf16[1024,512]{1,0:T(8,128)(2,1)} %copy-done.2, bf16[512,512]{1,0:T(8,128)(2,1)} %refs_2_.3, bf16[512,512]{1,0:T(8,128)(2,1)} %refs_3_.3, ...), custom_call_target="tpu_custom_call" | custom-call | tf_op jit(solution)/shard_map/ffn/pallas_call | solution.py:216
  42.0 3.4 %collective-permute-done.2.refs_4_ = bf16[1,512]{1,0:T(2,128)(2,1)S(1)} collective-permute-done((bf16[1,512]{1,0:T(2,128)(2,1)S(1)}, bf16[1,512]{1,0:T(2,128)(2,1)S(1)}, u32[]{:S(2)}, u32[]{:S(2)}) %collective-permute-start.2) | collective-permute-done | bytes 1056 | tf_op jit(solution)/shard_map/ppermute | solution.py:357
  46.4 8.5 %ffn.6 = (bf16[1024,512]{1,0:T(8,128)(2,1)}, bf16[1024,512]{1,0:T(8,128)(2,1)}, f32[512,512]{1,0:T(8,128)}, f32[512,512]{1,0:T(8,128)}, f32[1,512]{1,0:T(1,128)}) custom-call(bf16[1024,512]{1,0:T(8,128)(2,1)} %copy-done.1, bf16[1024,512]{1,0:T(8,128)(2,1)} %copy-done.2, bf16[512,512]{1,0:T(8,128)(2,1)} %copy-done.5, bf16[512,512]{1,0:T(8,128)(2,1)} %copy-done.6, ...), custom_call_target="tpu_custom_call" | custom-call | tf_op jit(solution)/shard_map/ffn/pallas_call | solution.py:216
  55.5 9.2 %ffn.7 = (f32[1024,512]{1,0:T(8,128)}, f32[1024,512]{1,0:T(8,128)}, bf16[512,512]{1,0:T(8,128)(2,1)}, bf16[512,512]{1,0:T(8,128)(2,1)}, f32[1,512]{1,0:T(1,128)}) custom-call(bf16[1024,512]{1,0:T(8,128)(2,1)} %get-tuple-element.47.refs_0_, bf16[1024,512]{1,0:T(8,128)(2,1)} %get-tuple-element.48.refs_1_.glow, bf16[512,512]{1,0:T(8,128)(2,1)} %copy-done.5, ...), custom_call_target="tpu_custom_call" | custom-call | tf_op jit(solution)/shard_map/ffn/pallas_call | solution.py:216
  64.7 1.8 %collective-permute-start.17 = (bf16[512,512]{1,0:T(8,128)(2,1)}, bf16[512,512]{1,0:T(8,128)(2,1)S(1)}, u32[]{:S(2)}, u32[]{:S(2)}) collective-permute-start(bf16[512,512]{1,0:T(8,128)(2,1)} %get-tuple-element.77), channel_id=1, source_target_pairs={{0,2},{1,3},{2,0},{3,1},{4,6},{5,7},{6,4},{7,5},{8,10},{9,11},{10,... | collective-permute-start | bytes 1572872 | tf_op jit(solution)/shard_map/ppermute | solution.py:357
  70.1 17.5 %back.1 = (bf16[1024,512]{1,0:T(8,128)(2,1)}, bf16[1024,512]{1,0:T(8,128)(2,1)}, bf16[512,1280]{1,0:T(8,128)(2,1)}) custom-call(f32[1024,512]{1,0:T(8,128)} %get-tuple-element.59.out_own, bf16[1024,512]{1,0:T(8,128)(2,1)} %copy-done.8, f32[1024,512]{1,0:T(8,128)} %get-tuple-element.61.second_own, bf16[1024,512]{1,0:T(8,128)(2,1)} %copy-done.9, ...), custom_call_target="tpu_custom_call" | custom-call | tf_op jit(solution)/shard_map/back/pallas_call | solution.py:345
  89.1 1.9 %collective-permute-start.18 = (bf16[256,512]{1,0:T(8,128)(2,1)S(1)}, bf16[256,512]{1,0:T(8,128)(2,1)S(1)}, u32[]{:S(2)}, u32[]{:S(2)}) collective-permute-start(bf16[256,512]{1,0:T(8,128)(2,1)S(1)} %constant_dynamic-slice_fusion.5), channel_id=1, source_target_pairs={{0,8},{1,9},{2,10},{3,11},{4,12},{5,13},{6,14},{7,15},{8,0},{9,1},... | collective-permute-start | bytes 786440 | tf_op jit(solution)/shard_map/ppermute | solution.py:357
  91.2 1.6 collective-permute-start.25
  93.0 1.6 collective-permute-start.8
  94.5 3.4 %collective-permute-done.18 = bf16[256,512]{1,0:T(8,128)(2,1)S(1)} collective-permute-done((bf16[256,512]{1,0:T(8,128)(2,1)S(1)}, bf16[256,512]{1,0:T(8,128)(2,1)S(1)}, u32[]{:S(2)}, u32[]{:S(2)}) %collective-permute-start.18) | collective-permute-done | bytes 262176 | tf_op jit(solution)/shard_map/ppermute | solution.py:357
  98.0 2.8 %collective-permute-start.19 = (bf16[128,512]{1,0:T(8,128)(2,1)S(1)}, bf16[128,512]{1,0:T(8,128)(2,1)S(1)}, u32[]{:S(2)}, u32[]{:S(2)}) collective-permute-start(bf16[128,512]{1,0:T(8,128)(2,1)S(1)} %constant_dynamic-slice_fusion.4), channel_id=1, source_target_pairs={{0,16},{1,17},{2,18},{3,19},{4,20},{5,21},{6,22},{7,23},{8,24},{9,... | collective-permute-start | bytes 393224 | tf_op jit(solution)/shard_map/ppermute | solution.py:357
  100.9 1.7 %collective-permute-done.8 = bf16[128,1280]{1,0:T(8,128)(2,1)S(1)} collective-permute-done((bf16[128,1280]{1,0:T(8,128)(2,1)S(1)}, bf16[128,1280]{1,0:T(8,128)(2,1)S(1)}, u32[]{:S(2)}, u32[]{:S(2)}) %collective-permute-start.8) | collective-permute-done | bytes 327712 | tf_op jit(solution)/shard_map/ppermute | solution.py:357
  104.7 3.4 %collective-permute-done.9 = bf16[64,1280]{1,0:T(8,128)(2,1)S(1)} collective-permute-done((bf16[64,1280]{1,0:T(8,128)(2,1)S(1)}, bf16[64,1280]{1,0:T(8,128)(2,1)S(1)}, u32[]{:S(2)}, u32[]{:S(2)}) %collective-permute-start.9) | collective-permute-done | bytes 163872 | tf_op jit(solution)/shard_map/ppermute | solution.py:357
  108.7 3.9 %collective-permute-done.10 = bf16[32,1280]{1,0:T(8,128)(2,1)S(1)} collective-permute-done((bf16[32,1280]{1,0:T(8,128)(2,1)S(1)}, bf16[32,1280]{1,0:T(8,128)(2,1)S(1)}, u32[]{:S(2)}, u32[]{:S(2)}) %collective-permute-start.10) | collective-permute-done | bytes 81952 | tf_op jit(solution)/shard_map/ppermute | solution.py:357
  112.7 2.7 %collective-permute-start.11 = (bf16[16,1280]{1,0:T(8,128)(2,1)S(1)}, bf16[16,1280]{1,0:T(8,128)(2,1)S(1)}, u32[]{:S(2)}, u32[]{:S(2)}) collective-permute-start(bf16[16,1280]{1,0:T(8,128)(2,1)S(1)} %constant_dynamic-slice_fusion.6), channel_id=1, source_target_pairs={{0,16},{1,17},{2,18},{3,19},{4,20},{5,21},{6,22},{7,23},{8,24},{9,... | collective-permute-start | bytes 122888 | tf_op jit(solution)/shard_map/ppermute | solution.py:357
  115.9 2.5 %collective-permute-done.11 = bf16[16,1280]{1,0:T(8,128)(2,1)S(1)} collective-permute-done((bf16[16,1280]{1,0:T(8,128)(2,1)S(1)}, bf16[16,1280]{1,0:T(8,128)(2,1)S(1)}, u32[]{:S(2)}, u32[]{:S(2)}) %collective-permute-start.11) | collective-permute-done | bytes 40992 | tf_op jit(solution)/shard_map/ppermute | solution.py:357
  118.4 2.3 %collective-permute-start.12 = (bf16[16,1280]{1,0:T(8,128)(2,1)S(1)}, bf16[16,1280]{1,0:T(8,128)(2,1)S(1)}, u32[]{:S(2)}, u32[]{:S(2)}) collective-permute-start(bf16[16,1280]{1,0:T(8,128)(2,1)S(1)} %add_convert_fusion.12), channel_id=1, source_target_pairs={{0,16},{1,17},{2,18},{3,19},{4,20},{5,21},{6,22},{7,23},{8,24},{9,... | collective-permute-start | bytes 122888 | tf_op jit(solution)/shard_map/ppermute | solution.py:357
  120.7 2.9 %collective-permute-done.12 = bf16[16,1280]{1,0:T(8,128)(2,1)S(1)} collective-permute-done((bf16[16,1280]{1,0:T(8,128)(2,1)S(1)}, bf16[16,1280]{1,0:T(8,128)(2,1)S(1)}, u32[]{:S(2)}, u32[]{:S(2)}) %collective-permute-start.12) | collective-permute-done | bytes 40992 | tf_op jit(solution)/shard_map/ppermute | solution.py:357
  123.8 2.1 %collective-permute-start.27 = (bf16[64,512]{1,0:T(8,128)(2,1)S(1)}, bf16[64,512]{1,0:T(8,128)(2,1)S(1)}, u32[]{:S(2)}, u32[]{:S(2)}) collective-permute-start(bf16[64,512]{1,0:T(8,128)(2,1)S(1)} %constant_dynamic-slice_fusion), channel_id=1, source_target_pairs={{0,16},{1,17},{2,18},{3,19},{4,20},{5,21},{6,22},{7,23},{8,24},{9,... | collective-permute-start | bytes 196616 | tf_op jit(solution)/shard_map/ppermute | solution.py:357
  125.9 2.3 %collective-permute-done.13 = bf16[32,1280]{1,0:T(8,128)(2,1)S(1)} collective-permute-done((bf16[32,1280]{1,0:T(8,128)(2,1)S(1)}, bf16[32,1280]{1,0:T(8,128)(2,1)S(1)}, u32[]{:S(2)}, u32[]{:S(2)}) %collective-permute-start.13) | collective-permute-done | bytes 81952 | tf_op jit(solution)/shard_map/ppermute | solution.py:357
  130.7 3.2 %collective-permute-done.14 = bf16[64,1280]{1,0:T(8,128)(2,1)S(1)} collective-permute-done((bf16[64,1280]{1,0:T(8,128)(2,1)S(1)}, bf16[64,1280]{1,0:T(8,128)(2,1)S(1)}, u32[]{:S(2)}, u32[]{:S(2)}) %collective-permute-start.14) | collective-permute-done | bytes 163872 | tf_op jit(solution)/shard_map/ppermute | solution.py:357
  134.0 1.6 collective-permute-start.15
  135.6 2.0 %collective-permute-start.28 = (bf16[64,512]{1,0:T(8,128)(2,1)S(1)}, bf16[64,512]{1,0:T(8,128)(2,1)S(1)}, u32[]{:S(2)}, u32[]{:S(2)}) collective-permute-start(bf16[64,512]{1,0:T(8,128)(2,1)S(1)} %add_convert_fusion.10), channel_id=1, source_target_pairs={{0,16},{1,17},{2,18},{3,19},{4,20},{5,21},{6,22},{7,23},{8,24},{9,... | collective-permute-start | bytes 196616 | tf_op jit(solution)/shard_map/ppermute | solution.py:357
  138.7 2.8 %collective-permute-done.28 = bf16[64,512]{1,0:T(8,128)(2,1)S(1)} collective-permute-done((bf16[64,512]{1,0:T(8,128)(2,1)S(1)}, bf16[64,512]{1,0:T(8,128)(2,1)S(1)}, u32[]{:S(2)}, u32[]{:S(2)}) %collective-permute-start.28) | collective-permute-done | bytes 65568 | tf_op jit(solution)/shard_map/ppermute | solution.py:357
  143.3 1.7 %collective-permute-done.22 = bf16[128,512]{1,0:T(8,128)(2,1)S(1)} collective-permute-done((bf16[128,512]{1,0:T(8,128)(2,1)S(1)}, bf16[128,512]{1,0:T(8,128)(2,1)S(1)}, u32[]{:S(2)}, u32[]{:S(2)}) %collective-permute-start.22) | collective-permute-done | bytes 131104 | tf_op jit(solution)/shard_map/ppermute | solution.py:357
  146.6 1.7 %collective-permute-start.30 = (bf16[256,512]{1,0:T(8,128)(2,1)S(1)}, bf16[256,512]{1,0:T(8,128)(2,1)S(1)}, u32[]{:S(2)}, u32[]{:S(2)}) collective-permute-start(bf16[256,512]{1,0:T(8,128)(2,1)S(1)} %maximum_select_fusion.6), channel_id=1, source_target_pairs={{0,4},{1,5},{2,6},{3,7},{4,0},{5,1},{6,2},{7,3},{8,12},{9,13},{10,... | collective-permute-start | bytes 786440 | tf_op jit(solution)/shard_map/ppermute | solution.py:357
  148.3 3.8 %collective-permute-done.23 = bf16[256,512]{1,0:T(8,128)(2,1)S(1)} collective-permute-done((bf16[256,512]{1,0:T(8,128)(2,1)S(1)}, bf16[256,512]{1,0:T(8,128)(2,1)S(1)}, u32[]{:S(2)}, u32[]{:S(2)}) %collective-permute-start.23) | collective-permute-done | bytes 262176 | tf_op jit(solution)/shard_map/ppermute | solution.py:357
  156.9 1.6 %fusion.4 = (f32[512,512]{1,0:T(8,128)}, f32[512,512]{1,0:T(8,128)}) fusion(f32[512,1280]{1,0:T(8,128)S(1)} %fusion), kind=kLoop, calls=%fused_computation.49 | loop fusion | bytes 4194304 | tf_op jit(solution)/shard_map/slice | solution.py:525
  (121 shorter events, 33.6 us)
Async XLA Ops:
  7.2 14.9 %copy-start.15 = (bf16[512]{0:T(512)(128)(2,1)S(1)}, bf16[512]{0:T(512)(128)(2,1)}, u32[]{:S(2)}) copy-start(bf16[512]{0:T(512)(128)(2,1)} %param.31) | copy-start | bytes 3076
  18.4 13.9 %collective-permute-start.3 = (bf16[1024,512]{1,0:T(8,128)(2,1)}, bf16[1024,512]{1,0:T(8,128)(2,1)S(1)}, u32[]{:S(2)}, u32[]{:S(2)}) collective-permute-start(bf16[1024,512]{1,0:T(8,128)(2,1)} %get-tuple-element.47.refs_0_), channel_id=1, source_target_pairs={{0,1},{1,0},{2,3},{3,2},{4,5},{5,4},{6,7},{7,6},{8,9},{9,8},{10,11... | collective-permute-start | bytes 3145736 | tf_op jit(solution)/shard_map/ppermute | solution.py:357
  19.0 13.4 %collective-permute-start.4 = (bf16[1024,512]{1,0:T(8,128)(2,1)}, bf16[1024,512]{1,0:T(8,128)(2,1)S(1)}, u32[]{:S(2)}, u32[]{:S(2)}) collective-permute-start(bf16[1024,512]{1,0:T(8,128)(2,1)} %get-tuple-element.48.refs_1_.glow), channel_id=1, source_target_pairs={{0,1},{1,0},{2,3},{3,2},{4,5},{5,4},{6,7},{7,6},{8,9},{9,8},{10,11... | collective-permute-start | bytes 3145736 | tf_op jit(solution)/shard_map/ppermute | solution.py:357
  19.0 26.4 %collective-permute-start = (bf16[512,512]{1,0:T(8,128)(2,1)S(1)}, bf16[512,512]{1,0:T(8,128)(2,1)S(1)}, u32[]{:S(2)}, u32[]{:S(2)}) collective-permute-start(bf16[512,512]{1,0:T(8,128)(2,1)S(1)} %copy-done.3), channel_id=1, source_target_pairs={{0,2},{1,3},{2,0},{3,1},{4,6},{5,7},{6,4},{7,5},{8,10},{9,11},{10,... | collective-permute-start | bytes 1572872 | tf_op jit(solution)/shard_map/ppermute | solution.py:357
  22.0 23.5 %collective-permute-start.1 = (bf16[512,512]{1,0:T(8,128)(2,1)S(1)}, bf16[512,512]{1,0:T(8,128)(2,1)S(1)}, u32[]{:S(2)}, u32[]{:S(2)}) collective-permute-start(bf16[512,512]{1,0:T(8,128)(2,1)S(1)} %copy-done.4), channel_id=1, source_target_pairs={{0,2},{1,3},{2,0},{3,1},{4,6},{5,7},{6,4},{7,5},{8,10},{9,11},{10,... | collective-permute-start | bytes 1572872 | tf_op jit(solution)/shard_map/ppermute | solution.py:357
  22.1 23.4 %collective-permute-start.2 = (bf16[1,512]{1,0:T(2,128)(2,1)S(1)}, bf16[1,512]{1,0:T(2,128)(2,1)S(1)}, u32[]{:S(2)}, u32[]{:S(2)}) collective-permute-start(bf16[1,512]{1,0:T(2,128)(2,1)S(1)} %reshape.72.refs_4_), channel_id=1, source_target_pairs={{0,2},{1,3},{2,0},{3,1},{4,6},{5,7},{6,4},{7,5},{8,10},{9,11},{10,... | collective-permute-start | bytes 3080 | tf_op jit(solution)/shard_map/ppermute | solution.py:357
  54.9 13.9 %collective-permute-start.5 = (bf16[1024,512]{1,0:T(8,128)(2,1)}, bf16[1024,512]{1,0:T(8,128)(2,1)S(1)}, u32[]{:S(2)}, u32[]{:S(2)}) collective-permute-start(bf16[1024,512]{1,0:T(8,128)(2,1)} %get-tuple-element.60), channel_id=1, source_target_pairs={{0,1},{1,0},{2,3},{3,2},{4,5},{5,4},{6,7},{7,6},{8,9},{9,8},{10,11... | collective-permute-start | bytes 3145736 | tf_op jit(solution)/shard_map/ppermute | solution.py:357
  55.0 13.8 %collective-permute-start.6 = (bf16[1024,512]{1,0:T(8,128)(2,1)}, bf16[1024,512]{1,0:T(8,128)(2,1)S(1)}, u32[]{:S(2)}, u32[]{:S(2)}) collective-permute-start(bf16[1024,512]{1,0:T(8,128)(2,1)} %get-tuple-element.62), channel_id=1, source_target_pairs={{0,1},{1,0},{2,3},{3,2},{4,5},{5,4},{6,7},{7,6},{8,9},{9,8},{10,11... | collective-permute-start | bytes 3145736 | tf_op jit(solution)/shard_map/ppermute | solution.py:357
  64.7 24.2 %collective-permute-start.17 = (bf16[512,512]{1,0:T(8,128)(2,1)}, bf16[512,512]{1,0:T(8,128)(2,1)S(1)}, u32[]{:S(2)}, u32[]{:S(2)}) collective-permute-start(bf16[512,512]{1,0:T(8,128)(2,1)} %get-tuple-element.77), channel_id=1, source_target_pairs={{0,2},{1,3},{2,0},{3,1},{4,6},{5,7},{6,4},{7,5},{8,10},{9,11},{10,... | collective-permute-start | bytes 1572872 | tf_op jit(solution)/shard_map/ppermute | solution.py:357
  67.1 23.9 %collective-permute-start.24 = (bf16[512,512]{1,0:T(8,128)(2,1)}, bf16[512,512]{1,0:T(8,128)(2,1)S(1)}, u32[]{:S(2)}, u32[]{:S(2)}) collective-permute-start(bf16[512,512]{1,0:T(8,128)(2,1)} %get-tuple-element.79), channel_id=1, source_target_pairs={{0,2},{1,3},{2,0},{3,1},{4,6},{5,7},{6,4},{7,5},{8,10},{9,11},{10,... | collective-permute-start | bytes 1572872 | tf_op jit(solution)/shard_map/ppermute | solution.py:357
  88.8 3.9 %collective-permute-start.7 = (bf16[256,1280]{1,0:T(8,128)(2,1)S(1)}, bf16[256,1280]{1,0:T(8,128)(2,1)S(1)}, u32[]{:S(2)}, u32[]{:S(2)}) collective-permute-start(bf16[256,1280]{1,0:T(8,128)(2,1)S(1)} %constant_dynamic-slice_fusion.10), channel_id=1, source_target_pairs={{0,1},{1,0},{2,3},{3,2},{4,5},{5,4},{6,7},{7,6},{8,9},{9,8},{10,11... | collective-permute-start | bytes 1966088 | tf_op jit(solution)/shard_map/ppermute | solution.py:357
  89.1 8.8 %collective-permute-start.18 = (bf16[256,512]{1,0:T(8,128)(2,1)S(1)}, bf16[256,512]{1,0:T(8,128)(2,1)S(1)}, u32[]{:S(2)}, u32[]{:S(2)}) collective-permute-start(bf16[256,512]{1,0:T(8,128)(2,1)S(1)} %constant_dynamic-slice_fusion.5), channel_id=1, source_target_pairs={{0,8},{1,9},{2,10},{3,11},{4,12},{5,13},{6,14},{7,15},{8,0},{9,1},... | collective-permute-start | bytes 786440 | tf_op jit(solution)/shard_map/ppermute | solution.py:357
  91.2 12.1 %collective-permute-start.25 = (bf16[256,512]{1,0:T(8,128)(2,1)S(1)}, bf16[256,512]{1,0:T(8,128)(2,1)S(1)}, u32[]{:S(2)}, u32[]{:S(2)}) collective-permute-start(bf16[256,512]{1,0:T(8,128)(2,1)S(1)} %constant_dynamic-slice_fusion.2), channel_id=1, source_target_pairs={{0,4},{1,5},{2,6},{3,7},{4,0},{5,1},{6,2},{7,3},{8,12},{9,13},{10,... | collective-permute-start | bytes 786440 | tf_op jit(solution)/shard_map/ppermute | solution.py:357
  93.0 9.6 %collective-permute-start.8 = (bf16[128,1280]{1,0:T(8,128)(2,1)S(1)}, bf16[128,1280]{1,0:T(8,128)(2,1)S(1)}, u32[]{:S(2)}, u32[]{:S(2)}) collective-permute-start(bf16[128,1280]{1,0:T(8,128)(2,1)S(1)} %constant_dynamic-slice_fusion.9), channel_id=1, source_target_pairs={{0,2},{1,3},{2,0},{3,1},{4,6},{5,7},{6,4},{7,5},{8,10},{9,11},{10,... | collective-permute-start | bytes 983048 | tf_op jit(solution)/shard_map/ppermute | solution.py:357
  98.0 10.6 %collective-permute-start.19 = (bf16[128,512]{1,0:T(8,128)(2,1)S(1)}, bf16[128,512]{1,0:T(8,128)(2,1)S(1)}, u32[]{:S(2)}, u32[]{:S(2)}) collective-permute-start(bf16[128,512]{1,0:T(8,128)(2,1)S(1)} %constant_dynamic-slice_fusion.4), channel_id=1, source_target_pairs={{0,16},{1,17},{2,18},{3,19},{4,20},{5,21},{6,22},{7,23},{8,24},{9,... | collective-permute-start | bytes 393224 | tf_op jit(solution)/shard_map/ppermute | solution.py:357
  102.7 5.4 %collective-permute-start.9 = (bf16[64,1280]{1,0:T(8,128)(2,1)S(1)}, bf16[64,1280]{1,0:T(8,128)(2,1)S(1)}, u32[]{:S(2)}, u32[]{:S(2)}) collective-permute-start(bf16[64,1280]{1,0:T(8,128)(2,1)S(1)} %constant_dynamic-slice_fusion.8), channel_id=1, source_target_pairs={{0,4},{1,5},{2,6},{3,7},{4,0},{5,1},{6,2},{7,3},{8,12},{9,13},{10,... | collective-permute-start | bytes 491528 | tf_op jit(solution)/shard_map/ppermute | solution.py:357
  103.4 17.3 %collective-permute-start.26 = (bf16[128,512]{1,0:T(8,128)(2,1)S(1)}, bf16[128,512]{1,0:T(8,128)(2,1)S(1)}, u32[]{:S(2)}, u32[]{:S(2)}) collective-permute-start(bf16[128,512]{1,0:T(8,128)(2,1)S(1)} %constant_dynamic-slice_fusion.1), channel_id=1, source_target_pairs={{0,8},{1,9},{2,10},{3,11},{4,12},{5,13},{6,14},{7,15},{8,0},{9,1},... | collective-permute-start | bytes 393224 | tf_op jit(solution)/shard_map/ppermute | solution.py:357
  108.1 4.5 %collective-permute-start.10 = (bf16[32,1280]{1,0:T(8,128)(2,1)S(1)}, bf16[32,1280]{1,0:T(8,128)(2,1)S(1)}, u32[]{:S(2)}, u32[]{:S(2)}) collective-permute-start(bf16[32,1280]{1,0:T(8,128)(2,1)S(1)} %constant_dynamic-slice_fusion.7), channel_id=1, source_target_pairs={{0,8},{1,9},{2,10},{3,11},{4,12},{5,13},{6,14},{7,15},{8,0},{9,1},... | collective-permute-start | bytes 245768 | tf_op jit(solution)/shard_map/ppermute | solution.py:357
  112.7 5.7 %collective-permute-start.11 = (bf16[16,1280]{1,0:T(8,128)(2,1)S(1)}, bf16[16,1280]{1,0:T(8,128)(2,1)S(1)}, u32[]{:S(2)}, u32[]{:S(2)}) collective-permute-start(bf16[16,1280]{1,0:T(8,128)(2,1)S(1)} %constant_dynamic-slice_fusion.6), channel_id=1, source_target_pairs={{0,16},{1,17},{2,18},{3,19},{4,20},{5,21},{6,22},{7,23},{8,24},{9,... | collective-permute-start | bytes 122888 | tf_op jit(solution)/shard_map/ppermute | solution.py:357
  115.4 14.2 %collective-permute-start.20 = (bf16[64,512]{1,0:T(8,128)(2,1)S(1)}, bf16[64,512]{1,0:T(8,128)(2,1)S(1)}, u32[]{:S(2)}, u32[]{:S(2)}) collective-permute-start(bf16[64,512]{1,0:T(8,128)(2,1)S(1)} %constant_dynamic-slice_fusion.3), channel_id=1, source_target_pairs={{0,4},{1,5},{2,6},{3,7},{4,0},{5,1},{6,2},{7,3},{8,12},{9,13},{10,... | collective-permute-start | bytes 196616 | tf_op jit(solution)/shard_map/ppermute | solution.py:357
  118.4 5.3 %collective-permute-start.12 = (bf16[16,1280]{1,0:T(8,128)(2,1)S(1)}, bf16[16,1280]{1,0:T(8,128)(2,1)S(1)}, u32[]{:S(2)}, u32[]{:S(2)}) collective-permute-start(bf16[16,1280]{1,0:T(8,128)(2,1)S(1)} %add_convert_fusion.12), channel_id=1, source_target_pairs={{0,16},{1,17},{2,18},{3,19},{4,20},{5,21},{6,22},{7,23},{8,24},{9,... | collective-permute-start | bytes 122888 | tf_op jit(solution)/shard_map/ppermute | solution.py:357
  123.7 4.5 %collective-permute-start.13 = (bf16[32,1280]{1,0:T(8,128)(2,1)S(1)}, bf16[32,1280]{1,0:T(8,128)(2,1)S(1)}, u32[]{:S(2)}, u32[]{:S(2)}) collective-permute-start(bf16[32,1280]{1,0:T(8,128)(2,1)S(1)} %maximum_select_fusion.10), channel_id=1, source_target_pairs={{0,8},{1,9},{2,10},{3,11},{4,12},{5,13},{6,14},{7,15},{8,0},{9,1},... | collective-permute-start | bytes 245768 | tf_op jit(solution)/shard_map/ppermute | solution.py:357
  123.8 11.8 %collective-permute-start.27 = (bf16[64,512]{1,0:T(8,128)(2,1)S(1)}, bf16[64,512]{1,0:T(8,128)(2,1)S(1)}, u32[]{:S(2)}, u32[]{:S(2)}) collective-permute-start(bf16[64,512]{1,0:T(8,128)(2,1)S(1)} %constant_dynamic-slice_fusion), channel_id=1, source_target_pairs={{0,16},{1,17},{2,18},{3,19},{4,20},{5,21},{6,22},{7,23},{8,24},{9,... | collective-permute-start | bytes 196616 | tf_op jit(solution)/shard_map/ppermute | solution.py:357
  128.3 5.6 %collective-permute-start.14 = (bf16[64,1280]{1,0:T(8,128)(2,1)S(1)}, bf16[64,1280]{1,0:T(8,128)(2,1)S(1)}, u32[]{:S(2)}, u32[]{:S(2)}) collective-permute-start(bf16[64,1280]{1,0:T(8,128)(2,1)S(1)} %maximum_select_fusion.7), channel_id=1, source_target_pairs={{0,4},{1,5},{2,6},{3,7},{4,0},{5,1},{6,2},{7,3},{8,12},{9,13},{10,... | collective-permute-start | bytes 491528 | tf_op jit(solution)/shard_map/ppermute | solution.py:357
  129.6 8.0 %collective-permute-start.21 = (bf16[64,512]{1,0:T(8,128)(2,1)S(1)}, bf16[64,512]{1,0:T(8,128)(2,1)S(1)}, u32[]{:S(2)}, u32[]{:S(2)}) collective-permute-start(bf16[64,512]{1,0:T(8,128)(2,1)S(1)} %add_convert_fusion.11), channel_id=1, source_target_pairs={{0,4},{1,5},{2,6},{3,7},{4,0},{5,1},{6,2},{7,3},{8,12},{9,13},{10,... | collective-permute-start | bytes 196616 | tf_op jit(solution)/shard_map/ppermute | solution.py:357
  134.0 9.1 %collective-permute-start.15 = (bf16[128,1280]{1,0:T(8,128)(2,1)S(1)}, bf16[128,1280]{1,0:T(8,128)(2,1)S(1)}, u32[]{:S(2)}, u32[]{:S(2)}) collective-permute-start(bf16[128,1280]{1,0:T(8,128)(2,1)S(1)} %maximum_select_fusion.4), channel_id=1, source_target_pairs={{0,2},{1,3},{2,0},{3,1},{4,6},{5,7},{6,4},{7,5},{8,10},{9,11},{10,... | collective-permute-start | bytes 983048 | tf_op jit(solution)/shard_map/ppermute | solution.py:357
  135.6 5.9 %collective-permute-start.28 = (bf16[64,512]{1,0:T(8,128)(2,1)S(1)}, bf16[64,512]{1,0:T(8,128)(2,1)S(1)}, u32[]{:S(2)}, u32[]{:S(2)}) collective-permute-start(bf16[64,512]{1,0:T(8,128)(2,1)S(1)} %add_convert_fusion.10), channel_id=1, source_target_pairs={{0,16},{1,17},{2,18},{3,19},{4,20},{5,21},{6,22},{7,23},{8,24},{9,... | collective-permute-start | bytes 196616 | tf_op jit(solution)/shard_map/ppermute | solution.py:357
  137.6 7.3 %collective-permute-start.22 = (bf16[128,512]{1,0:T(8,128)(2,1)S(1)}, bf16[128,512]{1,0:T(8,128)(2,1)S(1)}, u32[]{:S(2)}, u32[]{:S(2)}) collective-permute-start(bf16[128,512]{1,0:T(8,128)(2,1)S(1)} %maximum_select_fusion.8), channel_id=1, source_target_pairs={{0,16},{1,17},{2,18},{3,19},{4,20},{5,21},{6,22},{7,23},{8,24},{9,... | collective-permute-start | bytes 393224 | tf_op jit(solution)/shard_map/ppermute | solution.py:357
  141.5 5.1 %collective-permute-start.29 = (bf16[128,512]{1,0:T(8,128)(2,1)S(1)}, bf16[128,512]{1,0:T(8,128)(2,1)S(1)}, u32[]{:S(2)}, u32[]{:S(2)}) collective-permute-start(bf16[128,512]{1,0:T(8,128)(2,1)S(1)} %maximum_select_fusion.9), channel_id=1, source_target_pairs={{0,8},{1,9},{2,10},{3,11},{4,12},{5,13},{6,14},{7,15},{8,0},{9,1},... | collective-permute-start | bytes 393224 | tf_op jit(solution)/shard_map/ppermute | solution.py:357
  143.2 11.3 %collective-permute-start.16 = (bf16[256,1280]{1,0:T(8,128)(2,1)S(1)}, bf16[256,1280]{1,0:T(8,128)(2,1)}, u32[]{:S(2)}, u32[]{:S(2)}) collective-permute-start(bf16[256,1280]{1,0:T(8,128)(2,1)S(1)} %maximum_select_fusion.1), channel_id=1, source_target_pairs={{0,1},{1,0},{2,3},{3,2},{4,5},{5,4},{6,7},{7,6},{8,9},{9,8},{10,11... | collective-permute-start | bytes 1966088 | tf_op jit(solution)/shard_map/ppermute | solution.py:357
  145.0 7.1 %collective-permute-start.23 = (bf16[256,512]{1,0:T(8,128)(2,1)S(1)}, bf16[256,512]{1,0:T(8,128)(2,1)S(1)}, u32[]{:S(2)}, u32[]{:S(2)}) collective-permute-start(bf16[256,512]{1,0:T(8,128)(2,1)S(1)} %maximum_select_fusion.5), channel_id=1, source_target_pairs={{0,8},{1,9},{2,10},{3,11},{4,12},{5,13},{6,14},{7,15},{8,0},{9,1},... | collective-permute-start | bytes 786440 | tf_op jit(solution)/shard_map/ppermute | solution.py:357
  146.6 6.7 %collective-permute-start.30 = (bf16[256,512]{1,0:T(8,128)(2,1)S(1)}, bf16[256,512]{1,0:T(8,128)(2,1)S(1)}, u32[]{:S(2)}, u32[]{:S(2)}) collective-permute-start(bf16[256,512]{1,0:T(8,128)(2,1)S(1)} %maximum_select_fusion.6), channel_id=1, source_target_pairs={{0,4},{1,5},{2,6},{3,7},{4,0},{5,1},{6,2},{7,3},{8,12},{9,13},{10,... | collective-permute-start | bytes 786440 | tf_op jit(solution)/shard_map/ppermute | solution.py:357
  (17 other events, 69.6 us)

commit v2 on v1

v2 whole, which is shorter than its diff:
```python
import functools
import math

import jax
import jax.numpy as jnp
from jax import lax
from jax.experimental import pallas as pl
from jax.experimental.pallas import tpu as pltpu
from jax.sharding import PartitionSpec as P

F32 = jnp.float32
BF16 = jnp.bfloat16
epsilon = 1e-05
AXES = ("dp", "mp")
TILE = 128
BIG = 256
VMEM_LIMIT = 36 << 20
LANES = 128
VECTOR_ROW = 8


def dot(left, right):
    return lax.dot_general(left, right, (((1,), (0,)), ((), ())), preferred_element_type=F32)


def dot_nt(left, right):
    return lax.dot_general(left, right, (((1,), (1,)), ((), ())), preferred_element_type=F32)


def dot_tn(left, right):
    return lax.dot_general(left, right, (((0,), (0,)), ((), ())), preferred_element_type=F32)


def normed(rows_in):
    middle = jnp.mean(rows_in, axis=-1, keepdims=True)
    center = rows_in - middle
    inverse = lax.rsqrt(jnp.mean(center * center, axis=-1, keepdims=True) + epsilon)
    return center * inverse, inverse


def norm_back(grad_normed, gain, normed_hat, inverse):
    scaled = grad_normed * gain
    mean_one = jnp.mean(scaled, axis=-1, keepdims=True)
    mean_two = jnp.mean(scaled * normed_hat, axis=-1, keepdims=True)
    return inverse * (scaled - mean_one - normed_hat * mean_two)


def as_row(vector):
    return vector[...].astype(F32).reshape(1, -1)


def row_sum(values):
    return jnp.sum(values, axis=0, keepdims=True)


def pair_masks(first_id, second_id, pairs):
    half = (lax.broadcasted_iota(jnp.int32, (TILE, LANES), 1) >= LANES // 2).astype(F32)
    low = first_id - half
    high = second_id - half
    return [(low == 2.0 * pair, high == 2.0 * pair) for pair in range(pairs)]


def window_of(tile, tiles):
    width = min(3, tiles)
    return min(max(tile - 1, 0), tiles - width) * TILE, width * TILE


class Copies:
    def __init__(self, semaphores):
        self.semaphores = semaphores
        self.used = 0
        self.pending = {}

    def start(self, name, source, target):
        copy = pltpu.make_async_copy(source, target, self.semaphores.at[self.used])
        self.used += 1
        copy.start()
        self.pending.setdefault(name, []).append(copy)

    def wait(self, *names):
        for name in names:
            for copy in self.pending.pop(name, ()):
                copy.wait()

    def finish(self):
        self.wait(*list(self.pending))


def attend_kernel(
    sent, valid, expert, gain1, shift1, gain2, shift2, router,
    tok_far, wq_far, wkv_far, cot_far, wo_far,
    res_far, low2_far, glow_far, mixed_far, qsel_far, kv_far, chance_far, gates_far,
    tok, wq, wkv, cot, wo,
    res, low2, glow, mixed, qsel, kv, chance, gates,
    queries, logits, semaphores,
):
    rows, width = tok.shape
    tiles = rows // TILE
    pairs = width // LANES
    scale = (wkv.shape[1] // 2) ** -0.5
    copies = Copies(semaphores)
    copies.start("tok", tok_far, tok)
    copies.start("wq", wq_far, wq)
    copies.start("wkv", wkv_far, wkv)
    copies.start("cot", cot_far, cot)
    copies.start("wo", wo_far, wo)
    half_lane = lax.broadcasted_iota(jnp.int32, (BIG, LANES), 1) < LANES // 2
    copies.wait("tok", "wq", "wkv")
    for at in range(0, rows, BIG):
        span = pl.ds(at, BIG)
        hat, _ = normed(tok[span, :].astype(F32))
        low = (hat * as_row(gain1) + as_row(shift1)).astype(BF16)
        queries[span, :] = dot(low, wq[...]).astype(BF16)
        logits[span, :] = dot_nt(low, router[...])
        both = dot(low, wkv[...])
        turned = pltpu.roll(both, LANES // 2, 1)
        kv[span, :LANES] = jnp.where(half_lane, both, turned).astype(BF16)
        kv[span, LANES:] = jnp.where(half_lane, turned, both).astype(BF16)
    copies.start("out", kv, kv_far)
    copies.wait("cot", "wo")
    for tile in range(tiles):
        at = tile * TILE
        span = pl.ds(at, TILE)
        meta = jnp.concatenate(
            [
                sent[:, at : at + TILE],
                valid[:, at : at + TILE],
                expert[:, at : at + TILE],
                jnp.zeros((4, TILE), jnp.int32),
            ],
            axis=0,
        ).astype(F32)
        column = jnp.transpose(meta)
        own_sent, own_valid = column[:, 0:1], column[:, 1:2]
        first_id, second_id = column[:, 2:3], column[:, 3:4]
        glow[span, :] = jnp.where(own_valid > 0.5, cot[span, :].astype(F32), 0.0).astype(BF16)
        scored = logits[span, :]
        slot = lax.broadcasted_iota(jnp.int32, scored.shape, 1).astype(F32)
        pick0 = jnp.sum(jnp.where(slot == first_id, scored, 0.0), axis=-1, keepdims=True)
        pick1 = jnp.sum(jnp.where(slot == second_id, scored, 0.0), axis=-1, keepdims=True)
        most = jnp.maximum(pick0, pick1)
        raise0, raise1 = jnp.exp(pick0 - most), jnp.exp(pick1 - most)
        gate0 = raise0 / (raise0 + raise1)
        gate1 = raise1 / (raise0 + raise1)
        lane = lax.broadcasted_iota(jnp.int32, (TILE, 8), 1)
        gates[:, at : at + TILE] = jnp.transpose(
            jnp.where(
                lane == 0,
                gate0,
                jnp.where(lane == 1, gate1, jnp.where(lane == 2, first_id, second_id)),
            )
        )
        masks = pair_masks(first_id, second_id, pairs)
        q0 = jnp.zeros((TILE, LANES), F32)
        q1 = jnp.zeros((TILE, LANES), F32)
        for pair in range(pairs):
            block = queries[span, pair * LANES : (pair + 1) * LANES].astype(F32)
            q0 = jnp.where(masks[pair][0], block, q0)
            q1 = jnp.where(masks[pair][1], block, q1)
        picked = (jnp.concatenate([q0, q1], axis=0) * scale).astype(BF16)
        qsel[tile] = picked
        start, extent = window_of(tile, tiles)
        near = pl.ds(start, extent)
        scores = dot_nt(picked, kv[near, :LANES])
        same = own_sent == sent[:, start : start + extent].astype(F32)
        same = jnp.concatenate([same, same], axis=0)
        scores = jnp.where(same, scores, -1e30)
        weights = jnp.exp(scores - jnp.max(scores, axis=-1, keepdims=True))
        share = (weights * (1.0 / jnp.sum(weights, axis=-1, keepdims=True))).astype(BF16)
        chance[tile] = share
        context = dot(share, kv[near, LANES:])
        part0 = context[:TILE] * gate0
        part1 = context[TILE:] * gate1
        for pair in range(pairs):
            mixed[span, pair * LANES : (pair + 1) * LANES] = jnp.where(
                masks[pair][0], part0, jnp.where(masks[pair][1], part1, 0.0)
            ).astype(BF16)
        if tile % (tiles // 2) == tiles // 2 - 1:
            done = pl.ds((tile + 1 - tiles // 2), tiles // 2)
            copies.start("out", chance.at[done], chance_far.at[done])
    copies.start("out", glow, glow_far)
    copies.start("out", qsel, qsel_far)
    copies.start("out", mixed, mixed_far)
    copies.start("out", gates, gates_far)
    for at in range(0, rows, BIG):
        span = pl.ds(at, BIG)
        total = tok[span, :].astype(F32) + dot(mixed[span, :], wo[...])
        res[span, :] = total.astype(BF16)
        hat, _ = normed(total)
        low2[span, :] = (hat * as_row(gain2) + as_row(shift2)).astype(BF16)
        if (at + BIG) % (rows // 2) == 0:
            done = pl.ds(at + BIG - rows // 2, rows // 2)
            copies.start("out", low2.at[done, :], low2_far.at[done, :])
            copies.start("out", res.at[done, :], res_far.at[done, :])
    copies.finish()


def ffn_kernel(*refs, units, more):
    low2, glow, weights = refs[:3]
    at = 3
    if "cut" in more:
        mine = refs[at]
        at += 1
    if "rows" in more:
        out_in, second_in = refs[at : at + 2]
        at += 2
    if "weights" in more:
        contract_in, expand_in, bias_in = refs[at : at + 3]
        at += 3
    if "cut" in more:
        out, second, contract_out, keep_out, send_out, bias_out, hidden, grad, uncut = refs[at:]
    else:
        out, second, contract_out, expand_out, bias_out, hidden, grad = refs[at:]
    rows = low2.shape[0]
    contract = weights.at[:units, :]
    expand = weights.at[units + 16 :, :units]
    bias = weights[units : units + 1, :units].astype(F32)
    bias_sum = bias_in[...] if "weights" in more else jnp.zeros((1, units), F32)
    for first in range(0, rows, BIG):
        span = pl.ds(first, BIG)
        preact = dot(low2[span, :], expand[...]) + bias
        cumulative = 0.5 * (1.0 + lax.erf(preact * (1.0 / math.sqrt(2.0))))
        bell = jnp.exp(-0.5 * preact * preact) * (1.0 / math.sqrt(2.0 * math.pi))
        high = (preact * cumulative).astype(BF16)
        hidden[span, :] = high
        slope = cumulative + preact * bell
        low_grad = (dot_nt(glow[span, :], contract[...]) * slope).astype(BF16)
        grad[span, :] = low_grad
        bias_sum += row_sum(low_grad.astype(F32))
        out_part = dot(high, contract[...])
        second_part = dot_nt(low_grad, expand[...])
        if "rows" in more:
            out_part += out_in[span, :].astype(F32)
            second_part += second_in[span, :].astype(F32)
        out[span, :] = out_part.astype(out.dtype)
        second[span, :] = second_part.astype(second.dtype)
    contract_sum = dot_tn(hidden[...], glow[...])
    expand_sum = dot_tn(low2[...], grad[...])
    if "weights" in more:
        contract_sum += contract_in[...]
        expand_sum += expand_in[...]
    contract_out[...] = contract_sum.astype(contract_out.dtype)
    bias_out[...] = bias_sum
    if "cut" in more:
        half = uncut.shape[0] // 2
        uncut[...] = expand_sum.astype(uncut.dtype)
        keep_out[...] = uncut[pl.ds(pl.multiple_of(mine[0] * half, half), half), :]
        send_out[...] = uncut[pl.ds(pl.multiple_of((1 - mine[0]) * half, half), half), :]
    else:
        expand_out[...] = expand_sum.astype(expand_out.dtype)


def ffn(rows_far, low2, glow, weights, weights_far, units, rows_in=None, weights_in=None,
        rows_out=("far", "far"), cut=None, carry="near"):
    rows, width = low2.shape
    more = []
    operands = [low2, glow, weights]
    spaces = [rows_far, rows_far, weights_far]
    if cut is not None:
        more.append("cut")
        operands.append(cut)
        spaces.append("scalar")
    if rows_in is not None:
        more.append("rows")
        operands += rows_in
        spaces += ["far" if rows_far else "near"] * 2
    if weights_in is not None:
        more.append("weights")
        operands += weights_in
        spaces += [carry, carry, "near"]
    scratch = [pltpu.VMEM((rows, units), BF16), pltpu.VMEM((rows, units), BF16)]
    if cut is None:
        sums = [
            jax.ShapeDtypeStruct((units, width), F32), jax.ShapeDtypeStruct((width, units), F32)
        ]
        sums_out = [carry, carry]
    else:
        sums = [jax.ShapeDtypeStruct((units, width), BF16)]
        sums += [jax.ShapeDtypeStruct((width // 2, units), BF16)] * 2
        sums_out = ["far", "far", "far"]
        scratch.append(pltpu.VMEM((width, units), BF16))
    outs = placed_call(
        functools.partial(ffn_kernel, units=units, more=tuple(more)),
        "ffn",
        operands,
        spaces,
        [jax.ShapeDtypeStruct((rows, width), BF16)] * 2
        + sums
        + [jax.ShapeDtypeStruct((1, units), F32)],
        list(rows_out) + sums_out + ["near"],
        scratch,
    )
    return list(outs[:2]), list(outs[2:])


def back_kernel(
    place, second_own, second_got, unit_own, unit_peers,
    res, glow, wo, gates, mixed, kv, chance, qsel, tok, wq, wkv,
    gain1, shift1, gain2, router,
    tok_grad, keep, send,
    packed, low1, grad_res, grad_mixed, grad_q, grad_log, key_sum, value_sum, vectors,
):
    rows, width = tok.shape
    tiles = rows // TILE
    pairs = width // LANES
    scale = (wkv.shape[1] // 2) ** -0.5
    experts = router.shape[0]
    gain_one, gain_two = as_row(gain1), as_row(gain2)
    gain2_sum = shift2_sum = bias_sum = jnp.zeros((1, width), F32)
    for at in range(0, rows, BIG):
        span = pl.ds(at, BIG)
        hat, inverse = normed(res[span, :].astype(F32))
        second = second_own[span, :].astype(F32) + second_got[span, :].astype(F32)
        gain2_sum += row_sum(second * hat)
        shift2_sum += row_sum(second)
        outer = glow[span, :].astype(F32)
        bias_sum += row_sum(outer)
        grad = outer + norm_back(second, gain_two, hat, inverse)
        grad_res[span, :] = grad
        grad_mixed[span, :] = dot_nt(grad.astype(BF16), wo[...])
    packed[:, width : 2 * width] = dot_tn(mixed[...], grad_res[...].astype(BF16)).astype(BF16)
    key_sum[...] = jnp.zeros_like(key_sum)
    value_sum[...] = jnp.zeros_like(value_sum)
    for tile in range(tiles):
        at = tile * TILE
        span = pl.ds(at, TILE)
        column = jnp.transpose(gates[:, at : at + TILE])
        gate0, gate1 = column[:, 0:1], column[:, 1:2]
        first_id, second_id = column[:, 2:3], column[:, 3:4]
        masks = pair_masks(first_id, second_id, pairs)
        g0 = jnp.zeros((TILE, LANES), F32)
        g1 = jnp.zeros((TILE, LANES), F32)
        use0 = jnp.zeros((TILE, LANES), F32)
        use1 = jnp.zeros((TILE, LANES), F32)
        for pair in range(pairs):
            lanes = slice(pair * LANES, (pair + 1) * LANES)
            block = grad_mixed[span, lanes]
            both = block * mixed[span, lanes].astype(F32)
            g0 = jnp.where(masks[pair][0], block, g0)
            g1 = jnp.where(masks[pair][1], block, g1)
            use0 = jnp.where(masks[pair][0], both, use0)
            use1 = jnp.where(masks[pair][1], both, use1)
        use0 = jnp.sum(use0, axis=-1, keepdims=True)
        use1 = jnp.sum(use1, axis=-1, keepdims=True)
        turn = gate1 * use0 - gate0 * use1
        lane = lax.broadcasted_iota(jnp.int32, (TILE, LANES), 1).astype(F32)
        grad_log[span, :] = jnp.where(
            lane == first_id, turn, jnp.where(lane == second_id, -turn, 0.0)
        ).astype(BF16)
        grad_ctx = jnp.concatenate([g0 * gate0, g1 * gate1], axis=0).astype(BF16)
        delta = jnp.concatenate([use0, use1], axis=0)
        start, extent = window_of(tile, tiles)
        near = pl.ds(start, extent)
        grad_share = dot_nt(grad_ctx, kv[near, LANES:])
        share = chance[tile]
        raw = (share.astype(F32) * (grad_share - delta)).astype(BF16)
        grad_query = dot(raw, kv[near, :LANES]) * scale
        for pair in range(pairs):
            grad_q[span, pair * LANES : (pair + 1) * LANES] = jnp.where(
                masks[pair][0],
                grad_query[:TILE],
                jnp.where(masks[pair][1], grad_query[TILE:], 0.0),
            ).astype(BF16)
        key_sum[near, :] += dot_tn(raw, qsel[tile])
        value_sum[near, :] += dot_tn(share, grad_ctx)
    keys, values = key_sum[...], value_sum[...]
    keys = keys + pltpu.roll(keys, LANES // 2, 1)
    values = values + pltpu.roll(values, LANES // 2, 1)
    half_lane = lax.broadcasted_iota(jnp.int32, (rows, LANES), 1) < LANES // 2
    grad_kv = jnp.where(half_lane, keys, values).astype(BF16)
    gain1_sum = shift1_sum = jnp.zeros((1, width), F32)
    for at in range(0, rows, BIG):
        span = pl.ds(at, BIG)
        hat, inverse = normed(tok[span, :].astype(F32))
        low1[span, :] = (hat * gain_one + as_row(shift1)).astype(BF16)
        grad = (
            dot_nt(grad_q[span, :], wq[...])
            + dot_nt(grad_kv[at : at + BIG], wkv[...])
            + dot(grad_log[span, :experts], router[...])
        )
        gain1_sum += row_sum(grad * hat)
        shift1_sum += row_sum(grad)
        tok_grad[span, :] = (grad_res[span, :] + norm_back(grad, gain_one, hat, inverse)).astype(
            BF16
        )
    packed[:, :width] = dot_tn(low1[...], grad_q[...]).astype(BF16)
    packed[:, 2 * width : 2 * width + LANES] = dot_tn(low1[...], grad_kv).astype(BF16)
    vectors[...] = jnp.zeros_like(vectors)
    sums = (gain1_sum, shift1_sum, gain2_sum, shift2_sum, bias_sum)
    for at, values in enumerate(sums):
        vectors[VECTOR_ROW + at : VECTOR_ROW + at + 1, :] = values
    units = unit_own.shape[1]
    own = place[0]
    for step in range(unit_peers.shape[0] + 1):
        owner = own ^ (2 * step)
        part = unit_own[...] if step == 0 else unit_peers[step - 1 : step, :]
        vectors[pl.ds(VECTOR_ROW + len(sums) + owner, 1), :units] = part
    packed[:, 2 * width + LANES :] = (
        dot_tn(low1[...], grad_log[...]) + jnp.transpose(vectors[...])
    ).astype(BF16)
    half = width // 2
    mine = own % 2
    keep[...] = packed[pl.ds(pl.multiple_of(mine * half, half), half), :]
    send[...] = packed[pl.ds(pl.multiple_of((1 - mine) * half, half), half), :]


def unpack_kernel(place, mine, other, gain1, shift1, router, query, output, keyval, gain2, shift2, unit, bias):
    half, width = mine.shape[0], query.shape[1]
    for end, values in ((place[0] % 2, mine), (1 - place[0] % 2, other)):
        span = pl.ds(pl.multiple_of(end * half, half), half)
        query[span, :] = values[:, :width].astype(F32)
        output[span, :] = values[:, width : 2 * width].astype(F32)
        keyval[span, :] = values[:, 2 * width : 2 * width + LANES].astype(F32)
        router[span, :] = values[:, 2 * width + LANES :].astype(F32)
    rows = jnp.transpose(router[...])
    for at, target in enumerate((gain1, shift1, gain2, shift2, bias)):
        target[...] = rows[VECTOR_ROW + at : VECTOR_ROW + at + 1, :]
    owner = lax.broadcasted_iota(jnp.int32, rows.shape, 0) - (VECTOR_ROW + 5)
    unit[...] = jnp.sum(jnp.where(owner == place[0], rows, 0.0), axis=0, keepdims=True)[
        :, : unit.shape[1]
    ]


def far_call(kernel, name, near, far, out_shape, scratch, copies):
    buffers = [pltpu.VMEM(item.shape, item.dtype) for item in list(far) + list(out_shape)]
    return pl.pallas_call(
        kernel,
        out_shape=[pltpu.HBM(item.shape, item.dtype) for item in out_shape],
        in_specs=[pl.BlockSpec(memory_space=pltpu.VMEM)] * len(near)
        + [pl.BlockSpec(memory_space=pl.ANY)] * len(far),
        out_specs=[pl.BlockSpec(memory_space=pl.ANY)] * len(out_shape),
        scratch_shapes=buffers + scratch + [pltpu.SemaphoreType.DMA((copies,))],
        compiler_params=pltpu.CompilerParams(vmem_limit_bytes=VMEM_LIMIT),
        cost_estimate=pl.CostEstimate(flops=1000, bytes_accessed=1000, transcendentals=0),
        name=name,
    )(
        *[pltpu.with_memory_space_constraint(item, pltpu.HBM) for item in near],
        *[pltpu.with_memory_space_constraint(item, pltpu.HBM) for item in far],
    )


def placed_call(kernel, name, operands, spaces, out_shape, out_spaces, scratch):
    where = {"far": pltpu.HBM, "near": pltpu.VMEM}
    lies = [pltpu.SMEM if space == "scalar" else pltpu.VMEM for space in spaces]
    operands = [
        pltpu.with_memory_space_constraint(item, where[space]) if space in where else item
        for item, space in zip(operands, spaces)
    ]
    results = [
        where[space](item.shape, item.dtype) if space in where else item
        for item, space in zip(out_shape, out_spaces)
    ]
    return pl.pallas_call(
        kernel,
        out_shape=results,
        in_specs=[pl.BlockSpec(memory_space=space) for space in lies],
        out_specs=[pl.BlockSpec(memory_space=pltpu.VMEM)] * len(results),
        scratch_shapes=scratch,
        compiler_params=pltpu.CompilerParams(vmem_limit_bytes=VMEM_LIMIT),
        cost_estimate=pl.CostEstimate(flops=1000, bytes_accessed=1000, transcendentals=0),
        name=name,
    )(*operands)


def swap(values, bit, devices):
    return lax.ppermute(values, AXES, [(at, at ^ bit) for at in range(devices)])


def halves(values, mine):
    size = values.shape[0] // 2
    keep = lax.dynamic_slice_in_dim(values, mine * size, size, 0)
    send = lax.dynamic_slice_in_dim(values, (1 - mine) * size, size, 0)
    return keep, send


def add_low(left, right):
    return (left.astype(F32) + right.astype(F32)).astype(BF16)


def scatter_sum(values, bits, place, devices, cut=None):
    if not bits:
        return values
    mines = [(place // bit) % 2 for bit in bits]
    keep, send = halves(values, mines[0]) if cut is None else cut
    for at, bit in enumerate(bits):
        got = swap(send, bit, devices)
        if at + 1 < len(bits):
            (keep, send), (keep_got, send_got) = (
                halves(item, mines[at + 1]) for item in (keep, got)
            )
            send = add_low(send, send_got)
            keep = add_low(keep, keep_got)
        else:
            values = add_low(keep, got)
    return values


def all_sum(values, bits, place, devices, whole=1):
    cut, full = bits[: len(bits) - whole], bits[len(bits) - whole :]
    values = scatter_sum(values, cut, place, devices)
    values = whole_sum(values, full, devices)
    return gather(values, cut, place, devices)


def whole_sum(values, bits, devices):
    for bit in bits:
        values = add_low(values, swap(values, bit, devices))
    return values


def joined(values, got, mine):
    return jnp.where(
        mine == 0,
        jnp.concatenate([values, got], axis=0),
        jnp.concatenate([got, values], axis=0),
    )


def gather(values, bits, place, devices):
    for bit in reversed(bits):
        values = joined(values, swap(values, bit, devices), (place // bit) % 2)
    return values


def shards(
    n_dp,
    n_mp,
    tokens,
    sentence_ids,
    validity,
    expert_ids,
    cotangent,
    first_gain,
    first_shift,
    router,
    query_weight,
    output_weight,
    keyval_weight,
    second_gain,
    second_shift,
    expand_weight,
    expand_bias,
    contract_weight,
    contract_bias,
):
    devices = n_dp * n_mp
    rows, width = tokens.shape
    units = expand_weight.shape[1]
    tiles = rows // TILE
    _, extent = window_of(0, tiles)
    place = lax.axis_index(AXES)
    mp_place = lax.axis_index("mp")

    def row(vector):
        return vector.reshape(1, -1)

    def shape(*dims, dtype=BF16):
        return jax.ShapeDtypeStruct(dims, dtype)

    bias_rows = jnp.broadcast_to(jnp.pad(expand_bias, (0, width - units))[None], (16, width))
    wide_expand = jnp.pad(expand_weight, ((0, 0), (0, width - units)))
    own = jnp.concatenate([contract_weight, bias_rows, wide_expand], axis=0)
    turned_router = router.T
    chips = n_mp // 2
    others = [swap(own, 2 * step, devices) for step in range(1, chips)]
    res, low2, glow, mixed, qsel, kv, chance, gates = far_call(
        attend_kernel,
        "attend",
        [
            row(sentence_ids), row(validity), expert_ids.T, first_gain, first_shift, second_gain,
            second_shift, turned_router,
        ],
        [tokens, query_weight, keyval_weight, cotangent, output_weight],
        [
            shape(rows, width),
            shape(rows, width),
            shape(rows, width),
            shape(rows, width),
            shape(tiles, 2 * TILE, LANES),
            shape(rows, 2 * LANES),
            shape(tiles, 2 * TILE, extent),
            shape(8, rows, dtype=F32),
        ],
        [pltpu.VMEM((rows, width), BF16), pltpu.VMEM((rows, router.shape[1]), F32)],
        20,
    )
    low2_pair = swap(low2, 1, devices)
    glow_pair = swap(glow, 1, devices)
    dp_bits = [n_mp << at for at in range(n_dp.bit_length() - 1)]
    mp_bits = [1 << at for at in range(n_mp.bit_length() - 1)]
    first_bit = dp_bits[min(1, len(dp_bits) - 1)]
    later_bits = [bit for bit in dp_bits if bit != first_bit]
    first_mine = jnp.full((1,), (place // first_bit) % 2, jnp.int32)
    rows_own, grads_own = ffn("far", low2, glow, own, "far", units, carry="far")
    rows_pair, grads_own = ffn(
        None, low2_pair, glow_pair, own, "far", units, weights_in=grads_own, rows_out=(None, None),
        cut=first_mine, carry="far",
    )
    contract_sum, expand_keep, expand_send, unit_own = grads_own
    unit_peers = []
    waiting = []
    for step in range(1, chips):
        final = step == chips - 1
        rows_pair, grads = ffn(
            None,
            low2_pair,
            glow_pair,
            others[step - 1],
            None,
            units,
            rows_in=rows_pair,
            rows_out=(None, None),
            carry="far",
        )
        if final:
            out_got, second_got = (swap(item, 1, devices) for item in rows_pair)
        rows_own, grads = ffn(
            "far",
            low2,
            glow,
            others[step - 1],
            None,
            units,
            rows_in=rows_own,
            weights_in=grads,
            rows_out=("far", "near" if final else "far"),
            cut=first_mine,
            carry="far",
        )
        contract_part, keep, send, unit_part = grads
        unit_peers.append(unit_part)
        contract_got = swap(contract_part, 2 * step, devices)
        waiting.append((contract_got, keep, swap(send, first_bit, devices)))
    expand_got = swap(expand_send, first_bit, devices)
    scalars = jnp.full((1,), mp_place, jnp.int32)
    tok_grad, keep, send = placed_call(
        back_kernel,
        "back",
        [
            scalars, rows_own[1], second_got, unit_own, jnp.concatenate(unit_peers, axis=0),
            res, glow, output_weight, gates, mixed, kv, chance, qsel, tokens, query_weight,
            keyval_weight, first_gain, first_shift, second_gain, turned_router,
        ],
        ["scalar", "near", None, None, None] + ["far"] * 15,
        [shape(rows, width)] + [shape(width // 2, 2 * width + 2 * LANES)] * 2,
        ["far", "near", "near"],
        [
            pltpu.VMEM((width, 2 * width + 2 * LANES), BF16),
            pltpu.VMEM((rows, width), BF16),
            pltpu.VMEM((rows, width), F32),
            pltpu.VMEM((rows, width), F32),
            pltpu.VMEM((rows, width), BF16),
            pltpu.VMEM((rows, LANES), BF16),
            pltpu.VMEM((rows, LANES), F32),
            pltpu.VMEM((rows, LANES), F32),
            pltpu.VMEM((LANES, width), F32),
        ],
    )
    send, expand_got, waiting = lax.optimization_barrier((send, expand_got, waiting))
    expand_sum = add_low(expand_keep, expand_got)
    for step in range(1, chips):
        contract_got, peer_keep, peer_got = waiting[step - 1]
        contract_sum = add_low(contract_sum, contract_got)
        expand_part = add_low(peer_keep, peer_got)
        expand_sum = add_low(expand_sum, swap(expand_part, 2 * step, devices))
    order = mp_bits + dp_bits
    cut, full = order[:-2], order[-2:]
    packed = scatter_sum(None, cut, place, devices, (keep, send))
    layer = (
        res.astype(F32) + rows_own[0].astype(F32) + out_got.astype(F32) + contract_bias.astype(F32)
    ).astype(BF16)
    contract_grad = all_sum(contract_sum, dp_bits, place, devices).astype(F32)
    expand_sum = all_sum(expand_sum, later_bits, place, devices)
    expand_grad = gather(expand_sum, [first_bit], place, devices).astype(F32)
    packed = gather(whole_sum(packed, full, devices), cut[1:], place, devices)
    other = swap(packed, mp_bits[0], devices)
    square = shape(width, width, dtype=F32)
    line = shape(1, width, dtype=F32)
    (
        gain1_grad, shift1_grad, router_grad, query_grad, output_grad, keyval_grad, gain2_grad,
        shift2_grad, unit_grad, bias_grad,
    ) = placed_call(
        unpack_kernel,
        "unpack",
        [scalars, packed, other],
        ["scalar", None, None],
        [
            line, line, shape(width, LANES, dtype=F32), square, square,
            shape(width, LANES, dtype=F32), line, line, shape(1, units, dtype=F32), line,
        ],
        [None] * 10,
        [],
    )
    return (
        layer,
        tok_grad,
        gain1_grad[0],
        shift1_grad[0],
        router_grad[:, : router.shape[1]],
        query_grad,
        output_grad,
        keyval_grad,
        gain2_grad[0],
        shift2_grad[0],
        expand_grad,
        unit_grad[0],
        contract_grad,
        bias_grad[0],
    )


def solution(mesh):
    tokens_spec = P(AXES, None)
    placed = (
        tokens_spec,
        P(AXES),
        P(AXES),
        tokens_spec,
        tokens_spec,
        P(),
        P(),
        P(),
        P(),
        P(),
        P(),
        P(),
        P(),
        P(None, "mp"),
        P("mp"),
        P("mp", None),
        P(),
    )
    return jax.shard_map(
        functools.partial(shards, mesh.shape["dp"], mesh.shape["mp"]),
        mesh=mesh,
        in_specs=placed,
        out_specs=(
            tokens_spec,
            tokens_spec,
            P(),
            P(),
            P(),
            P(),
            P(),
            P(),
            P(),
            P(),
            P(None, "mp"),
            P("mp"),
            P("mp", None),
            P(),
        ),
        check_vma=False,
    )
```

time: 162 us -> 128 us (0.79)
  local copies, waits for them, and re-layouts: 17.5 us -> 2.4 us
  starting transfers between devices: 36.8 us -> 25.6 us
  Pallas kernels: 63.1 us -> 53.6 us
  other arithmetic: 6.53 us -> 8.26 us
    ppermute x31 -> x26, starting transfers between devices: 36.8 us -> 25.6 us  [swap(): return lax.ppermute(values, AXES, [(at, at ^ bit) for at in range(devices)])]
    pallas_call x6 -> x7, Pallas kernels: 63.1 us -> 53.6 us  [the longest x6 42.2 us: placed_call(): pl.pallas_call(kernel, out_shape=results, in_specs=[pl.BlockSpec(memory_s...]
    reshape x6 -> x0, local copies, waits for them, and re-layouts: 5.62 us -> none  [row(): return vector.reshape(1, -1)]
    unnamed x36 -> x29, local copies, waits for them, and re-layouts: 5.78 us -> 1.67 us
    slice x5 -> x0, local copies, waits for them, and re-layouts: 3.85 us -> none  [the longest x1 1.64 us: shards(): packed[:, width:2 * width]]
    concatenate x0 -> x1, other arithmetic: none -> 2.24 us  [shards(): own = jnp.concatenate([contract_weight, bias_rows, wide_expand], axis=0)]
    convert_element_type x16 -> x17, other arithmetic: 4.77 us -> 5.71 us  [the longest x13 1.92 us: add_low(): return (left.astype(F32) + right.astype(F32)).astype(BF16)]
    ppermute x31 -> x26, waiting for transfers between devices: 36.6 us -> 36.9 us  [swap(): return lax.ppermute(values, AXES, [(at, at ^ bit) for at in range(devices)])]
  transfers between devices with their start and end apart: 31 -> 26, of which waited for: 13 -> 10; matrix products, arithmetic and copies ran while one was open for 4% -> 5% of each run, Pallas kernels for 27% -> 37%
where the time goes in v2:
time: 128 us
  Pallas kernels  53.6 us (42%)
  waiting for transfers between devices  36.9 us (29%)
  starting transfers between devices  25.6 us (20%)
  other arithmetic  8.26 us (6%)
  local copies, waits for them, and re-layouts  2.4 us (2%)
    pallas_call x6, Pallas kernels, placed_call(): pl.pallas_call(kernel, out_shape=results, in_specs=[pl.BlockSpec(memory_s...  42.2 us
    ppermute x26, waiting for transfers between devices, swap(): return lax.ppermute(values, AXES, [(at, at ^ bit) for at in range(devices)])  36.9 us
    ppermute x26, starting transfers between devices, swap(): return lax.ppermute(values, AXES, [(at, at ^ bit) for at in range(devices)])  25.6 us
    pallas_call x1, Pallas kernels, far_call(): pl.pallas_call(kernel, out_shape=[pltpu.HBM(item.shape, item.dtype) for i...  11.4 us
  transfers between devices with their start and end apart: 26, of which 10 were waited for; matrix products, arithmetic and copies ran while one was open for 5% of the time, Pallas kernels for 37%

profile of v2, /device:TPU:0, one launch (start us, length us, event | category | flops | bytes accessed | tf_op | source)
XLA Modules:
  0.0 127.8 jit_solution(12218429635083608082)
XLA Ops:
  1.3 2.2 %pad_maximum_fusion.refs_2_ = bf16[1040,512]{1,0:T(8,128)(2,1)} fusion(bf16[512,512]{1,0:T(8,128)(2,1)} %param.30, bf16[16,512]{1,0:T(8,128)(2,1)S(1)} %broadcast_in_dim.6, bf16[512,512]{1,0:T(8,128)(2,1)} %param.32), kind=kLoop, calls=%fused_computation.1 | loop fusion | flops 3194880 | bytes 2129920 | tf_op jit(solution)/shard_map/concatenate | solution.py:562
  3.6 2.9 %collective-permute-start = (bf16[1040,512]{1,0:T(8,128)(2,1)}, bf16[1040,512]{1,0:T(8,128)(2,1)S(1)}, u32[]{:S(2)}, u32[]{:S(2)}) collective-permute-start(bf16[1040,512]{1,0:T(8,128)(2,1)} %pad_maximum_fusion.refs_2_), channel_id=1, source_target_pairs={{0,2},{1,3},{2,0},{3,1},{4,6},{5,7},{6,4},{7,5},{8,10},{9,11},{10,... | collective-permute-start | bytes 3194888 | tf_op jit(solution)/shard_map/ppermute | solution.py:466
  6.5 11.4 %attend.1 = (bf16[1024,512]{1,0:T(8,128)(2,1)}, bf16[1024,512]{1,0:T(8,128)(2,1)}, bf16[1024,512]{1,0:T(8,128)(2,1)}, bf16[1024,512]{1,0:T(8,128)(2,1)}, bf16[8,...) custom-call(s32[1,1024]{1,0:T(1,128)} %bitcast.17, ...), custom_call_target="tpu_custom_call" | custom-call | flops 1000 | bytes 1000 | tf_op jit(solution)/shard_map/attend/pallas_call | solution.py:426
  18.5 6.6 %ffn.4 = (bf16[1024,512]{1,0:T(8,128)(2,1)}, bf16[1024,512]{1,0:T(8,128)(2,1)}, f32[512,512]{1,0:T(8,128)}, f32[512,512]{1,0:T(8,128)}, f32[1,512]{1,0:T(1,128)S(1)}) custom-call(bf16[1024,512]{1,0:T(8,128)(2,1)} %get-tuple-element.63.refs_0_, bf16[1024,512]{1,0:T(8,128)(2,1)} %get-tuple-element.64.refs_1_.glow, bf16[1040,512]{1,0:T(8,128)(2,1)} %pad_maximum_fusion.refs_2_), custom_call_target="tpu_custom_call" | custom-call | flops 1000 | bytes 1000 | tf_op jit(solution)/shard_map/ffn/pallas_call | solution.py:453
  25.1 6.6 %ffn.5 = (bf16[1024,512]{1,0:T(8,128)(2,1)S(1)}, bf16[1024,512]{1,0:T(8,128)(2,1)S(1)}, bf16[512,512]{1,0:T(8,128)(2,1)}, bf16[256,512]{1,0:T(8,128)(2,1)}, bf16...) custom-call(bf16[1024,512]{1,0:T(8,128)(2,1)S(1)} %collective-permute-done.1.refs_0_, ...), custom_call_target="tpu_custom_call" | custom-call | flops 1000 | bytes 1000 | tf_op jit(solution)/shard_map/ffn/pallas_call | solution.py:453
  31.7 4.8 %ffn.6 = (bf16[1024,512]{1,0:T(8,128)(2,1)S(1)}, bf16[1024,512]{1,0:T(8,128)(2,1)S(1)}, f32[512,512]{1,0:T(8,128)}, f32[512,512]{1,0:T(8,128)}, f32[1,512]{1,0:T(1,128)S(1)}) custom-call(bf16[1024,512]{1,0:T(8,128)(2,1)S(1)} %collective-permute-done.1.refs_0_, bf16[1024,512]{1,0:T(8,128)(2,1)S(1)} %collective-permute-done.2.refs_1_, ...), custom_call_target="tpu_custom_call" | custom-call | flops 1000 | bytes 1000 | tf_op jit(solution)/shard_map/ffn/pallas_call | solution.py:453
  36.7 7.8 %ffn.7 = (bf16[1024,512]{1,0:T(8,128)(2,1)}, bf16[1024,512]{1,0:T(8,128)(2,1)S(1)}, bf16[512,512]{1,0:T(8,128)(2,1)}, bf16[256,512]{1,0:T(8,128)(2,1)}, bf16[256,512]{1,0:T(8,128)(2,1)}, /*index=5*/f32[1,512]{1,0:T(1,128)S(1)}) custom-call(bf16[1024,512]{1,0:T(8,128)(2,1)} %get-tuple-element.63.refs_0_, bf16[1024,512]{1,0:T(8,128)(2,1)} %get-tuple-element.64.refs_1_.glow, ...), custom_call_target="tpu_custom_call" | custom-call | flops 1000 | bytes 1000 | tf_op jit(solution)/shard_map/ffn/pallas_call | solution.py:453
  44.7 1.9 %collective-permute-start.5 = (bf16[256,512]{1,0:T(8,128)(2,1)S(1)}, bf16[256,512]{1,0:T(8,128)(2,1)S(1)}, u32[]{:S(2)}, u32[]{:S(2)}) collective-permute-start(bf16[256,512]{1,0:T(8,128)(2,1)S(1)} %copy-done.13), channel_id=1, source_target_pairs={{0,8},{1,9},{2,10},{3,11},{4,12},{5,13},{6,14},{7,15},{8,0},{9,1},... | collective-permute-start | bytes 786440 | tf_op jit(solution)/shard_map/ppermute | solution.py:466
  46.8 14.7 %back.1 = (bf16[1024,512]{1,0:T(8,128)(2,1)}, bf16[256,1280]{1,0:T(8,128)(2,1)S(1)}, bf16[256,1280]{1,0:T(8,128)(2,1)S(1)}) custom-call(s32[1]{0:T(128)} %bitcast.5.place, bf16[1024,512]{1,0:T(8,128)(2,1)S(1)} %get-tuple-element.77.second_own, bf16[1024,512]{1,0:T(8,128)(2,1)S(1)} %collective-permute-done.4.second_got, ...), custom_call_target="tpu_custom_call" | custom-call | flops 1000 | bytes 1000 | tf_op jit(solution)/shard_map/back/pallas_call | solution.py:453
  63.0 1.2 add_convert_fusion.1
  64.3 1.9 %collective-permute-start.21 = (bf16[256,512]{1,0:T(8,128)(2,1)S(1)}, bf16[256,512]{1,0:T(8,128)(2,1)S(1)}, u32[]{:S(2)}, u32[]{:S(2)}) collective-permute-start(bf16[256,512]{1,0:T(8,128)(2,1)S(1)} %constant_dynamic-slice_fusion), channel_id=1, source_target_pairs={{0,4},{1,5},{2,6},{3,7},{4,0},{5,1},{6,2},{7,3},{8,12},{9,13},{10,... | collective-permute-start | bytes 786440 | tf_op jit(solution)/shard_map/ppermute | solution.py:466
  66.3 1.6 %collective-permute-start.9 = (bf16[128,1280]{1,0:T(8,128)(2,1)S(1)}, bf16[128,1280]{1,0:T(8,128)(2,1)S(1)}, u32[]{:S(2)}, u32[]{:S(2)}) collective-permute-start(bf16[128,1280]{1,0:T(8,128)(2,1)S(1)} %get-tuple-element.125), channel_id=1, source_target_pairs={{0,2},{1,3},{2,0},{3,1},{4,6},{5,7},{6,4},{7,5},{8,10},{9,11},{10,... | collective-permute-start | bytes 983048 | tf_op jit(solution)/shard_map/ppermute | solution.py:466
  68.6 4.2 %collective-permute-done.21 = bf16[256,512]{1,0:T(8,128)(2,1)S(1)} collective-permute-done((bf16[256,512]{1,0:T(8,128)(2,1)S(1)}, bf16[256,512]{1,0:T(8,128)(2,1)S(1)}, u32[]{:S(2)}, u32[]{:S(2)}) %collective-permute-start.21) | collective-permute-done | bytes 262176 | tf_op jit(solution)/shard_map/ppermute | solution.py:466
  72.8 1.9 %collective-permute-start.22 = (bf16[128,512]{1,0:T(8,128)(2,1)S(1)}, bf16[128,512]{1,0:T(8,128)(2,1)S(1)}, u32[]{:S(2)}, u32[]{:S(2)}) collective-permute-start(bf16[128,512]{1,0:T(8,128)(2,1)S(1)} %add_convert_fusion.14), channel_id=1, source_target_pairs={{0,8},{1,9},{2,10},{3,11},{4,12},{5,13},{6,14},{7,15},{8,0},{9,1},... | collective-permute-start | bytes 393224 | tf_op jit(solution)/shard_map/ppermute | solution.py:466
  74.7 2.3 %collective-permute-done.9 = bf16[128,1280]{1,0:T(8,128)(2,1)S(1)} collective-permute-done((bf16[128,1280]{1,0:T(8,128)(2,1)S(1)}, bf16[128,1280]{1,0:T(8,128)(2,1)S(1)}, u32[]{:S(2)}, u32[]{:S(2)}) %collective-permute-start.9) | collective-permute-done | bytes 327712 | tf_op jit(solution)/shard_map/ppermute | solution.py:466
  77.3 4.2 %collective-permute-done.16 = bf16[256,512]{1,0:T(8,128)(2,1)S(1)} collective-permute-done((bf16[256,512]{1,0:T(8,128)(2,1)S(1)}, bf16[256,512]{1,0:T(8,128)(2,1)S(1)}, u32[]{:S(2)}, u32[]{:S(2)}) %collective-permute-start.16) | collective-permute-done | bytes 262176 | tf_op jit(solution)/shard_map/ppermute | solution.py:466
  82.5 1.6 %collective-permute-start.11 = (bf16[64,1280]{1,0:T(8,128)(2,1)S(1)}, bf16[64,1280]{1,0:T(8,128)(2,1)S(1)}, u32[]{:S(2)}, u32[]{:S(2)}) collective-permute-start(bf16[64,1280]{1,0:T(8,128)(2,1)S(1)} %add_convert_fusion.9), channel_id=1, source_target_pairs={{0,8},{1,9},{2,10},{3,11},{4,12},{5,13},{6,14},{7,15},{8,0},{9,1},... | collective-permute-start | bytes 491528 | tf_op jit(solution)/shard_map/ppermute | solution.py:466
  84.2 2.6 %collective-permute-start.23 = (bf16[128,512]{1,0:T(8,128)(2,1)S(1)}, bf16[128,512]{1,0:T(8,128)(2,1)S(1)}, u32[]{:S(2)}, u32[]{:S(2)}) collective-permute-start(bf16[128,512]{1,0:T(8,128)(2,1)S(1)} %add_convert_fusion.13), channel_id=1, source_target_pairs={{0,16},{1,17},{2,18},{3,19},{4,20},{5,21},{6,22},{7,23},{8,24},{9,... | collective-permute-start | bytes 393224 | tf_op jit(solution)/shard_map/ppermute | solution.py:466
  86.9 2.6 %collective-permute-done.11 = bf16[64,1280]{1,0:T(8,128)(2,1)S(1)} collective-permute-done((bf16[64,1280]{1,0:T(8,128)(2,1)S(1)}, bf16[64,1280]{1,0:T(8,128)(2,1)S(1)}, u32[]{:S(2)}, u32[]{:S(2)}) %collective-permute-start.11) | collective-permute-done | bytes 163872 | tf_op jit(solution)/shard_map/ppermute | solution.py:466
  89.5 1.8 %collective-permute-start.12 = (bf16[64,1280]{1,0:T(8,128)(2,1)S(1)}, bf16[64,1280]{1,0:T(8,128)(2,1)S(1)}, u32[]{:S(2)}, u32[]{:S(2)}) collective-permute-start(bf16[64,1280]{1,0:T(8,128)(2,1)S(1)} %add_convert_fusion.8), channel_id=1, source_target_pairs={{0,16},{1,17},{2,18},{3,19},{4,20},{5,21},{6,22},{7,23},{8,24},{9,... | collective-permute-start | bytes 491528 | tf_op jit(solution)/shard_map/ppermute | solution.py:466
  91.3 1.3 %collective-permute-start.18 = (bf16[128,512]{1,0:T(8,128)(2,1)S(1)}, bf16[128,512]{1,0:T(8,128)(2,1)S(1)}, u32[]{:S(2)}, u32[]{:S(2)}) collective-permute-start(bf16[128,512]{1,0:T(8,128)(2,1)S(1)} %add_convert_fusion.17), channel_id=1, source_target_pairs={{0,16},{1,17},{2,18},{3,19},{4,20},{5,21},{6,22},{7,23},{8,24},{9,... | collective-permute-start | bytes 393224 | tf_op jit(solution)/shard_map/ppermute | solution.py:466
  92.6 10.0 %collective-permute-done.12 = bf16[64,1280]{1,0:T(8,128)(2,1)S(1)} collective-permute-done((bf16[64,1280]{1,0:T(8,128)(2,1)S(1)}, bf16[64,1280]{1,0:T(8,128)(2,1)S(1)}, u32[]{:S(2)}, u32[]{:S(2)}) %collective-permute-start.12) | collective-permute-done | bytes 163872 | tf_op jit(solution)/shard_map/ppermute | solution.py:466
  102.7 1.3 %collective-permute-start.13 = (bf16[64,1280]{1,0:T(8,128)(2,1)S(1)}, bf16[64,1280]{1,0:T(8,128)(2,1)S(1)}, u32[]{:S(2)}, u32[]{:S(2)}) collective-permute-start(bf16[64,1280]{1,0:T(8,128)(2,1)S(1)} %add_convert_fusion.7), channel_id=1, source_target_pairs={{0,4},{1,5},{2,6},{3,7},{4,0},{5,1},{6,2},{7,3},{8,12},{9,13},{10,... | collective-permute-start | bytes 491528 | tf_op jit(solution)/shard_map/ppermute | solution.py:466
  104.2 3.9 %collective-permute-done.13 = bf16[64,1280]{1,0:T(8,128)(2,1)S(1)} collective-permute-done((bf16[64,1280]{1,0:T(8,128)(2,1)S(1)}, bf16[64,1280]{1,0:T(8,128)(2,1)S(1)}, u32[]{:S(2)}, u32[]{:S(2)}) %collective-permute-start.13) | collective-permute-done | bytes 163872 | tf_op jit(solution)/shard_map/ppermute | solution.py:466
  108.1 1.5 %collective-permute-start.14 = (bf16[128,1280]{1,0:T(8,128)(2,1)S(1)}, bf16[128,1280]{1,0:T(8,128)(2,1)S(1)}, u32[]{:S(2)}, u32[]{:S(2)}) collective-permute-start(bf16[128,1280]{1,0:T(8,128)(2,1)S(1)} %maximum_select_fusion.3), channel_id=1, source_target_pairs={{0,2},{1,3},{2,0},{3,1},{4,6},{5,7},{6,4},{7,5},{8,10},{9,11},{10,... | collective-permute-start | bytes 983048 | tf_op jit(solution)/shard_map/ppermute | solution.py:466
  109.7 1.4 %collective-permute-start.19 = (bf16[128,512]{1,0:T(8,128)(2,1)S(1)}, bf16[128,512]{1,0:T(8,128)(2,1)S(1)}, u32[]{:S(2)}, u32[]{:S(2)}) collective-permute-start(bf16[128,512]{1,0:T(8,128)(2,1)S(1)} %add_convert_fusion.16), channel_id=1, source_target_pairs={{0,4},{1,5},{2,6},{3,7},{4,0},{5,1},{6,2},{7,3},{8,12},{9,13},{10,... | collective-permute-start | bytes 393224 | tf_op jit(solution)/shard_map/ppermute | solution.py:466
  111.9 3.3 %collective-permute-done.14 = bf16[128,1280]{1,0:T(8,128)(2,1)S(1)} collective-permute-done((bf16[128,1280]{1,0:T(8,128)(2,1)S(1)}, bf16[128,1280]{1,0:T(8,128)(2,1)S(1)}, u32[]{:S(2)}, u32[]{:S(2)}) %collective-permute-start.14) | collective-permute-done | bytes 327712 | tf_op jit(solution)/shard_map/ppermute | solution.py:466
  115.6 1.4 %add_convert_fusion = bf16[1024,512]{1,0:T(8,128)(2,1)} fusion(bf16[1024,512]{1,0:T(8,128)(2,1)S(1)} %collective-permute-done.3, bf16[1024,512]{1,0:T(8,128)(2,1)S(1)} %copy-done.3, bf16[1024,512]{1,0:T(8,128)(2,1)S(1)} %copy-done.2, f32[512]{0:T(512)S(1)} %convert_element_type.177), kind=kLoop, calls=%fused_computation | loop fusion | flops 3670016 | bytes 4196352 | tf_op jit(solution)/shard_map/convert_element_type | solution.py:671
  117.9 1.2 fusion.1
  119.0 5.3 %collective-permute-done.20 = bf16[256,512]{1,0:T(8,128)(2,1)S(1)} collective-permute-done((bf16[256,512]{1,0:T(8,128)(2,1)S(1)}, bf16[256,512]{1,0:T(8,128)(2,1)S(1)}, u32[]{:S(2)}, u32[]{:S(2)}) %collective-permute-start.20) | collective-permute-done | bytes 262176 | tf_op jit(solution)/shard_map/ppermute | solution.py:466
  124.3 1.2 fusion
  125.5 1.6 %unpack.1 = (f32[1,512]{1,0:T(1,128)}, f32[1,512]{1,0:T(1,128)}, f32[512,128]{1,0:T(8,128)S(1)}, f32[512,512]{1,0:T(8,128)}, f32[512,512]{1,0:T(8,128)}, /*index...) custom-call(s32[1]{0:T(128)} %bitcast.5.place, ...), custom_call_target="tpu_custom_call" | custom-call | flops 1000 | bytes 1000 | tf_op jit(solution)/shard_map/unpack/pallas_call | solution.py:453
  (81 shorter events, 8.4 us)
Async XLA Ops:
  3.6 28.2 %collective-permute-start = (bf16[1040,512]{1,0:T(8,128)(2,1)}, bf16[1040,512]{1,0:T(8,128)(2,1)S(1)}, u32[]{:S(2)}, u32[]{:S(2)}) collective-permute-start(bf16[1040,512]{1,0:T(8,128)(2,1)} %pad_maximum_fusion.refs_2_), channel_id=1, source_target_pairs={{0,2},{1,3},{2,0},{3,1},{4,6},{5,7},{6,4},{7,5},{8,10},{9,11},{10,... | collective-permute-start | bytes 3194888 | tf_op jit(solution)/shard_map/ppermute | solution.py:466
  17.9 7.2 %collective-permute-start.2 = (bf16[1024,512]{1,0:T(8,128)(2,1)}, bf16[1024,512]{1,0:T(8,128)(2,1)S(1)}, u32[]{:S(2)}, u32[]{:S(2)}) collective-permute-start(bf16[1024,512]{1,0:T(8,128)(2,1)} %get-tuple-element.64.refs_1_.glow), channel_id=1, source_target_pairs={{0,1},{1,0},{2,3},{3,2},{4,5},{5,4},{6,7},{7,6},{8,9},{9,8},{10,11... | collective-permute-start | bytes 3145736 | tf_op jit(solution)/shard_map/ppermute | solution.py:466
  18.0 7.1 %collective-permute-start.1 = (bf16[1024,512]{1,0:T(8,128)(2,1)}, bf16[1024,512]{1,0:T(8,128)(2,1)S(1)}, u32[]{:S(2)}, u32[]{:S(2)}) collective-permute-start(bf16[1024,512]{1,0:T(8,128)(2,1)} %get-tuple-element.63.refs_0_), channel_id=1, source_target_pairs={{0,1},{1,0},{2,3},{3,2},{4,5},{5,4},{6,7},{7,6},{8,9},{9,8},{10,11... | collective-permute-start | bytes 3145736 | tf_op jit(solution)/shard_map/ppermute | solution.py:466
  36.6 10.2 %collective-permute-start.4 = (bf16[1024,512]{1,0:T(8,128)(2,1)S(1)}, bf16[1024,512]{1,0:T(8,128)(2,1)S(1)}, u32[]{:S(2)}, u32[]{:S(2)}) collective-permute-start(bf16[1024,512]{1,0:T(8,128)(2,1)S(1)} %get-tuple-element.78), channel_id=1, source_target_pairs={{0,1},{1,0},{2,3},{3,2},{4,5},{5,4},{6,7},{7,6},{8,9},{9,8},{10,11... | collective-permute-start | bytes 3145736 | tf_op jit(solution)/shard_map/ppermute | solution.py:466
  44.5 17.0 %collective-permute-start.6 = (bf16[512,512]{1,0:T(8,128)(2,1)}, bf16[512,512]{1,0:T(8,128)(2,1)S(1)}, u32[]{:S(2)}, u32[]{:S(2)}) collective-permute-start(bf16[512,512]{1,0:T(8,128)(2,1)} %get-tuple-element.90), channel_id=1, source_target_pairs={{0,2},{1,3},{2,0},{3,1},{4,6},{5,7},{6,4},{7,5},{8,10},{9,11},{10,... | collective-permute-start | bytes 1572872 | tf_op jit(solution)/shard_map/ppermute | solution.py:466
  44.7 16.8 %collective-permute-start.5 = (bf16[256,512]{1,0:T(8,128)(2,1)S(1)}, bf16[256,512]{1,0:T(8,128)(2,1)S(1)}, u32[]{:S(2)}, u32[]{:S(2)}) collective-permute-start(bf16[256,512]{1,0:T(8,128)(2,1)S(1)} %copy-done.13), channel_id=1, source_target_pairs={{0,8},{1,9},{2,10},{3,11},{4,12},{5,13},{6,14},{7,15},{8,0},{9,1},... | collective-permute-start | bytes 786440 | tf_op jit(solution)/shard_map/ppermute | solution.py:466
  46.6 14.9 %collective-permute-start.7 = (bf16[256,512]{1,0:T(8,128)(2,1)}, bf16[256,512]{1,0:T(8,128)(2,1)S(1)}, u32[]{:S(2)}, u32[]{:S(2)}) collective-permute-start(bf16[256,512]{1,0:T(8,128)(2,1)} %get-tuple-element.92), channel_id=1, source_target_pairs={{0,8},{1,9},{2,10},{3,11},{4,12},{5,13},{6,14},{7,15},{8,0},{9,1},... | collective-permute-start | bytes 786440 | tf_op jit(solution)/shard_map/ppermute | solution.py:466
  46.7 15.8 %copy-start.12 = (bf16[512]{0:T(512)(128)(2,1)S(1)}, bf16[512]{0:T(512)(128)(2,1)}, u32[]{:S(2)}) copy-start(bf16[512]{0:T(512)(128)(2,1)} %param.33) | copy-start | bytes 3076
  46.7 15.8 %copy-start.1 = (bf16[1024,512]{1,0:T(8,128)(2,1)S(1)}, bf16[1024,512]{1,0:T(8,128)(2,1)}, u32[]{:S(2)}) copy-start(bf16[1024,512]{1,0:T(8,128)(2,1)} %copy-done) | copy-start | bytes 3145732
  46.7 16.3 %copy-start.4 = (bf16[512,512]{1,0:T(8,128)(2,1)S(1)}, bf16[512,512]{1,0:T(8,128)(2,1)}, u32[]{:S(2)}) copy-start(bf16[512,512]{1,0:T(8,128)(2,1)} %get-tuple-element.107) | copy-start | bytes 1572868
  62.4 3.7 %collective-permute-start.8 = (bf16[256,1280]{1,0:T(8,128)(2,1)S(1)}, bf16[256,1280]{1,0:T(8,128)(2,1)S(1)}, u32[]{:S(2)}, u32[]{:S(2)}) collective-permute-start(bf16[256,1280]{1,0:T(8,128)(2,1)S(1)} %get-tuple-element.93), channel_id=1, source_target_pairs={{0,1},{1,0},{2,3},{3,2},{4,5},{5,4},{6,7},{7,6},{8,9},{9,8},{10,11... | collective-permute-start | bytes 1966088 | tf_op jit(solution)/shard_map/ppermute | solution.py:466
  62.6 53.0 %collective-permute-start.3 = (bf16[1024,512]{1,0:T(8,128)(2,1)S(1)}, bf16[1024,512]{1,0:T(8,128)(2,1)S(1)}, u32[]{:S(2)}, u32[]{:S(2)}) collective-permute-start(bf16[1024,512]{1,0:T(8,128)(2,1)S(1)} %copy-done.1), channel_id=1, source_target_pairs={{0,1},{1,0},{2,3},{3,2},{4,5},{5,4},{6,7},{7,6},{8,9},{9,8},{10,11... | collective-permute-start | bytes 3145736 | tf_op jit(solution)/shard_map/ppermute | solution.py:466
  64.3 8.5 %collective-permute-start.21 = (bf16[256,512]{1,0:T(8,128)(2,1)S(1)}, bf16[256,512]{1,0:T(8,128)(2,1)S(1)}, u32[]{:S(2)}, u32[]{:S(2)}) collective-permute-start(bf16[256,512]{1,0:T(8,128)(2,1)S(1)} %constant_dynamic-slice_fusion), channel_id=1, source_target_pairs={{0,4},{1,5},{2,6},{3,7},{4,0},{5,1},{6,2},{7,3},{8,12},{9,13},{10,... | collective-permute-start | bytes 786440 | tf_op jit(solution)/shard_map/ppermute | solution.py:466
  66.2 15.3 %copy-start.9 = (bf16[256,512]{1,0:T(8,128)(2,1)S(1)}, bf16[256,512]{1,0:T(8,128)(2,1)}, u32[]{:S(2)}) copy-start(bf16[256,512]{1,0:T(8,128)(2,1)} %get-tuple-element.102) | copy-start | bytes 786436
  66.2 15.3 %copy-start.11 = (bf16[256,512]{1,0:T(8,128)(2,1)S(1)}, bf16[256,512]{1,0:T(8,128)(2,1)}, u32[]{:S(2)}) copy-start(bf16[256,512]{1,0:T(8,128)(2,1)} %copy-done.10) | copy-start | bytes 786436
  66.3 10.7 %collective-permute-start.9 = (bf16[128,1280]{1,0:T(8,128)(2,1)S(1)}, bf16[128,1280]{1,0:T(8,128)(2,1)S(1)}, u32[]{:S(2)}, u32[]{:S(2)}) collective-permute-start(bf16[128,1280]{1,0:T(8,128)(2,1)S(1)} %get-tuple-element.125), channel_id=1, source_target_pairs={{0,2},{1,3},{2,0},{3,1},{4,6},{5,7},{6,4},{7,5},{8,10},{9,11},{10,... | collective-permute-start | bytes 983048 | tf_op jit(solution)/shard_map/ppermute | solution.py:466
  68.0 13.5 %collective-permute-start.16 = (bf16[256,512]{1,0:T(8,128)(2,1)S(1)}, bf16[256,512]{1,0:T(8,128)(2,1)S(1)}, u32[]{:S(2)}, u32[]{:S(2)}) collective-permute-start(bf16[256,512]{1,0:T(8,128)(2,1)S(1)} %add_convert_fusion.5), channel_id=1, source_target_pairs={{0,2},{1,3},{2,0},{3,1},{4,6},{5,7},{6,4},{7,5},{8,10},{9,11},{10,... | collective-permute-start | bytes 786440 | tf_op jit(solution)/shard_map/ppermute | solution.py:466
  72.8 11.3 %collective-permute-start.22 = (bf16[128,512]{1,0:T(8,128)(2,1)S(1)}, bf16[128,512]{1,0:T(8,128)(2,1)S(1)}, u32[]{:S(2)}, u32[]{:S(2)}) collective-permute-start(bf16[128,512]{1,0:T(8,128)(2,1)S(1)} %add_convert_fusion.14), channel_id=1, source_target_pairs={{0,8},{1,9},{2,10},{3,11},{4,12},{5,13},{6,14},{7,15},{8,0},{9,1},... | collective-permute-start | bytes 393224 | tf_op jit(solution)/shard_map/ppermute | solution.py:466
  77.0 5.4 %collective-permute-start.10 = (bf16[64,1280]{1,0:T(8,128)(2,1)S(1)}, bf16[64,1280]{1,0:T(8,128)(2,1)S(1)}, u32[]{:S(2)}, u32[]{:S(2)}) collective-permute-start(bf16[64,1280]{1,0:T(8,128)(2,1)S(1)} %add_convert_fusion.10), channel_id=1, source_target_pairs={{0,4},{1,5},{2,6},{3,7},{4,0},{5,1},{6,2},{7,3},{8,12},{9,13},{10,... | collective-permute-start | bytes 491528 | tf_op jit(solution)/shard_map/ppermute | solution.py:466
  81.6 9.7 %collective-permute-start.17 = (bf16[128,512]{1,0:T(8,128)(2,1)S(1)}, bf16[128,512]{1,0:T(8,128)(2,1)S(1)}, u32[]{:S(2)}, u32[]{:S(2)}) collective-permute-start(bf16[128,512]{1,0:T(8,128)(2,1)S(1)} %constant_dynamic-slice_fusion.1), channel_id=1, source_target_pairs={{0,4},{1,5},{2,6},{3,7},{4,0},{5,1},{6,2},{7,3},{8,12},{9,13},{10,... | collective-permute-start | bytes 393224 | tf_op jit(solution)/shard_map/ppermute | solution.py:466
  82.5 7.0 %collective-permute-start.11 = (bf16[64,1280]{1,0:T(8,128)(2,1)S(1)}, bf16[64,1280]{1,0:T(8,128)(2,1)S(1)}, u32[]{:S(2)}, u32[]{:S(2)}) collective-permute-start(bf16[64,1280]{1,0:T(8,128)(2,1)S(1)} %add_convert_fusion.9), channel_id=1, source_target_pairs={{0,8},{1,9},{2,10},{3,11},{4,12},{5,13},{6,14},{7,15},{8,0},{9,1},... | collective-permute-start | bytes 491528 | tf_op jit(solution)/shard_map/ppermute | solution.py:466
  84.2 19.8 %collective-permute-start.23 = (bf16[128,512]{1,0:T(8,128)(2,1)S(1)}, bf16[128,512]{1,0:T(8,128)(2,1)S(1)}, u32[]{:S(2)}, u32[]{:S(2)}) collective-permute-start(bf16[128,512]{1,0:T(8,128)(2,1)S(1)} %add_convert_fusion.13), channel_id=1, source_target_pairs={{0,16},{1,17},{2,18},{3,19},{4,20},{5,21},{6,22},{7,23},{8,24},{9,... | collective-permute-start | bytes 393224 | tf_op jit(solution)/shard_map/ppermute | solution.py:466
  89.5 13.1 %collective-permute-start.12 = (bf16[64,1280]{1,0:T(8,128)(2,1)S(1)}, bf16[64,1280]{1,0:T(8,128)(2,1)S(1)}, u32[]{:S(2)}, u32[]{:S(2)}) collective-permute-start(bf16[64,1280]{1,0:T(8,128)(2,1)S(1)} %add_convert_fusion.8), channel_id=1, source_target_pairs={{0,16},{1,17},{2,18},{3,19},{4,20},{5,21},{6,22},{7,23},{8,24},{9,... | collective-permute-start | bytes 491528 | tf_op jit(solution)/shard_map/ppermute | solution.py:466
  91.3 18.4 %collective-permute-start.18 = (bf16[128,512]{1,0:T(8,128)(2,1)S(1)}, bf16[128,512]{1,0:T(8,128)(2,1)S(1)}, u32[]{:S(2)}, u32[]{:S(2)}) collective-permute-start(bf16[128,512]{1,0:T(8,128)(2,1)S(1)} %add_convert_fusion.17), channel_id=1, source_target_pairs={{0,16},{1,17},{2,18},{3,19},{4,20},{5,21},{6,22},{7,23},{8,24},{9,... | collective-permute-start | bytes 393224 | tf_op jit(solution)/shard_map/ppermute | solution.py:466
  102.7 5.4 %collective-permute-start.13 = (bf16[64,1280]{1,0:T(8,128)(2,1)S(1)}, bf16[64,1280]{1,0:T(8,128)(2,1)S(1)}, u32[]{:S(2)}, u32[]{:S(2)}) collective-permute-start(bf16[64,1280]{1,0:T(8,128)(2,1)S(1)} %add_convert_fusion.7), channel_id=1, source_target_pairs={{0,4},{1,5},{2,6},{3,7},{4,0},{5,1},{6,2},{7,3},{8,12},{9,13},{10,... | collective-permute-start | bytes 491528 | tf_op jit(solution)/shard_map/ppermute | solution.py:466
  104.0 11.6 %copy-start.2 = (bf16[1024,512]{1,0:T(8,128)(2,1)S(1)}, bf16[1024,512]{1,0:T(8,128)(2,1)}, u32[]{:S(2)}) copy-start(bf16[1024,512]{1,0:T(8,128)(2,1)} %get-tuple-element.62.res) | copy-start | bytes 3145732
  104.1 7.0 %collective-permute-start.24 = (bf16[128,512]{1,0:T(8,128)(2,1)S(1)}, bf16[128,512]{1,0:T(8,128)(2,1)S(1)}, u32[]{:S(2)}, u32[]{:S(2)}) collective-permute-start(bf16[128,512]{1,0:T(8,128)(2,1)S(1)} %add_convert_fusion.12), channel_id=1, source_target_pairs={{0,8},{1,9},{2,10},{3,11},{4,12},{5,13},{6,14},{7,15},{8,0},{9,1},... | collective-permute-start | bytes 393224 | tf_op jit(solution)/shard_map/ppermute | solution.py:466
  108.1 7.1 %collective-permute-start.14 = (bf16[128,1280]{1,0:T(8,128)(2,1)S(1)}, bf16[128,1280]{1,0:T(8,128)(2,1)S(1)}, u32[]{:S(2)}, u32[]{:S(2)}) collective-permute-start(bf16[128,1280]{1,0:T(8,128)(2,1)S(1)} %maximum_select_fusion.3), channel_id=1, source_target_pairs={{0,2},{1,3},{2,0},{3,1},{4,6},{5,7},{6,4},{7,5},{8,10},{9,11},{10,... | collective-permute-start | bytes 983048 | tf_op jit(solution)/shard_map/ppermute | solution.py:466
  109.7 5.8 %collective-permute-start.19 = (bf16[128,512]{1,0:T(8,128)(2,1)S(1)}, bf16[128,512]{1,0:T(8,128)(2,1)S(1)}, u32[]{:S(2)}, u32[]{:S(2)}) collective-permute-start(bf16[128,512]{1,0:T(8,128)(2,1)S(1)} %add_convert_fusion.16), channel_id=1, source_target_pairs={{0,4},{1,5},{2,6},{3,7},{4,0},{5,1},{6,2},{7,3},{8,12},{9,13},{10,... | collective-permute-start | bytes 393224 | tf_op jit(solution)/shard_map/ppermute | solution.py:466
  111.1 6.8 %collective-permute-start.25 = (bf16[256,512]{1,0:T(8,128)(2,1)S(1)}, bf16[256,512]{1,0:T(8,128)(2,1)S(1)}, u32[]{:S(2)}, u32[]{:S(2)}) collective-permute-start(bf16[256,512]{1,0:T(8,128)(2,1)S(1)} %maximum_select_fusion.5), channel_id=1, source_target_pairs={{0,4},{1,5},{2,6},{3,7},{4,0},{5,1},{6,2},{7,3},{8,12},{9,13},{10,... | collective-permute-start | bytes 786440 | tf_op jit(solution)/shard_map/ppermute | solution.py:466
  115.4 10.1 %collective-permute-start.15 = (bf16[256,1280]{1,0:T(8,128)(2,1)S(1)}, bf16[256,1280]{1,0:T(8,128)(2,1)S(1)}, u32[]{:S(2)}, u32[]{:S(2)}) collective-permute-start(bf16[256,1280]{1,0:T(8,128)(2,1)S(1)} %maximum_select_fusion.mine), channel_id=1, source_target_pairs={{0,1},{1,0},{2,3},{3,2},{4,5},{5,4},{6,7},{7,6},{8,9},{9,8},{10,11... | collective-permute-start | bytes 1966088 | tf_op jit(solution)/shard_map/ppermute | solution.py:466
  115.5 8.8 %collective-permute-start.20 = (bf16[256,512]{1,0:T(8,128)(2,1)S(1)}, bf16[256,512]{1,0:T(8,128)(2,1)S(1)}, u32[]{:S(2)}, u32[]{:S(2)}) collective-permute-start(bf16[256,512]{1,0:T(8,128)(2,1)S(1)} %maximum_select_fusion.4), channel_id=1, source_target_pairs={{0,8},{1,9},{2,10},{3,11},{4,12},{5,13},{6,14},{7,15},{8,0},{9,1},... | collective-permute-start | bytes 786440 | tf_op jit(solution)/shard_map/ppermute | solution.py:466
  (8 other events, 37.6 us)

commit v3 on v2

--- a/solution.py
+++ b/solution.py
@@ -198,17 +198,14 @@
 def ffn_kernel(*refs, units, more):
     low2, glow, weights = refs[:3]
     at = 3
-    if "cut" in more:
-        mine = refs[at]
-        at += 1
     if "rows" in more:
         out_in, second_in = refs[at : at + 2]
         at += 2
     if "weights" in more:
         contract_in, expand_in, bias_in = refs[at : at + 3]
         at += 3
-    if "cut" in more:
-        out, second, contract_out, keep_out, send_out, bias_out, hidden, grad, uncut = refs[at:]
+    if "final" in more:
+        out, second, contract_out, folded_out, bias_out, hidden, grad = refs[at:]
     else:
         out, second, contract_out, expand_out, bias_out, hidden, grad = refs[at:]
     rows = low2.shape[0]
@@ -237,29 +234,27 @@
     contract_sum = dot_tn(hidden[...], glow[...])
     expand_sum = dot_tn(low2[...], grad[...])
     if "weights" in more:
-        contract_sum += contract_in[...]
-        expand_sum += expand_in[...]
-    contract_out[...] = contract_sum.astype(contract_out.dtype)
+        contract_sum += contract_in[...].astype(F32)
+        expand_sum += expand_in[...].astype(F32)
     bias_out[...] = bias_sum
-    if "cut" in more:
-        half = uncut.shape[0] // 2
-        uncut[...] = expand_sum.astype(uncut.dtype)
-        keep_out[...] = uncut[pl.ds(pl.multiple_of(mine[0] * half, half), half), :]
-        send_out[...] = uncut[pl.ds(pl.multiple_of((1 - mine[0]) * half, half), half), :]
+    if "final" in more:
+        contract_out[...] = contract_sum.astype(contract_out.dtype)
+        for at in range(0, expand_sum.shape[0], units):
+            block = expand_sum[at : at + units, :]
+            folded_out[:, at : at + units] = block.astype(folded_out.dtype)
     else:
+        contract_out[...] = contract_sum.astype(contract_out.dtype)
         expand_out[...] = expand_sum.astype(expand_out.dtype)
 
 
 def ffn(rows_far, low2, glow, weights, weights_far, units, rows_in=None, weights_in=None,
-        rows_out=("far", "far"), cut=None, carry="near"):
+        rows_out=("far", "far"), final=False, carry="far"):
     rows, width = low2.shape
     more = []
     operands = [low2, glow, weights]
     spaces = [rows_far, rows_far, weights_far]
-    if cut is not None:
-        more.append("cut")
-        operands.append(cut)
-        spaces.append("scalar")
+    if final:
+        more.append("final")
     if rows_in is not None:
         more.append("rows")
         operands += rows_in
@@ -269,16 +264,13 @@
         operands += weights_in
         spaces += [carry, carry, "near"]
     scratch = [pltpu.VMEM((rows, units), BF16), pltpu.VMEM((rows, units), BF16)]
-    if cut is None:
+    if final:
+        sums = [jax.ShapeDtypeStruct((units, width), BF16)] * 2
+    else:
         sums = [
-            jax.ShapeDtypeStruct((units, width), F32), jax.ShapeDtypeStruct((width, units), F32)
+            jax.ShapeDtypeStruct((units, width), BF16), jax.ShapeDtypeStruct((width, units), BF16)
         ]
-        sums_out = [carry, carry]
-    else:
-        sums = [jax.ShapeDtypeStruct((units, width), BF16)]
-        sums += [jax.ShapeDtypeStruct((width // 2, units), BF16)] * 2
-        sums_out = ["far", "far", "far"]
-        scratch.append(pltpu.VMEM((width, units), BF16))
+    sums_out = [carry] * len(sums)
     outs = placed_call(
         functools.partial(ffn_kernel, units=units, more=tuple(more)),
         "ffn",
@@ -404,15 +396,20 @@
     send[...] = packed[pl.ds(pl.multiple_of((1 - mine) * half, half), half), :]
 
 
-def unpack_kernel(place, mine, other, gain1, shift1, router, query, output, keyval, gain2, shift2, unit, bias):
+def unpack_kernel(
+    place, mine, other,
+    gain1, shift1, router, query, output, keyval, gain2, shift2, unit, bias,
+    rest,
+):
     half, width = mine.shape[0], query.shape[1]
     for end, values in ((place[0] % 2, mine), (1 - place[0] % 2, other)):
         span = pl.ds(pl.multiple_of(end * half, half), half)
         query[span, :] = values[:, :width].astype(F32)
         output[span, :] = values[:, width : 2 * width].astype(F32)
         keyval[span, :] = values[:, 2 * width : 2 * width + LANES].astype(F32)
-        router[span, :] = values[:, 2 * width + LANES :].astype(F32)
-    rows = jnp.transpose(router[...])
+        rest[span, :] = values[:, 2 * width + LANES :].astype(F32)
+    rows = jnp.transpose(rest[...])
+    router[...] = rows[: router.shape[0], :]
     for at, target in enumerate((gain1, shift1, gain2, shift2, bias)):
         target[...] = rows[VECTOR_ROW + at : VECTOR_ROW + at + 1, :]
     owner = lax.broadcasted_iota(jnp.int32, rows.shape, 0) - (VECTOR_ROW + 5)
@@ -477,35 +474,65 @@
     return (left.astype(F32) + right.astype(F32)).astype(BF16)
 
 
-def scatter_sum(values, bits, place, devices, cut=None):
-    if not bits:
-        return values
-    mines = [(place // bit) % 2 for bit in bits]
-    keep, send = halves(values, mines[0]) if cut is None else cut
-    for at, bit in enumerate(bits):
-        got = swap(send, bit, devices)
-        if at + 1 < len(bits):
+class Chain:
+    def __init__(self, steps, place, devices):
+        self.steps = list(steps)
+        self.place, self.devices = place, devices
+        self.values = self.keep = self.outgoing = None
+
+    def mine(self, at):
+        return (self.place // self.steps[at][1]) % 2
+
+    def feed(self, values):
+        self.values = values
+        if self.steps and self.steps[0][0] == "cut":
+            self.keep, self.outgoing = halves(values, self.mine(0))
+        else:
+            self.outgoing = values
+        return self
+
+    def feed_halves(self, keep, send):
+        self.keep, self.outgoing = keep, send
+        return self
+
+    def send(self):
+        return swap(self.outgoing, self.steps[0][1], self.devices)
+
+    def take(self, got):
+        kind = self.steps[0][0]
+        if kind == "cut" and len(self.steps) > 1 and self.steps[1][0] == "cut":
             (keep, send), (keep_got, send_got) = (
-                halves(item, mines[at + 1]) for item in (keep, got)
+                halves(item, self.mine(1)) for item in (self.keep, got)
             )
-            send = add_low(send, send_got)
-            keep = add_low(keep, keep_got)
+            self.outgoing = add_low(send, send_got)
+            self.keep = add_low(keep, keep_got)
         else:
-            values = add_low(keep, got)
-    return values
-
-
-def all_sum(values, bits, place, devices, whole=1):
+            if kind == "cut":
+                values = add_low(self.keep, got)
+            elif kind == "full":
+                values = add_low(self.values, got)
+            else:
+                values = joined(self.values, got, self.mine(0))
+            self.values = self.outgoing = values
+        self.steps.pop(0)
+
+    def run(self, steps):
+        for _ in range(min(steps, len(self.steps))):
+            self.take(self.send())
+        return self.values
+
+
+def plan(bits, whole=1):
     cut, full = bits[: len(bits) - whole], bits[len(bits) - whole :]
-    values = scatter_sum(values, cut, place, devices)
-    values = whole_sum(values, full, devices)
-    return gather(values, cut, place, devices)
-
-
-def whole_sum(values, bits, devices):
-    for bit in bits:
-        values = add_low(values, swap(values, bit, devices))
-    return values
+    return (
+        [("cut", bit) for bit in cut]
+        + [("full", bit) for bit in full]
+        + [("join", bit) for bit in reversed(cut)]
+    )
+
+
+def sum_low(parts):
+    return functools.reduce(jnp.add, [part.astype(F32) for part in parts]).astype(BF16)
 
 
 def joined(values, got, mine):
@@ -514,12 +541,6 @@
         jnp.concatenate([values, got], axis=0),
         jnp.concatenate([got, values], axis=0),
     )
-
-
-def gather(values, bits, place, devices):
-    for bit in reversed(bits):
-        values = joined(values, swap(values, bit, devices), (place // bit) % 2)
-    return values
 
 
 def shards(
@@ -557,7 +578,7 @@
     def shape(*dims, dtype=BF16):
         return jax.ShapeDtypeStruct(dims, dtype)
 
-    bias_rows = jnp.broadcast_to(jnp.pad(expand_bias, (0, width - units))[None], (16, width))
+    bias_rows = jnp.pad(expand_bias[None], ((0, 15), (0, width - units)))
     wide_expand = jnp.pad(expand_weight, ((0, 0), (0, width - units)))
     own = jnp.concatenate([contract_weight, bias_rows, wide_expand], axis=0)
     turned_router = router.T
@@ -588,15 +609,12 @@
     glow_pair = swap(glow, 1, devices)
     dp_bits = [n_mp << at for at in range(n_dp.bit_length() - 1)]
     mp_bits = [1 << at for at in range(n_mp.bit_length() - 1)]
-    first_bit = dp_bits[min(1, len(dp_bits) - 1)]
-    later_bits = [bit for bit in dp_bits if bit != first_bit]
-    first_mine = jnp.full((1,), (place // first_bit) % 2, jnp.int32)
-    rows_own, grads_own = ffn("far", low2, glow, own, "far", units, carry="far")
+    rows_own, grads_own = ffn("far", low2, glow, own, "far", units)
     rows_pair, grads_own = ffn(
         None, low2_pair, glow_pair, own, "far", units, weights_in=grads_own, rows_out=(None, None),
-        cut=first_mine, carry="far",
-    )
-    contract_sum, expand_keep, expand_send, unit_own = grads_own
+        final=True,
+    )
+    contract_sum, expand_sum, unit_own = grads_own
     unit_peers = []
     waiting = []
     for step in range(1, chips):
@@ -610,7 +628,6 @@
             units,
             rows_in=rows_pair,
             rows_out=(None, None),
-            carry="far",
         )
         if final:
             out_got, second_got = (swap(item, 1, devices) for item in rows_pair)
@@ -624,14 +641,10 @@
             rows_in=rows_own,
             weights_in=grads,
             rows_out=("far", "near" if final else "far"),
-            cut=first_mine,
-            carry="far",
+            final=True,
         )
-        contract_part, keep, send, unit_part = grads
-        unit_peers.append(unit_part)
-        contract_got = swap(contract_part, 2 * step, devices)
-        waiting.append((contract_got, keep, swap(send, first_bit, devices)))
-    expand_got = swap(expand_send, first_bit, devices)
+        unit_peers.append(grads[2])
+        waiting.append([swap(item, 2 * step, devices) for item in grads[:2]])
     scalars = jnp.full((1,), mp_place, jnp.int32)
     tok_grad, keep, send = placed_call(
         back_kernel,
@@ -656,47 +669,60 @@
             pltpu.VMEM((LANES, width), F32),
         ],
     )
-    send, expand_got, waiting = lax.optimization_barrier((send, expand_got, waiting))
-    expand_sum = add_low(expand_keep, expand_got)
-    for step in range(1, chips):
-        contract_got, peer_keep, peer_got = waiting[step - 1]
-        contract_sum = add_low(contract_sum, contract_got)
-        expand_part = add_low(peer_keep, peer_got)
-        expand_sum = add_low(expand_sum, swap(expand_part, 2 * step, devices))
-    order = mp_bits + dp_bits
-    cut, full = order[:-2], order[-2:]
-    packed = scatter_sum(None, cut, place, devices, (keep, send))
+    order = mp_bits[:1] + dp_bits[:1] + mp_bits[1:] + dp_bits[1:]
+    contract_got = [item[0] for item in waiting]
+    expand_got = [item[1] for item in waiting]
+    send, contract_got = lax.optimization_barrier((send, contract_got))
+    first = Chain(plan(dp_bits[1:2] + dp_bits[:1] + dp_bits[2:]), place, devices)
+    first.feed(sum_low([contract_sum, *contract_got]))
+    second = Chain(plan(dp_bits), place, devices)
+    chain = Chain(plan(order, 2)[:-1], place, devices).feed_halves(keep, send)
+    for at in range(len(chain.steps)):
+        got = chain.send()
+        if at == 1:
+            got, expand_got = lax.optimization_barrier((got, expand_got))
+            second.feed(sum_low([expand_sum, *expand_got]))
+        chain.take(got)
+    packed = chain.values
     layer = (
         res.astype(F32) + rows_own[0].astype(F32) + out_got.astype(F32) + contract_bias.astype(F32)
     ).astype(BF16)
-    contract_grad = all_sum(contract_sum, dp_bits, place, devices).astype(F32)
-    expand_sum = all_sum(expand_sum, later_bits, place, devices)
-    expand_grad = gather(expand_sum, [first_bit], place, devices).astype(F32)
-    packed = gather(whole_sum(packed, full, devices), cut[1:], place, devices)
+    contract_sum = first.run(len(first.steps))
+    contract_grad = contract_sum.astype(F32)
     other = swap(packed, mp_bits[0], devices)
     square = shape(width, width, dtype=F32)
     line = shape(1, width, dtype=F32)
-    (
-        gain1_grad, shift1_grad, router_grad, query_grad, output_grad, keyval_grad, gain2_grad,
-        shift2_grad, unit_grad, bias_grad,
-    ) = placed_call(
+    unpacked = placed_call(
         unpack_kernel,
         "unpack",
         [scalars, packed, other],
         ["scalar", None, None],
         [
-            line, line, shape(width, LANES, dtype=F32), square, square,
+            line, line, shape(router.shape[1], width, dtype=F32), square, square,
             shape(width, LANES, dtype=F32), line, line, shape(1, units, dtype=F32), line,
         ],
         [None] * 10,
-        [],
-    )
+        [pltpu.VMEM((width, LANES), F32)],
+    )
+    second.run(len(second.steps) - 1)
+    got, unpacked, contract_grad, layer = lax.optimization_barrier(
+        (second.send(), unpacked, contract_grad, layer)
+    )
+    second.take(got)
+    expand_sum = second.values
+    expand_grad = jnp.concatenate(
+        [expand_sum[:, at : at + units] for at in range(0, width, units)], axis=0
+    ).astype(F32)
+    (
+        gain1_grad, shift1_grad, router_grad, query_grad, output_grad, keyval_grad, gain2_grad,
+        shift2_grad, unit_grad, bias_grad,
+    ) = unpacked
     return (
         layer,
         tok_grad,
         gain1_grad[0],
         shift1_grad[0],
-        router_grad[:, : router.shape[1]],
+        router_grad.T,
         query_grad,
         output_grad,
         keyval_grad,

time: 128 us -> 123 us (0.961)
  waiting for transfers between devices: 36.9 us -> 32.9 us
  local copies, waits for them, and re-layouts: 2.4 us -> 0.77 us
    ppermute x26 -> x25, waiting for transfers between devices: 36.9 us -> 32.9 us  [swap(): return lax.ppermute(values, AXES, [(at, at ^ bit) for at in range(devices)])]
    convert_element_type x2 -> x4, other arithmetic: 2.36 us -> 4.77 us  [the longest x2 2.41 us: sum_low(): functools.reduce(jnp.add, [part.astype(F32) for part in parts]).astype(BF16)]
    unnamed x29 -> x16, local copies, waits for them, and re-layouts: 1.67 us -> 0.04 us
    ppermute x26 -> x25, starting transfers between devices: 25.6 us -> 26.5 us  [swap(): return lax.ppermute(values, AXES, [(at, at ^ bit) for at in range(devices)])]
  transfers between devices with their start and end apart: 26 -> 25, of which waited for: 10 -> 11; matrix products, arithmetic and copies ran while one was open for 5% -> 6% of each run, Pallas kernels for 37% -> 39%
where the time goes in v3:
time: 123 us
  Pallas kernels  52.4 us (43%)
  waiting for transfers between devices  32.9 us (27%)
  starting transfers between devices  26.5 us (22%)
  other arithmetic  9.35 us (8%)
    pallas_call x6, Pallas kernels, placed_call(): pl.pallas_call(kernel, out_shape=results, in_specs=[pl.BlockSpec(memory_s...  41 us
    ppermute x25, waiting for transfers between devices, swap(): return lax.ppermute(values, AXES, [(at, at ^ bit) for at in range(devices)])  32.9 us
    ppermute x25, starting transfers between devices, swap(): return lax.ppermute(values, AXES, [(at, at ^ bit) for at in range(devices)])  26.5 us
    pallas_call x1, Pallas kernels, far_call(): pl.pallas_call(kernel, out_shape=[pltpu.HBM(item.shape, item.dtype) for i...  11.4 us
  transfers between devices with their start and end apart: 25, of which 11 were waited for; matrix products, arithmetic and copies ran while one was open for 6% of the time, Pallas kernels for 39%

profile of v3, /device:TPU:0, one launch (start us, length us, event | category | flops | bytes accessed | tf_op | source)
XLA Modules:
  0.0 122.9 jit_solution(5337393890877365249)
XLA Ops:
  1.3 1.3 %fusion.3.refs_2_ = bf16[1040,512]{1,0:T(8,128)(2,1)S(1)} fusion(bf16[1,512]{1,0:T(2,128)(2,1)S(1)} %broadcast_in_dim.7, bf16[512,512]{1,0:T(8,128)(2,1)} %param.30, bf16[512,512]{1,0:T(8,128)(2,1)} %param.32), kind=kLoop, calls=%fused_computation.6 | loop fusion | flops 5324800 | bytes 2114560 | tf_op jit(solution)/shard_map/concatenate | solution.py:583
  2.6 3.0 %collective-permute-start.2 = (bf16[1040,512]{1,0:T(8,128)(2,1)S(1)}, bf16[1040,512]{1,0:T(8,128)(2,1)S(1)}, u32[]{:S(2)}, u32[]{:S(2)}) collective-permute-start(bf16[1040,512]{1,0:T(8,128)(2,1)S(1)} %fusion.3.refs_2_), channel_id=1, source_target_pairs={{0,2},{1,3},{2,0},{3,1},{4,6},{5,7},{6,4},{7,5},{8,10},{9,11},{10,... | collective-permute-start | bytes 3194888 | tf_op jit(solution)/shard_map/ppermute | solution.py:463
  5.6 11.4 %attend.1 = (bf16[1024,512]{1,0:T(8,128)(2,1)}, bf16[1024,512]{1,0:T(8,128)(2,1)}, bf16[1024,512]{1,0:T(8,128)(2,1)}, bf16[1024,512]{1,0:T(8,128)(2,1)}, bf16[8,...) custom-call(s32[1,1024]{1,0:T(1,128)} %bitcast.15, ...), custom_call_target="tpu_custom_call" | custom-call | flops 1000 | bytes 1000 | tf_op jit(solution)/shard_map/attend/pallas_call | solution.py:423
  17.6 6.4 %ffn.4 = (bf16[1024,512]{1,0:T(8,128)(2,1)}, bf16[1024,512]{1,0:T(8,128)(2,1)}, bf16[512,512]{1,0:T(8,128)(2,1)}, bf16[512,512]{1,0:T(8,128)(2,1)}, f32[1,512]{1,0:T(1,128)S(1)}) custom-call(bf16[1024,512]{1,0:T(8,128)(2,1)} %get-tuple-element.72.refs_0_, bf16[1024,512]{1,0:T(8,128)(2,1)} %get-tuple-element.73.refs_1_.glow, bf16[1040,512]{1,0:T(8,128)(2,1)} %copy-done.2), custom_call_target="tpu_custom_call" | custom-call | flops 1000 | bytes 1000 | tf_op jit(solution)/shard_map/ffn/pallas_call | solution.py:450
  24.0 6.3 %ffn.5 = (bf16[1024,512]{1,0:T(8,128)(2,1)S(1)}, bf16[1024,512]{1,0:T(8,128)(2,1)S(1)}, bf16[512,512]{1,0:T(8,128)(2,1)}, bf16[512,512]{1,0:T(8,128)(2,1)}, f32[1,512]{1,0:T(1,128)S(1)}) custom-call(bf16[1024,512]{1,0:T(8,128)(2,1)S(1)} %collective-permute-done.refs_0_, bf16[1024,512]{1,0:T(8,128)(2,1)S(1)} %collective-permute-done.1.refs_1_, ...), custom_call_target="tpu_custom_call" | custom-call | flops 1000 | bytes 1000 | tf_op jit(solution)/shard_map/ffn/pallas_call | solution.py:450
  30.3 4.7 %ffn.6 = (bf16[1024,512]{1,0:T(8,128)(2,1)S(1)}, bf16[1024,512]{1,0:T(8,128)(2,1)}, bf16[512,512]{1,0:T(8,128)(2,1)}, bf16[512,512]{1,0:T(8,128)(2,1)}, f32[1,512]{1,0:T(1,128)S(1)}) custom-call(bf16[1024,512]{1,0:T(8,128)(2,1)S(1)} %collective-permute-done.refs_0_, bf16[1024,512]{1,0:T(8,128)(2,1)S(1)} %collective-permute-done.1.refs_1_, ...), custom_call_target="tpu_custom_call" | custom-call | flops 1000 | bytes 1000 | tf_op jit(solution)/shard_map/ffn/pallas_call | solution.py:450
  35.1 7.4 %ffn.7 = (bf16[1024,512]{1,0:T(8,128)(2,1)}, bf16[1024,512]{1,0:T(8,128)(2,1)S(1)}, bf16[512,512]{1,0:T(8,128)(2,1)}, bf16[512,512]{1,0:T(8,128)(2,1)}, f32[1,512]{1,0:T(1,128)S(1)}) custom-call(bf16[1024,512]{1,0:T(8,128)(2,1)} %get-tuple-element.72.refs_0_, bf16[1024,512]{1,0:T(8,128)(2,1)} %get-tuple-element.73.refs_1_.glow, ...), custom_call_target="tpu_custom_call" | custom-call | flops 1000 | bytes 1000 | tf_op jit(solution)/shard_map/ffn/pallas_call | solution.py:450
  43.0 14.6 %back.1 = (bf16[1024,512]{1,0:T(8,128)(2,1)}, bf16[256,1280]{1,0:T(8,128)(2,1)S(1)}, bf16[256,1280]{1,0:T(8,128)(2,1)S(1)}) custom-call(s32[1]{0:T(128)} %bitcast.4.place, bf16[1024,512]{1,0:T(8,128)(2,1)S(1)} %get-tuple-element.85.second_own, bf16[1024,512]{1,0:T(8,128)(2,1)S(1)} %collective-permute-done.3.second_got, ...), custom_call_target="tpu_custom_call" | custom-call | flops 1000 | bytes 1000 | tf_op jit(solution)/shard_map/back/pallas_call | solution.py:450
  57.8 1.6 %collective-permute-start.7 = (bf16[512,512]{1,0:T(8,128)(2,1)}, bf16[512,512]{1,0:T(8,128)(2,1)}, u32[]{:S(2)}, u32[]{:S(2)}) collective-permute-start(bf16[512,512]{1,0:T(8,128)(2,1)} %get-tuple-element.99), channel_id=1, source_target_pairs={{0,2},{1,3},{2,0},{3,1},{4,6},{5,7},{6,4},{7,5},{8,10},{9,11},{10,... | collective-permute-start | bytes 1572872 | tf_op jit(solution)/shard_map/ppermute | solution.py:463
  60.0 1.6 %collective-permute-start.6 = (bf16[128,1280]{1,0:T(8,128)(2,1)S(1)}, bf16[128,1280]{1,0:T(8,128)(2,1)S(1)}, u32[]{:S(2)}, u32[]{:S(2)}) collective-permute-start(bf16[128,1280]{1,0:T(8,128)(2,1)S(1)} %get-tuple-element.131), channel_id=1, source_target_pairs={{0,4},{1,5},{2,6},{3,7},{4,0},{5,1},{6,2},{7,3},{8,12},{9,13},{10,... | collective-permute-start | bytes 983048 | tf_op jit(solution)/shard_map/ppermute | solution.py:463
  61.6 1.2 %add_convert_fusion.1 = bf16[512,512]{1,0:T(8,128)(2,1)S(1)} fusion(bf16[512,512]{1,0:T(8,128)(2,1)} %collective-permute-done.4, bf16[512,512]{1,0:T(8,128)(2,1)S(1)} %copy-done.6), kind=kLoop, calls=%fused_computation.7 | loop fusion | flops 1048576 | bytes 1572864 | tf_op jit(solution)/shard_map/convert_element_type | solution.py:535
  62.9 1.6 %collective-permute-start.19 = (bf16[256,512]{1,0:T(8,128)(2,1)S(1)}, bf16[256,512]{1,0:T(8,128)(2,1)S(1)}, u32[]{:S(2)}, u32[]{:S(2)}) collective-permute-start(bf16[256,512]{1,0:T(8,128)(2,1)S(1)} %constant_dynamic-slice_fusion.1), channel_id=1, source_target_pairs={{0,8},{1,9},{2,10},{3,11},{4,12},{5,13},{6,14},{7,15},{8,0},{9,1},... | collective-permute-start | bytes 786440 | tf_op jit(solution)/shard_map/ppermute | solution.py:463
  64.5 7.9 %collective-permute-done.7 = bf16[512,512]{1,0:T(8,128)(2,1)} collective-permute-done((bf16[512,512]{1,0:T(8,128)(2,1)}, bf16[512,512]{1,0:T(8,128)(2,1)}, u32[]{:S(2)}, u32[]{:S(2)}) %collective-permute-start.7) | collective-permute-done | bytes 524320 | tf_op jit(solution)/shard_map/ppermute | solution.py:463
  72.4 1.6 %collective-permute-start.13 = (bf16[64,1280]{1,0:T(8,128)(2,1)S(1)}, bf16[64,1280]{1,0:T(8,128)(2,1)}, u32[]{:S(2)}, u32[]{:S(2)}) collective-permute-start(bf16[64,1280]{1,0:T(8,128)(2,1)S(1)} %add_convert_fusion.8), channel_id=1, source_target_pairs={{0,2},{1,3},{2,0},{3,1},{4,6},{5,7},{6,4},{7,5},{8,10},{9,11},{10,... | collective-permute-start | bytes 491528 | tf_op jit(solution)/shard_map/ppermute | solution.py:463
  74.1 1.6 %collective-permute-start.20 = (bf16[128,512]{1,0:T(8,128)(2,1)S(1)}, bf16[128,512]{1,0:T(8,128)(2,1)S(1)}, u32[]{:S(2)}, u32[]{:S(2)}) collective-permute-start(bf16[128,512]{1,0:T(8,128)(2,1)S(1)} %add_convert_fusion.12), channel_id=1, source_target_pairs={{0,4},{1,5},{2,6},{3,7},{4,0},{5,1},{6,2},{7,3},{8,12},{9,13},{10,... | collective-permute-start | bytes 393224 | tf_op jit(solution)/shard_map/ppermute | solution.py:463
  75.7 2.5 %collective-permute-done.13 = bf16[64,1280]{1,0:T(8,128)(2,1)} collective-permute-done((bf16[64,1280]{1,0:T(8,128)(2,1)S(1)}, bf16[64,1280]{1,0:T(8,128)(2,1)}, u32[]{:S(2)}, u32[]{:S(2)}) %collective-permute-start.13) | collective-permute-done | bytes 163872 | tf_op jit(solution)/shard_map/ppermute | solution.py:463
  79.2 1.7 %collective-permute-start.14 = (bf16[64,1280]{1,0:T(8,128)(2,1)S(1)}, bf16[64,1280]{1,0:T(8,128)(2,1)S(1)}, u32[]{:S(2)}, u32[]{:S(2)}) collective-permute-start(bf16[64,1280]{1,0:T(8,128)(2,1)S(1)} %add_convert_fusion.7), channel_id=1, source_target_pairs={{0,8},{1,9},{2,10},{3,11},{4,12},{5,13},{6,14},{7,15},{8,0},{9,1},... | collective-permute-start | bytes 491528 | tf_op jit(solution)/shard_map/ppermute | solution.py:463
  82.1 1.6 %collective-permute-start.8 = (bf16[256,512]{1,0:T(8,128)(2,1)S(1)}, bf16[256,512]{1,0:T(8,128)(2,1)S(1)}, u32[]{:S(2)}, u32[]{:S(2)}) collective-permute-start(bf16[256,512]{1,0:T(8,128)(2,1)S(1)} %constant_dynamic-slice_fusion), channel_id=1, source_target_pairs={{0,4},{1,5},{2,6},{3,7},{4,0},{5,1},{6,2},{7,3},{8,12},{9,13},{10,... | collective-permute-start | bytes 786440 | tf_op jit(solution)/shard_map/ppermute | solution.py:463
  84.6 2.7 %collective-permute-start.15 = (bf16[64,1280]{1,0:T(8,128)(2,1)S(1)}, bf16[64,1280]{1,0:T(8,128)(2,1)S(1)}, u32[]{:S(2)}, u32[]{:S(2)}) collective-permute-start(bf16[64,1280]{1,0:T(8,128)(2,1)S(1)} %add_convert_fusion.6), channel_id=1, source_target_pairs={{0,16},{1,17},{2,18},{3,19},{4,20},{5,21},{6,22},{7,23},{8,24},{9,... | collective-permute-start | bytes 491528 | tf_op jit(solution)/shard_map/ppermute | solution.py:463
  89.5 7.8 %collective-permute-done.15 = bf16[64,1280]{1,0:T(8,128)(2,1)S(1)} collective-permute-done((bf16[64,1280]{1,0:T(8,128)(2,1)S(1)}, bf16[64,1280]{1,0:T(8,128)(2,1)S(1)}, u32[]{:S(2)}, u32[]{:S(2)}) %collective-permute-start.15) | collective-permute-done | bytes 163872 | tf_op jit(solution)/shard_map/ppermute | solution.py:463
  97.3 1.6 %collective-permute-start.16 = (bf16[64,1280]{1,0:T(8,128)(2,1)S(1)}, bf16[64,1280]{1,0:T(8,128)(2,1)S(1)}, u32[]{:S(2)}, u32[]{:S(2)}) collective-permute-start(bf16[64,1280]{1,0:T(8,128)(2,1)S(1)} %add_convert_fusion.5), channel_id=1, source_target_pairs={{0,2},{1,3},{2,0},{3,1},{4,6},{5,7},{6,4},{7,5},{8,10},{9,11},{10,... | collective-permute-start | bytes 491528 | tf_op jit(solution)/shard_map/ppermute | solution.py:463
  99.0 3.7 %collective-permute-done.16 = bf16[64,1280]{1,0:T(8,128)(2,1)S(1)} collective-permute-done((bf16[64,1280]{1,0:T(8,128)(2,1)S(1)}, bf16[64,1280]{1,0:T(8,128)(2,1)S(1)}, u32[]{:S(2)}, u32[]{:S(2)}) %collective-permute-start.16) | collective-permute-done | bytes 163872 | tf_op jit(solution)/shard_map/ppermute | solution.py:463
  102.8 1.6 %collective-permute-start.17 = (bf16[128,1280]{1,0:T(8,128)(2,1)S(1)}, bf16[128,1280]{1,0:T(8,128)(2,1)S(1)}, u32[]{:S(2)}, u32[]{:S(2)}) collective-permute-start(bf16[128,1280]{1,0:T(8,128)(2,1)S(1)} %maximum_select_fusion.3), channel_id=1, source_target_pairs={{0,4},{1,5},{2,6},{3,7},{4,0},{5,1},{6,2},{7,3},{8,12},{9,13},{10,... | collective-permute-start | bytes 983048 | tf_op jit(solution)/shard_map/ppermute | solution.py:463
  105.0 1.4 %collective-permute-done.10 = bf16[128,512]{1,0:T(8,128)(2,1)S(1)} collective-permute-done((bf16[128,512]{1,0:T(8,128)(2,1)S(1)}, bf16[128,512]{1,0:T(8,128)(2,1)S(1)}, u32[]{:S(2)}, u32[]{:S(2)}) %collective-permute-start.10) | collective-permute-done | bytes 131104 | tf_op jit(solution)/shard_map/ppermute | solution.py:463
  106.5 3.4 %collective-permute-done.17 = bf16[128,1280]{1,0:T(8,128)(2,1)S(1)} collective-permute-done((bf16[128,1280]{1,0:T(8,128)(2,1)S(1)}, bf16[128,1280]{1,0:T(8,128)(2,1)S(1)}, u32[]{:S(2)}, u32[]{:S(2)}) %collective-permute-start.17) | collective-permute-done | bytes 327712 | tf_op jit(solution)/shard_map/ppermute | solution.py:463
  110.1 1.2 collective-permute-done.22
  111.4 1.6 %collective-permute-start.23 = (bf16[256,512]{1,0:T(8,128)(2,1)S(1)}, bf16[256,512]{1,0:T(8,128)(2,1)S(1)}, u32[]{:S(2)}, u32[]{:S(2)}) collective-permute-start(bf16[256,512]{1,0:T(8,128)(2,1)S(1)} %maximum_select_fusion.5), channel_id=1, source_target_pairs={{0,8},{1,9},{2,10},{3,11},{4,12},{5,13},{6,14},{7,15},{8,0},{9,1},... | collective-permute-start | bytes 786440 | tf_op jit(solution)/shard_map/ppermute | solution.py:463
  113.1 1.6 %collective-permute-start.12 = (bf16[256,512]{1,0:T(8,128)(2,1)S(1)}, bf16[256,512]{1,0:T(8,128)(2,1)S(1)}, u32[]{:S(2)}, u32[]{:S(2)}) collective-permute-start(bf16[256,512]{1,0:T(8,128)(2,1)S(1)} %maximum_select_fusion.4), channel_id=1, source_target_pairs={{0,4},{1,5},{2,6},{3,7},{4,0},{5,1},{6,2},{7,3},{8,12},{9,13},{10,... | collective-permute-start | bytes 786440 | tf_op jit(solution)/shard_map/ppermute | solution.py:463
  114.7 1.4 %add_convert_fusion = bf16[1024,512]{1,0:T(8,128)(2,1)} fusion(bf16[1024,512]{1,0:T(8,128)(2,1)S(1)} %collective-permute-done.24, bf16[1024,512]{1,0:T(8,128)(2,1)S(1)} %copy-done.4, bf16[1024,512]{1,0:T(8,128)(2,1)S(1)} %copy-done.3, f32[512]{0:T(512)S(1)} %convert_element_type.231), kind=kLoop, calls=%fused_computation.4 | loop fusion | flops 3670016 | bytes 4196352 | tf_op jit(solution)/shard_map/convert_element_type | solution.py:689
  116.1 2.9 %collective-permute-done.23 = bf16[256,512]{1,0:T(8,128)(2,1)S(1)} collective-permute-done((bf16[256,512]{1,0:T(8,128)(2,1)S(1)}, bf16[256,512]{1,0:T(8,128)(2,1)S(1)}, u32[]{:S(2)}, u32[]{:S(2)}) %collective-permute-start.23) | collective-permute-done | bytes 262176 | tf_op jit(solution)/shard_map/ppermute | solution.py:463
  119.0 1.2 fusion.4
  120.2 1.6 %unpack.1 = (f32[1,512]{1,0:T(1,128)}, f32[1,512]{1,0:T(1,128)}, f32[8,512]{1,0:T(8,128)}, f32[512,512]{1,0:T(8,128)}, f32[512,512]{1,0:T(8,128)}, /*index=5*/f3...) custom-call(s32[1]{0:T(128)} %bitcast.4.place, ...), custom_call_target="tpu_custom_call" | custom-call | flops 1000 | bytes 1000 | tf_op jit(solution)/shard_map/unpack/pallas_call | solution.py:450
  (66 shorter events, 10.5 us)
Async XLA Ops:
  2.6 14.4 %copy-start.2 = (bf16[1040,512]{1,0:T(8,128)(2,1)}, bf16[1040,512]{1,0:T(8,128)(2,1)S(1)}, u32[]{:S(2)}) copy-start(bf16[1040,512]{1,0:T(8,128)(2,1)S(1)} %fusion.3.refs_2_) | copy-start | bytes 3194884
  2.6 27.7 %collective-permute-start.2 = (bf16[1040,512]{1,0:T(8,128)(2,1)S(1)}, bf16[1040,512]{1,0:T(8,128)(2,1)S(1)}, u32[]{:S(2)}, u32[]{:S(2)}) collective-permute-start(bf16[1040,512]{1,0:T(8,128)(2,1)S(1)} %fusion.3.refs_2_), channel_id=1, source_target_pairs={{0,2},{1,3},{2,0},{3,1},{4,6},{5,7},{6,4},{7,5},{8,10},{9,11},{10,... | collective-permute-start | bytes 3194888 | tf_op jit(solution)/shard_map/ppermute | solution.py:463
  17.0 7.0 %collective-permute-start.1 = (bf16[1024,512]{1,0:T(8,128)(2,1)}, bf16[1024,512]{1,0:T(8,128)(2,1)S(1)}, u32[]{:S(2)}, u32[]{:S(2)}) collective-permute-start(bf16[1024,512]{1,0:T(8,128)(2,1)} %get-tuple-element.73.refs_1_.glow), channel_id=1, source_target_pairs={{0,1},{1,0},{2,3},{3,2},{4,5},{5,4},{6,7},{7,6},{8,9},{9,8},{10,11... | collective-permute-start | bytes 3145736 | tf_op jit(solution)/shard_map/ppermute | solution.py:463
  17.1 6.9 %collective-permute-start = (bf16[1024,512]{1,0:T(8,128)(2,1)}, bf16[1024,512]{1,0:T(8,128)(2,1)S(1)}, u32[]{:S(2)}, u32[]{:S(2)}) collective-permute-start(bf16[1024,512]{1,0:T(8,128)(2,1)} %get-tuple-element.72.refs_0_), channel_id=1, source_target_pairs={{0,1},{1,0},{2,3},{3,2},{4,5},{5,4},{6,7},{7,6},{8,9},{9,8},{10,11... | collective-permute-start | bytes 3145736 | tf_op jit(solution)/shard_map/ppermute | solution.py:463
  35.0 7.5 %copy-start = (bf16[1024,512]{1,0:T(8,128)(2,1)}, bf16[1024,512]{1,0:T(8,128)(2,1)S(1)}, u32[]{:S(2)}) copy-start(bf16[1024,512]{1,0:T(8,128)(2,1)S(1)} %get-tuple-element.115) | copy-start | bytes 3145732
  35.0 8.0 %collective-permute-start.3 = (bf16[1024,512]{1,0:T(8,128)(2,1)}, bf16[1024,512]{1,0:T(8,128)(2,1)S(1)}, u32[]{:S(2)}, u32[]{:S(2)}) collective-permute-start(bf16[1024,512]{1,0:T(8,128)(2,1)} %get-tuple-element.86), channel_id=1, source_target_pairs={{0,1},{1,0},{2,3},{3,2},{4,5},{5,4},{6,7},{7,6},{8,9},{9,8},{10,11... | collective-permute-start | bytes 3145736 | tf_op jit(solution)/shard_map/ppermute | solution.py:463
  42.5 15.2 %collective-permute-start.4 = (bf16[512,512]{1,0:T(8,128)(2,1)}, bf16[512,512]{1,0:T(8,128)(2,1)}, u32[]{:S(2)}, u32[]{:S(2)}) collective-permute-start(bf16[512,512]{1,0:T(8,128)(2,1)} %get-tuple-element.97), channel_id=1, source_target_pairs={{0,2},{1,3},{2,0},{3,1},{4,6},{5,7},{6,4},{7,5},{8,10},{9,11},{10,... | collective-permute-start | bytes 1572872 | tf_op jit(solution)/shard_map/ppermute | solution.py:463
  57.6 2.2 %collective-permute-start.5 = (bf16[256,1280]{1,0:T(8,128)(2,1)S(1)}, bf16[256,1280]{1,0:T(8,128)(2,1)S(1)}, u32[]{:S(2)}, u32[]{:S(2)}) collective-permute-start(bf16[256,1280]{1,0:T(8,128)(2,1)S(1)} %get-tuple-element.98), channel_id=1, source_target_pairs={{0,1},{1,0},{2,3},{3,2},{4,5},{5,4},{6,7},{7,6},{8,9},{9,8},{10,11... | collective-permute-start | bytes 1966088 | tf_op jit(solution)/shard_map/ppermute | solution.py:463
  57.8 14.5 %collective-permute-start.7 = (bf16[512,512]{1,0:T(8,128)(2,1)}, bf16[512,512]{1,0:T(8,128)(2,1)}, u32[]{:S(2)}, u32[]{:S(2)}) collective-permute-start(bf16[512,512]{1,0:T(8,128)(2,1)} %get-tuple-element.99), channel_id=1, source_target_pairs={{0,2},{1,3},{2,0},{3,1},{4,6},{5,7},{6,4},{7,5},{8,10},{9,11},{10,... | collective-permute-start | bytes 1572872 | tf_op jit(solution)/shard_map/ppermute | solution.py:463
  60.0 14.0 %copy-start.7 = (bf16[512]{0:T(512)(128)(2,1)S(1)}, bf16[512]{0:T(512)(128)(2,1)}, u32[]{:S(2)}) copy-start(bf16[512]{0:T(512)(128)(2,1)} %param.33) | copy-start | bytes 3076
  60.0 14.0 %copy-start.1 = (bf16[1024,512]{1,0:T(8,128)(2,1)S(1)}, bf16[1024,512]{1,0:T(8,128)(2,1)}, u32[]{:S(2)}) copy-start(bf16[1024,512]{1,0:T(8,128)(2,1)} %copy-done) | copy-start | bytes 3145732
  60.0 12.4 %collective-permute-start.6 = (bf16[128,1280]{1,0:T(8,128)(2,1)S(1)}, bf16[128,1280]{1,0:T(8,128)(2,1)S(1)}, u32[]{:S(2)}, u32[]{:S(2)}) collective-permute-start(bf16[128,1280]{1,0:T(8,128)(2,1)S(1)} %get-tuple-element.131), channel_id=1, source_target_pairs={{0,4},{1,5},{2,6},{3,7},{4,0},{5,1},{6,2},{7,3},{8,12},{9,13},{10,... | collective-permute-start | bytes 983048 | tf_op jit(solution)/shard_map/ppermute | solution.py:463
  61.6 19.3 %copy-start.5 = (bf16[512,512]{1,0:T(8,128)(2,1)S(1)}, bf16[512,512]{1,0:T(8,128)(2,1)}, u32[]{:S(2)}) copy-start(bf16[512,512]{1,0:T(8,128)(2,1)} %get-tuple-element.77) | copy-start | bytes 1572868
  62.9 11.2 %collective-permute-start.19 = (bf16[256,512]{1,0:T(8,128)(2,1)S(1)}, bf16[256,512]{1,0:T(8,128)(2,1)S(1)}, u32[]{:S(2)}, u32[]{:S(2)}) collective-permute-start(bf16[256,512]{1,0:T(8,128)(2,1)S(1)} %constant_dynamic-slice_fusion.1), channel_id=1, source_target_pairs={{0,8},{1,9},{2,10},{3,11},{4,12},{5,13},{6,14},{7,15},{8,0},{9,1},... | collective-permute-start | bytes 786440 | tf_op jit(solution)/shard_map/ppermute | solution.py:463
  72.4 5.8 %collective-permute-start.13 = (bf16[64,1280]{1,0:T(8,128)(2,1)S(1)}, bf16[64,1280]{1,0:T(8,128)(2,1)}, u32[]{:S(2)}, u32[]{:S(2)}) collective-permute-start(bf16[64,1280]{1,0:T(8,128)(2,1)S(1)} %add_convert_fusion.8), channel_id=1, source_target_pairs={{0,2},{1,3},{2,0},{3,1},{4,6},{5,7},{6,4},{7,5},{8,10},{9,11},{10,... | collective-permute-start | bytes 491528 | tf_op jit(solution)/shard_map/ppermute | solution.py:463
  74.0 40.7 %collective-permute-start.24 = (bf16[1024,512]{1,0:T(8,128)(2,1)S(1)}, bf16[1024,512]{1,0:T(8,128)(2,1)S(1)}, u32[]{:S(2)}, u32[]{:S(2)}) collective-permute-start(bf16[1024,512]{1,0:T(8,128)(2,1)S(1)} %copy-done.1), channel_id=1, source_target_pairs={{0,1},{1,0},{2,3},{3,2},{4,5},{5,4},{6,7},{7,6},{8,9},{9,8},{10,11... | collective-permute-start | bytes 3145736 | tf_op jit(solution)/shard_map/ppermute | solution.py:463
  74.1 13.2 %collective-permute-start.20 = (bf16[128,512]{1,0:T(8,128)(2,1)S(1)}, bf16[128,512]{1,0:T(8,128)(2,1)S(1)}, u32[]{:S(2)}, u32[]{:S(2)}) collective-permute-start(bf16[128,512]{1,0:T(8,128)(2,1)S(1)} %add_convert_fusion.12), channel_id=1, source_target_pairs={{0,4},{1,5},{2,6},{3,7},{4,0},{5,1},{6,2},{7,3},{8,12},{9,13},{10,... | collective-permute-start | bytes 393224 | tf_op jit(solution)/shard_map/ppermute | solution.py:463
  79.2 5.4 %collective-permute-start.14 = (bf16[64,1280]{1,0:T(8,128)(2,1)S(1)}, bf16[64,1280]{1,0:T(8,128)(2,1)S(1)}, u32[]{:S(2)}, u32[]{:S(2)}) collective-permute-start(bf16[64,1280]{1,0:T(8,128)(2,1)S(1)} %add_convert_fusion.7), channel_id=1, source_target_pairs={{0,8},{1,9},{2,10},{3,11},{4,12},{5,13},{6,14},{7,15},{8,0},{9,1},... | collective-permute-start | bytes 491528 | tf_op jit(solution)/shard_map/ppermute | solution.py:463
  82.1 6.6 %collective-permute-start.8 = (bf16[256,512]{1,0:T(8,128)(2,1)S(1)}, bf16[256,512]{1,0:T(8,128)(2,1)S(1)}, u32[]{:S(2)}, u32[]{:S(2)}) collective-permute-start(bf16[256,512]{1,0:T(8,128)(2,1)S(1)} %constant_dynamic-slice_fusion), channel_id=1, source_target_pairs={{0,4},{1,5},{2,6},{3,7},{4,0},{5,1},{6,2},{7,3},{8,12},{9,13},{10,... | collective-permute-start | bytes 786440 | tf_op jit(solution)/shard_map/ppermute | solution.py:463
  84.6 12.7 %collective-permute-start.15 = (bf16[64,1280]{1,0:T(8,128)(2,1)S(1)}, bf16[64,1280]{1,0:T(8,128)(2,1)S(1)}, u32[]{:S(2)}, u32[]{:S(2)}) collective-permute-start(bf16[64,1280]{1,0:T(8,128)(2,1)S(1)} %add_convert_fusion.6), channel_id=1, source_target_pairs={{0,16},{1,17},{2,18},{3,19},{4,20},{5,21},{6,22},{7,23},{8,24},{9,... | collective-permute-start | bytes 491528 | tf_op jit(solution)/shard_map/ppermute | solution.py:463
  87.4 17.0 %collective-permute-start.21 = (bf16[128,512]{1,0:T(8,128)(2,1)S(1)}, bf16[128,512]{1,0:T(8,128)(2,1)S(1)}, u32[]{:S(2)}, u32[]{:S(2)}) collective-permute-start(bf16[128,512]{1,0:T(8,128)(2,1)S(1)} %add_convert_fusion.11), channel_id=1, source_target_pairs={{0,16},{1,17},{2,18},{3,19},{4,20},{5,21},{6,22},{7,23},{8,24},{9,... | collective-permute-start | bytes 393224 | tf_op jit(solution)/shard_map/ppermute | solution.py:463
  88.7 10.2 %collective-permute-start.9 = (bf16[128,512]{1,0:T(8,128)(2,1)S(1)}, bf16[128,512]{1,0:T(8,128)(2,1)S(1)}, u32[]{:S(2)}, u32[]{:S(2)}) collective-permute-start(bf16[128,512]{1,0:T(8,128)(2,1)S(1)} %add_convert_fusion.16), channel_id=1, source_target_pairs={{0,8},{1,9},{2,10},{3,11},{4,12},{5,13},{6,14},{7,15},{8,0},{9,1},... | collective-permute-start | bytes 393224 | tf_op jit(solution)/shard_map/ppermute | solution.py:463
  97.3 5.4 %collective-permute-start.16 = (bf16[64,1280]{1,0:T(8,128)(2,1)S(1)}, bf16[64,1280]{1,0:T(8,128)(2,1)S(1)}, u32[]{:S(2)}, u32[]{:S(2)}) collective-permute-start(bf16[64,1280]{1,0:T(8,128)(2,1)S(1)} %add_convert_fusion.5), channel_id=1, source_target_pairs={{0,2},{1,3},{2,0},{3,1},{4,6},{5,7},{6,4},{7,5},{8,10},{9,11},{10,... | collective-permute-start | bytes 491528 | tf_op jit(solution)/shard_map/ppermute | solution.py:463
  99.0 7.4 %collective-permute-start.10 = (bf16[128,512]{1,0:T(8,128)(2,1)S(1)}, bf16[128,512]{1,0:T(8,128)(2,1)S(1)}, u32[]{:S(2)}, u32[]{:S(2)}) collective-permute-start(bf16[128,512]{1,0:T(8,128)(2,1)S(1)} %add_convert_fusion.15), channel_id=1, source_target_pairs={{0,16},{1,17},{2,18},{3,19},{4,20},{5,21},{6,22},{7,23},{8,24},{9,... | collective-permute-start | bytes 393224 | tf_op jit(solution)/shard_map/ppermute | solution.py:463
  102.8 11.9 %copy-start.3 = (bf16[1024,512]{1,0:T(8,128)(2,1)S(1)}, bf16[1024,512]{1,0:T(8,128)(2,1)}, u32[]{:S(2)}) copy-start(bf16[1024,512]{1,0:T(8,128)(2,1)} %get-tuple-element.89.res) | copy-start | bytes 3145732
  102.8 11.9 %copy-start.4 = (bf16[1024,512]{1,0:T(8,128)(2,1)S(1)}, bf16[1024,512]{1,0:T(8,128)(2,1)}, u32[]{:S(2)}) copy-start(bf16[1024,512]{1,0:T(8,128)(2,1)} %get-tuple-element.114) | copy-start | bytes 3145732
  102.8 7.1 %collective-permute-start.17 = (bf16[128,1280]{1,0:T(8,128)(2,1)S(1)}, bf16[128,1280]{1,0:T(8,128)(2,1)S(1)}, u32[]{:S(2)}, u32[]{:S(2)}) collective-permute-start(bf16[128,1280]{1,0:T(8,128)(2,1)S(1)} %maximum_select_fusion.3), channel_id=1, source_target_pairs={{0,4},{1,5},{2,6},{3,7},{4,0},{5,1},{6,2},{7,3},{8,12},{9,13},{10,... | collective-permute-start | bytes 983048 | tf_op jit(solution)/shard_map/ppermute | solution.py:463
  104.4 6.9 %collective-permute-start.22 = (bf16[128,512]{1,0:T(8,128)(2,1)S(1)}, bf16[128,512]{1,0:T(8,128)(2,1)S(1)}, u32[]{:S(2)}, u32[]{:S(2)}) collective-permute-start(bf16[128,512]{1,0:T(8,128)(2,1)S(1)} %add_convert_fusion.10), channel_id=1, source_target_pairs={{0,4},{1,5},{2,6},{3,7},{4,0},{5,1},{6,2},{7,3},{8,12},{9,13},{10,... | collective-permute-start | bytes 393224 | tf_op jit(solution)/shard_map/ppermute | solution.py:463
  106.4 6.6 %collective-permute-start.11 = (bf16[128,512]{1,0:T(8,128)(2,1)S(1)}, bf16[128,512]{1,0:T(8,128)(2,1)S(1)}, u32[]{:S(2)}, u32[]{:S(2)}) collective-permute-start(bf16[128,512]{1,0:T(8,128)(2,1)S(1)} %add_convert_fusion.14), channel_id=1, source_target_pairs={{0,8},{1,9},{2,10},{3,11},{4,12},{5,13},{6,14},{7,15},{8,0},{9,1},... | collective-permute-start | bytes 393224 | tf_op jit(solution)/shard_map/ppermute | solution.py:463
  110.1 10.1 %collective-permute-start.18 = (bf16[256,1280]{1,0:T(8,128)(2,1)S(1)}, bf16[256,1280]{1,0:T(8,128)(2,1)S(1)}, u32[]{:S(2)}, u32[]{:S(2)}) collective-permute-start(bf16[256,1280]{1,0:T(8,128)(2,1)S(1)} %maximum_select_fusion.mine), channel_id=1, source_target_pairs={{0,1},{1,0},{2,3},{3,2},{4,5},{5,4},{6,7},{7,6},{8,9},{9,8},{10,11... | collective-permute-start | bytes 1966088 | tf_op jit(solution)/shard_map/ppermute | solution.py:463
  111.4 7.6 %collective-permute-start.23 = (bf16[256,512]{1,0:T(8,128)(2,1)S(1)}, bf16[256,512]{1,0:T(8,128)(2,1)S(1)}, u32[]{:S(2)}, u32[]{:S(2)}) collective-permute-start(bf16[256,512]{1,0:T(8,128)(2,1)S(1)} %maximum_select_fusion.5), channel_id=1, source_target_pairs={{0,8},{1,9},{2,10},{3,11},{4,12},{5,13},{6,14},{7,15},{8,0},{9,1},... | collective-permute-start | bytes 786440 | tf_op jit(solution)/shard_map/ppermute | solution.py:463
  113.1 8.6 %collective-permute-start.12 = (bf16[256,512]{1,0:T(8,128)(2,1)S(1)}, bf16[256,512]{1,0:T(8,128)(2,1)S(1)}, u32[]{:S(2)}, u32[]{:S(2)}) collective-permute-start(bf16[256,512]{1,0:T(8,128)(2,1)S(1)} %maximum_select_fusion.4), channel_id=1, source_target_pairs={{0,4},{1,5},{2,6},{3,7},{4,0},{5,1},{6,2},{7,3},{8,12},{9,13},{10,... | collective-permute-start | bytes 786440 | tf_op jit(solution)/shard_map/ppermute | solution.py:463
  (1 other events, 4.0 us)

commit v4 on v3

--- a/solution.py
+++ b/solution.py
@@ -65,47 +65,16 @@
     return min(max(tile - 1, 0), tiles - width) * TILE, width * TILE
 
 
-class Copies:
-    def __init__(self, semaphores):
-        self.semaphores = semaphores
-        self.used = 0
-        self.pending = {}
-
-    def start(self, name, source, target):
-        copy = pltpu.make_async_copy(source, target, self.semaphores.at[self.used])
-        self.used += 1
-        copy.start()
-        self.pending.setdefault(name, []).append(copy)
-
-    def wait(self, *names):
-        for name in names:
-            for copy in self.pending.pop(name, ()):
-                copy.wait()
-
-    def finish(self):
-        self.wait(*list(self.pending))
-
-
 def attend_kernel(
-    sent, valid, expert, gain1, shift1, gain2, shift2, router,
-    tok_far, wq_far, wkv_far, cot_far, wo_far,
-    res_far, low2_far, glow_far, mixed_far, qsel_far, kv_far, chance_far, gates_far,
-    tok, wq, wkv, cot, wo,
+    sent, valid, expert, gain1, shift1, gain2, shift2, router, tok, wq, wkv, cot, wo,
     res, low2, glow, mixed, qsel, kv, chance, gates,
-    queries, logits, semaphores,
+    queries, logits,
 ):
     rows, width = tok.shape
     tiles = rows // TILE
     pairs = width // LANES
     scale = (wkv.shape[1] // 2) ** -0.5
-    copies = Copies(semaphores)
-    copies.start("tok", tok_far, tok)
-    copies.start("wq", wq_far, wq)
-    copies.start("wkv", wkv_far, wkv)
-    copies.start("cot", cot_far, cot)
-    copies.start("wo", wo_far, wo)
     half_lane = lax.broadcasted_iota(jnp.int32, (BIG, LANES), 1) < LANES // 2
-    copies.wait("tok", "wq", "wkv")
     for at in range(0, rows, BIG):
         span = pl.ds(at, BIG)
         hat, _ = normed(tok[span, :].astype(F32))
@@ -116,8 +85,6 @@
         turned = pltpu.roll(both, LANES // 2, 1)
         kv[span, :LANES] = jnp.where(half_lane, both, turned).astype(BF16)
         kv[span, LANES:] = jnp.where(half_lane, turned, both).astype(BF16)
-    copies.start("out", kv, kv_far)
-    copies.wait("cot", "wo")
     for tile in range(tiles):
         at = tile * TILE
         span = pl.ds(at, TILE)
@@ -143,12 +110,8 @@
         gate0 = raise0 / (raise0 + raise1)
         gate1 = raise1 / (raise0 + raise1)
         lane = lax.broadcasted_iota(jnp.int32, (TILE, 8), 1)
-        gates[:, at : at + TILE] = jnp.transpose(
-            jnp.where(
-                lane == 0,
-                gate0,
-                jnp.where(lane == 1, gate1, jnp.where(lane == 2, first_id, second_id)),
-            )
+        gates[span, :] = jnp.where(
+            lane == 0, gate0, jnp.where(lane == 1, gate1, jnp.where(lane == 2, first_id, second_id))
         )
         masks = pair_masks(first_id, second_id, pairs)
         q0 = jnp.zeros((TILE, LANES), F32)
@@ -175,24 +138,12 @@
             mixed[span, pair * LANES : (pair + 1) * LANES] = jnp.where(
                 masks[pair][0], part0, jnp.where(masks[pair][1], part1, 0.0)
             ).astype(BF16)
-        if tile % (tiles // 2) == tiles // 2 - 1:
-            done = pl.ds((tile + 1 - tiles // 2), tiles // 2)
-            copies.start("out", chance.at[done], chance_far.at[done])
-    copies.start("out", glow, glow_far)
-    copies.start("out", qsel, qsel_far)
-    copies.start("out", mixed, mixed_far)
-    copies.start("out", gates, gates_far)
     for at in range(0, rows, BIG):
         span = pl.ds(at, BIG)
         total = tok[span, :].astype(F32) + dot(mixed[span, :], wo[...])
         res[span, :] = total.astype(BF16)
         hat, _ = normed(total)
         low2[span, :] = (hat * as_row(gain2) + as_row(shift2)).astype(BF16)
-        if (at + BIG) % (rows // 2) == 0:
-            done = pl.ds(at + BIG - rows // 2, rows // 2)
-            copies.start("out", low2.at[done, :], low2_far.at[done, :])
-            copies.start("out", res.at[done, :], res_far.at[done, :])
-    copies.finish()
 
 
 def ffn_kernel(*refs, units, more):
@@ -258,7 +209,7 @@
     if rows_in is not None:
         more.append("rows")
         operands += rows_in
-        spaces += ["far" if rows_far else "near"] * 2
+        spaces += ["far" if rows_far == "near" else "near"] * 2
     if weights_in is not None:
         more.append("weights")
         operands += weights_in
@@ -316,9 +267,8 @@
     for tile in range(tiles):
         at = tile * TILE
         span = pl.ds(at, TILE)
-        column = jnp.transpose(gates[:, at : at + TILE])
-        gate0, gate1 = column[:, 0:1], column[:, 1:2]
-        first_id, second_id = column[:, 2:3], column[:, 3:4]
+        gate0, gate1 = gates[span, 0:1], gates[span, 1:2]
+        first_id, second_id = gates[span, 2:3], gates[span, 3:4]
         masks = pair_masks(first_id, second_id, pairs)
         g0 = jnp.zeros((TILE, LANES), F32)
         g1 = jnp.zeros((TILE, LANES), F32)
@@ -418,24 +368,6 @@
     ]
 
 
-def far_call(kernel, name, near, far, out_shape, scratch, copies):
-    buffers = [pltpu.VMEM(item.shape, item.dtype) for item in list(far) + list(out_shape)]
-    return pl.pallas_call(
-        kernel,
-        out_shape=[pltpu.HBM(item.shape, item.dtype) for item in out_shape],
-        in_specs=[pl.BlockSpec(memory_space=pltpu.VMEM)] * len(near)
-        + [pl.BlockSpec(memory_space=pl.ANY)] * len(far),
-        out_specs=[pl.BlockSpec(memory_space=pl.ANY)] * len(out_shape),
-        scratch_shapes=buffers + scratch + [pltpu.SemaphoreType.DMA((copies,))],
-        compiler_params=pltpu.CompilerParams(vmem_limit_bytes=VMEM_LIMIT),
-        cost_estimate=pl.CostEstimate(flops=1000, bytes_accessed=1000, transcendentals=0),
-        name=name,
-    )(
-        *[pltpu.with_memory_space_constraint(item, pltpu.HBM) for item in near],
-        *[pltpu.with_memory_space_constraint(item, pltpu.HBM) for item in far],
-    )
-
-
 def placed_call(kernel, name, operands, spaces, out_shape, out_spaces, scratch):
     where = {"far": pltpu.HBM, "near": pltpu.VMEM}
     lies = [pltpu.SMEM if space == "scalar" else pltpu.VMEM for space in spaces]
@@ -584,32 +516,30 @@
     turned_router = router.T
     chips = n_mp // 2
     others = [swap(own, 2 * step, devices) for step in range(1, chips)]
-    res, low2, glow, mixed, qsel, kv, chance, gates = far_call(
+    operands = [
+        row(sentence_ids), row(validity), expert_ids.T, first_gain, first_shift, second_gain,
+        second_shift, turned_router, tokens, query_weight, keyval_weight, cotangent, output_weight,
+    ]
+    res, low2, glow, mixed, qsel, kv, chance, gates = placed_call(
         attend_kernel,
         "attend",
-        [
-            row(sentence_ids), row(validity), expert_ids.T, first_gain, first_shift, second_gain,
-            second_shift, turned_router,
-        ],
-        [tokens, query_weight, keyval_weight, cotangent, output_weight],
-        [
-            shape(rows, width),
-            shape(rows, width),
-            shape(rows, width),
-            shape(rows, width),
+        operands,
+        ["far"] * len(operands),
+        [shape(rows, width)] * 4
+        + [
             shape(tiles, 2 * TILE, LANES),
             shape(rows, 2 * LANES),
             shape(tiles, 2 * TILE, extent),
-            shape(8, rows, dtype=F32),
+            shape(rows, 8, dtype=F32),
         ],
+        ["far", "near", "near"] + ["far"] * 5,
         [pltpu.VMEM((rows, width), BF16), pltpu.VMEM((rows, router.shape[1]), F32)],
-        20,
     )
     low2_pair = swap(low2, 1, devices)
     glow_pair = swap(glow, 1, devices)
     dp_bits = [n_mp << at for at in range(n_dp.bit_length() - 1)]
     mp_bits = [1 << at for at in range(n_mp.bit_length() - 1)]
-    rows_own, grads_own = ffn("far", low2, glow, own, "far", units)
+    rows_own, grads_own = ffn("near", low2, glow, own, "far", units)
     rows_pair, grads_own = ffn(
         None, low2_pair, glow_pair, own, "far", units, weights_in=grads_own, rows_out=(None, None),
         final=True,
@@ -632,7 +562,7 @@
         if final:
             out_got, second_got = (swap(item, 1, devices) for item in rows_pair)
         rows_own, grads = ffn(
-            "far",
+            "near",
             low2,
             glow,
             others[step - 1],
@@ -654,7 +584,7 @@
             res, glow, output_weight, gates, mixed, kv, chance, qsel, tokens, query_weight,
             keyval_weight, first_gain, first_shift, second_gain, turned_router,
         ],
-        ["scalar", "near", None, None, None] + ["far"] * 15,
+        ["scalar", "near", None, None, None, "far", "near"] + ["far"] * 13,
         [shape(rows, width)] + [shape(width // 2, 2 * width + 2 * LANES)] * 2,
         ["far", "near", "near"],
         [
@@ -673,10 +603,10 @@
     contract_got = [item[0] for item in waiting]
     expand_got = [item[1] for item in waiting]
     send, contract_got = lax.optimization_barrier((send, contract_got))
-    first = Chain(plan(dp_bits[1:2] + dp_bits[:1] + dp_bits[2:]), place, devices)
+    first = Chain(plan(dp_bits[1:2] + dp_bits[:1] + dp_bits[2:], 1), place, devices)
     first.feed(sum_low([contract_sum, *contract_got]))
-    second = Chain(plan(dp_bits), place, devices)
-    chain = Chain(plan(order, 2)[:-1], place, devices).feed_halves(keep, send)
+    second = Chain(plan(dp_bits, 1), place, devices)
+    chain = Chain(plan(order, 1)[:-1], place, devices).feed_halves(keep, send)
     for at in range(len(chain.steps)):
         got = chain.send()
         if at == 1:
@@ -705,9 +635,7 @@
         [pltpu.VMEM((width, LANES), F32)],
     )
     second.run(len(second.steps) - 1)
-    got, unpacked, contract_grad, layer = lax.optimization_barrier(
-        (second.send(), unpacked, contract_grad, layer)
-    )
+    got, unpacked, layer = lax.optimization_barrier((second.send(), unpacked, layer))
     second.take(got)
     expand_sum = second.values
     expand_grad = jnp.concatenate(

time: 123 us -> 121 us (0.984)
  waiting for transfers between devices: 32.9 us -> 22.4 us
  starting transfers between devices: 26.5 us -> 34.2 us
  Pallas kernels: 52.4 us -> 50.3 us
  local copies, waits for them, and re-layouts: 0.77 us -> 2.3 us
    pallas_call x1 -> x0, Pallas kernels: 11.4 us -> none  [far_call(): pl.pallas_call(kernel, out_shape=[pltpu.HBM(item.shape, item.dtype) for i...]
    ppermute x25 -> x26, waiting for transfers between devices: 32.9 us -> 22.4 us  [swap(): return lax.ppermute(values, AXES, [(at, at ^ bit) for at in range(devices)])]
    pallas_call x6 -> x7, Pallas kernels: 41 us -> 50.3 us  [placed_call(): pl.pallas_call(kernel, out_shape=results, in_specs=[pl.BlockSpec(memory_s...]
    ppermute x25 -> x26, starting transfers between devices: 26.5 us -> 34.2 us  [swap(): return lax.ppermute(values, AXES, [(at, at ^ bit) for at in range(devices)])]
  transfers between devices with their start and end apart: 25 -> 26, of which waited for: 11 -> 12; matrix products, arithmetic and copies ran while one was open for 6% -> 7% of each run, Pallas kernels for 39% -> 38%
where the time goes in v4:
time: 121 us; the launch traced here: 120 us
  Pallas kernels  50.3 us (42%)
  starting transfers between devices  34.2 us (28%)
  waiting for transfers between devices  22.4 us (19%)
  other arithmetic  10.3 us (9%)
  local copies, waits for them, and re-layouts  2.3 us (2%)
    pallas_call x7, Pallas kernels, placed_call(): pl.pallas_call(kernel, out_shape=results, in_specs=[pl.BlockSpec(memory_s...  50.3 us
    ppermute x26, starting transfers between devices, swap(): return lax.ppermute(values, AXES, [(at, at ^ bit) for at in range(devices)])  34.2 us
    ppermute x26, waiting for transfers between devices, swap(): return lax.ppermute(values, AXES, [(at, at ^ bit) for at in range(devices)])  22.4 us
    convert_element_type x2, other arithmetic, sum_low(): functools.reduce(jnp.add, [part.astype(F32) for part in parts]).astype(BF16)  2.51 us
    convert_element_type x11, other arithmetic, add_low(): return (left.astype(F32) + right.astype(F32)).astype(BF16)  2.43 us
  transfers between devices with their start and end apart: 26, of which 12 were waited for; matrix products, arithmetic and copies ran while one was open for 7% of the time, Pallas kernels for 38%

profile of v4, /device:TPU:0, one launch (start us, length us, event | category | flops | bytes accessed | tf_op | source)
XLA Modules:
  0.0 120.4 jit_solution(4270786407956351055)
XLA Ops:
  2.6 3.0 %collective-permute-start.2 = (bf16[1040,512]{1,0:T(8,128)(2,1)S(1)}, bf16[1040,512]{1,0:T(8,128)(2,1)S(1)}, u32[]{:S(2)}, u32[]{:S(2)}) collective-permute-start(bf16[1040,512]{1,0:T(8,128)(2,1)S(1)} %fusion.3.refs_2_), channel_id=1, source_target_pairs={{0,2},{1,3},{2,0},{3,1},{4,6},{5,7},{6,4},{7,5},{8,10},{9,11},{10,... | collective-permute-start | bytes 3194888 | tf_op jit(solution)/shard_map/ppermute | solution.py:395
  5.6 10.6 %attend.1 = (bf16[1024,512]{1,0:T(8,128)(2,1)}, bf16[1024,512]{1,0:T(8,128)(2,1)S(1)}, bf16[1024,512]{1,0:T(8,128)(2,1)S(1)}, bf16[1024,512]{1,0:T(8,128)(2,1)},...) custom-call(s32[1,1024]{1,0:T(1,128)} %bitcast.15, ...), custom_call_target="tpu_custom_call" | custom-call | flops 1000 | bytes 1000 | tf_op jit(solution)/shard_map/attend/pallas_call | solution.py:382
  16.8 6.0 %ffn.4 = (bf16[1024,512]{1,0:T(8,128)(2,1)}, bf16[1024,512]{1,0:T(8,128)(2,1)}, bf16[512,512]{1,0:T(8,128)(2,1)}, bf16[512,512]{1,0:T(8,128)(2,1)}, f32[1,512]{1,0:T(1,128)S(1)}) custom-call(bf16[1024,512]{1,0:T(8,128)(2,1)S(1)} %get-tuple-element.71.refs_0_, bf16[1024,512]{1,0:T(8,128)(2,1)S(1)} %get-tuple-element.72.refs_1_.glow, bf16[1040,512]{1,0:T(8,128)(2,1)} %copy-done.4), custom_call_target="tpu_custom_call" | custom-call | flops 1000 | bytes 1000 | tf_op jit(solution)/shard_map/ffn/pallas_call | solution.py:382
  22.7 6.4 %ffn.5 = (bf16[1024,512]{1,0:T(8,128)(2,1)S(1)}, bf16[1024,512]{1,0:T(8,128)(2,1)S(1)}, bf16[512,512]{1,0:T(8,128)(2,1)}, bf16[512,512]{1,0:T(8,128)(2,1)}, f32[1,512]{1,0:T(1,128)S(1)}) custom-call(bf16[1024,512]{1,0:T(8,128)(2,1)S(1)} %collective-permute-done.refs_0_, bf16[1024,512]{1,0:T(8,128)(2,1)S(1)} %collective-permute-done.1.refs_1_, ...), custom_call_target="tpu_custom_call" | custom-call | flops 1000 | bytes 1000 | tf_op jit(solution)/shard_map/ffn/pallas_call | solution.py:382
  29.1 4.7 %ffn.6 = (bf16[1024,512]{1,0:T(8,128)(2,1)S(1)}, bf16[1024,512]{1,0:T(8,128)(2,1)}, bf16[512,512]{1,0:T(8,128)(2,1)}, bf16[512,512]{1,0:T(8,128)(2,1)}, f32[1,512]{1,0:T(1,128)S(1)}) custom-call(bf16[1024,512]{1,0:T(8,128)(2,1)S(1)} %collective-permute-done.refs_0_, bf16[1024,512]{1,0:T(8,128)(2,1)S(1)} %collective-permute-done.1.refs_1_, ...), custom_call_target="tpu_custom_call" | custom-call | flops 1000 | bytes 1000 | tf_op jit(solution)/shard_map/ffn/pallas_call | solution.py:382
  33.9 7.0 %ffn.7 = (bf16[1024,512]{1,0:T(8,128)(2,1)}, bf16[1024,512]{1,0:T(8,128)(2,1)S(1)}, bf16[512,512]{1,0:T(8,128)(2,1)}, bf16[512,512]{1,0:T(8,128)(2,1)}, f32[1,512]{1,0:T(1,128)S(1)}) custom-call(bf16[1024,512]{1,0:T(8,128)(2,1)S(1)} %get-tuple-element.71.refs_0_, bf16[1024,512]{1,0:T(8,128)(2,1)S(1)} %get-tuple-element.72.refs_1_.glow, ...), custom_call_target="tpu_custom_call" | custom-call | flops 1000 | bytes 1000 | tf_op jit(solution)/shard_map/ffn/pallas_call | solution.py:382
  40.9 1.7 %collective-permute-start.4 = (bf16[512,512]{1,0:T(8,128)(2,1)}, bf16[512,512]{1,0:T(8,128)(2,1)}, u32[]{:S(2)}, u32[]{:S(2)}) collective-permute-start(bf16[512,512]{1,0:T(8,128)(2,1)} %get-tuple-element.96), channel_id=1, source_target_pairs={{0,2},{1,3},{2,0},{3,1},{4,6},{5,7},{6,4},{7,5},{8,10},{9,11},{10,... | collective-permute-start | bytes 1572872 | tf_op jit(solution)/shard_map/ppermute | solution.py:395
  42.6 14.1 %back.1 = (bf16[1024,512]{1,0:T(8,128)(2,1)}, bf16[256,1280]{1,0:T(8,128)(2,1)S(1)}, bf16[256,1280]{1,0:T(8,128)(2,1)}) custom-call(s32[1]{0:T(128)} %bitcast.4.place, bf16[1024,512]{1,0:T(8,128)(2,1)S(1)} %get-tuple-element.84.second_own, bf16[1024,512]{1,0:T(8,128)(2,1)S(1)} %collective-permute-done.3.second_got, f32[1,512]{1,0:T(1,128)S(1)} %get-tuple-element.86.unit_own, ...), custom_call_target="tpu_custom_call" | custom-call | flops 1000 | bytes 1000 | tf_op jit(solution)/shard_map/back/pallas_call | solution.py:382
  58.1 1.3 %add_convert_fusion.1 = bf16[512,512]{1,0:T(8,128)(2,1)S(1)} fusion(bf16[512,512]{1,0:T(8,128)(2,1)} %collective-permute-done.4, bf16[512,512]{1,0:T(8,128)(2,1)} %get-tuple-element.125), kind=kLoop, calls=%fused_computation.7 | loop fusion | flops 1048576 | bytes 1572864 | tf_op jit(solution)/shard_map/convert_element_type | solution.py:467
  60.2 1.8 %collective-permute-start.21 = (bf16[256,512]{1,0:T(8,128)(2,1)}, bf16[256,512]{1,0:T(8,128)(2,1)}, u32[]{:S(2)}, u32[]{:S(2)}) collective-permute-start(bf16[256,512]{1,0:T(8,128)(2,1)} %constant_dynamic-slice_fusion.1), channel_id=1, source_target_pairs={{0,8},{1,9},{2,10},{3,11},{4,12},{5,13},{6,14},{7,15},{8,0},{9,1},... | collective-permute-start | bytes 786440 | tf_op jit(solution)/shard_map/ppermute | solution.py:395
  62.1 1.6 %collective-permute-start.6 = (bf16[128,1280]{1,0:T(8,128)(2,1)S(1)}, bf16[128,1280]{1,0:T(8,128)(2,1)S(1)}, u32[]{:S(2)}, u32[]{:S(2)}) collective-permute-start(bf16[128,1280]{1,0:T(8,128)(2,1)S(1)} %get-tuple-element.129), channel_id=1, source_target_pairs={{0,4},{1,5},{2,6},{3,7},{4,0},{5,1},{6,2},{7,3},{8,12},{9,13},{10,... | collective-permute-start | bytes 983048 | tf_op jit(solution)/shard_map/ppermute | solution.py:395
  63.8 5.0 %collective-permute-done.21 = bf16[256,512]{1,0:T(8,128)(2,1)} collective-permute-done((bf16[256,512]{1,0:T(8,128)(2,1)}, bf16[256,512]{1,0:T(8,128)(2,1)}, u32[]{:S(2)}, u32[]{:S(2)}) %collective-permute-start.21) | collective-permute-done | bytes 262176 | tf_op jit(solution)/shard_map/ppermute | solution.py:395
  69.8 1.7 %collective-permute-start.22 = (bf16[128,512]{1,0:T(8,128)(2,1)S(1)}, bf16[128,512]{1,0:T(8,128)(2,1)S(1)}, u32[]{:S(2)}, u32[]{:S(2)}) collective-permute-start(bf16[128,512]{1,0:T(8,128)(2,1)S(1)} %add_convert_fusion.9), channel_id=1, source_target_pairs={{0,4},{1,5},{2,6},{3,7},{4,0},{5,1},{6,2},{7,3},{8,12},{9,13},{10,... | collective-permute-start | bytes 393224 | tf_op jit(solution)/shard_map/ppermute | solution.py:395
  73.2 1.6 %collective-permute-done.22 = bf16[128,512]{1,0:T(8,128)(2,1)S(1)} collective-permute-done((bf16[128,512]{1,0:T(8,128)(2,1)S(1)}, bf16[128,512]{1,0:T(8,128)(2,1)S(1)}, u32[]{:S(2)}, u32[]{:S(2)}) %collective-permute-start.22) | collective-permute-done | bytes 131104 | tf_op jit(solution)/shard_map/ppermute | solution.py:395
  75.8 2.8 %collective-permute-start.23 = (bf16[128,512]{1,0:T(8,128)(2,1)S(1)}, bf16[128,512]{1,0:T(8,128)(2,1)S(1)}, u32[]{:S(2)}, u32[]{:S(2)}) collective-permute-start(bf16[128,512]{1,0:T(8,128)(2,1)S(1)} %add_convert_fusion.8), channel_id=1, source_target_pairs={{0,16},{1,17},{2,18},{3,19},{4,20},{5,21},{6,22},{7,23},{8,24},{9,... | collective-permute-start | bytes 393224 | tf_op jit(solution)/shard_map/ppermute | solution.py:395
  78.6 1.6 %collective-permute-start.14 = (bf16[32,1280]{1,0:T(8,128)(2,1)S(1)}, bf16[32,1280]{1,0:T(8,128)(2,1)S(1)}, u32[]{:S(2)}, u32[]{:S(2)}) collective-permute-start(bf16[32,1280]{1,0:T(8,128)(2,1)S(1)} %add_convert_fusion.17), channel_id=1, source_target_pairs={{0,8},{1,9},{2,10},{3,11},{4,12},{5,13},{6,14},{7,15},{8,0},{9,1},... | collective-permute-start | bytes 245768 | tf_op jit(solution)/shard_map/ppermute | solution.py:395
  81.5 1.7 %collective-permute-done.14 = bf16[32,1280]{1,0:T(8,128)(2,1)S(1)} collective-permute-done((bf16[32,1280]{1,0:T(8,128)(2,1)S(1)}, bf16[32,1280]{1,0:T(8,128)(2,1)S(1)}, u32[]{:S(2)}, u32[]{:S(2)}) %collective-permute-start.14) | collective-permute-done | bytes 81952 | tf_op jit(solution)/shard_map/ppermute | solution.py:395
  83.2 2.5 %collective-permute-start.15 = (bf16[32,1280]{1,0:T(8,128)(2,1)S(1)}, bf16[32,1280]{1,0:T(8,128)(2,1)S(1)}, u32[]{:S(2)}, u32[]{:S(2)}) collective-permute-start(bf16[32,1280]{1,0:T(8,128)(2,1)S(1)} %add_convert_fusion.16), channel_id=1, source_target_pairs={{0,16},{1,17},{2,18},{3,19},{4,20},{5,21},{6,22},{7,23},{8,24},{9,... | collective-permute-start | bytes 245768 | tf_op jit(solution)/shard_map/ppermute | solution.py:395
  85.7 1.6 %collective-permute-start.8 = (bf16[256,512]{1,0:T(8,128)(2,1)S(1)}, bf16[256,512]{1,0:T(8,128)(2,1)S(1)}, u32[]{:S(2)}, u32[]{:S(2)}) collective-permute-start(bf16[256,512]{1,0:T(8,128)(2,1)S(1)} %constant_dynamic-slice_fusion), channel_id=1, source_target_pairs={{0,4},{1,5},{2,6},{3,7},{4,0},{5,1},{6,2},{7,3},{8,12},{9,13},{10,... | collective-permute-start | bytes 786440 | tf_op jit(solution)/shard_map/ppermute | solution.py:395
  87.3 1.3 %collective-permute-done.15 = bf16[32,1280]{1,0:T(8,128)(2,1)S(1)} collective-permute-done((bf16[32,1280]{1,0:T(8,128)(2,1)S(1)}, bf16[32,1280]{1,0:T(8,128)(2,1)S(1)}, u32[]{:S(2)}, u32[]{:S(2)}) %collective-permute-start.15) | collective-permute-done | bytes 81952 | tf_op jit(solution)/shard_map/ppermute | solution.py:395
  88.6 2.1 %collective-permute-start.16 = (bf16[32,1280]{1,0:T(8,128)(2,1)S(1)}, bf16[32,1280]{1,0:T(8,128)(2,1)S(1)}, u32[]{:S(2)}, u32[]{:S(2)}) collective-permute-start(bf16[32,1280]{1,0:T(8,128)(2,1)S(1)} %add_convert_fusion.15), channel_id=1, source_target_pairs={{0,8},{1,9},{2,10},{3,11},{4,12},{5,13},{6,14},{7,15},{8,0},{9,1},... | collective-permute-start | bytes 245768 | tf_op jit(solution)/shard_map/ppermute | solution.py:395
  90.7 1.5 %collective-permute-done.8 = bf16[256,512]{1,0:T(8,128)(2,1)S(1)} collective-permute-done((bf16[256,512]{1,0:T(8,128)(2,1)S(1)}, bf16[256,512]{1,0:T(8,128)(2,1)S(1)}, u32[]{:S(2)}, u32[]{:S(2)}) %collective-permute-start.8) | collective-permute-done | bytes 262176 | tf_op jit(solution)/shard_map/ppermute | solution.py:395
  92.2 2.5 %collective-permute-start.9 = (bf16[128,512]{1,0:T(8,128)(2,1)S(1)}, bf16[128,512]{1,0:T(8,128)(2,1)S(1)}, u32[]{:S(2)}, u32[]{:S(2)}) collective-permute-start(bf16[128,512]{1,0:T(8,128)(2,1)S(1)} %add_convert_fusion.13), channel_id=1, source_target_pairs={{0,8},{1,9},{2,10},{3,11},{4,12},{5,13},{6,14},{7,15},{8,0},{9,1},... | collective-permute-start | bytes 393224 | tf_op jit(solution)/shard_map/ppermute | solution.py:395
  95.9 1.8 %collective-permute-done.9 = bf16[128,512]{1,0:T(8,128)(2,1)S(1)} collective-permute-done((bf16[128,512]{1,0:T(8,128)(2,1)S(1)}, bf16[128,512]{1,0:T(8,128)(2,1)S(1)}, u32[]{:S(2)}, u32[]{:S(2)}) %collective-permute-start.9) | collective-permute-done | bytes 131104 | tf_op jit(solution)/shard_map/ppermute | solution.py:395
  100.2 1.6 %collective-permute-start.18 = (bf16[128,1280]{1,0:T(8,128)(2,1)S(1)}, bf16[128,1280]{1,0:T(8,128)(2,1)S(1)}, u32[]{:S(2)}, u32[]{:S(2)}) collective-permute-start(bf16[128,1280]{1,0:T(8,128)(2,1)S(1)} %maximum_select_fusion.3), channel_id=1, source_target_pairs={{0,4},{1,5},{2,6},{3,7},{4,0},{5,1},{6,2},{7,3},{8,12},{9,13},{10,... | collective-permute-start | bytes 983048 | tf_op jit(solution)/shard_map/ppermute | solution.py:395
  102.4 1.3 %collective-permute-done.10 = bf16[128,512]{1,0:T(8,128)(2,1)S(1)} collective-permute-done((bf16[128,512]{1,0:T(8,128)(2,1)S(1)}, bf16[128,512]{1,0:T(8,128)(2,1)S(1)}, u32[]{:S(2)}, u32[]{:S(2)}) %collective-permute-start.10) | collective-permute-done | bytes 131104 | tf_op jit(solution)/shard_map/ppermute | solution.py:395
  103.8 2.2 %collective-permute-start.11 = (bf16[128,512]{1,0:T(8,128)(2,1)S(1)}, bf16[128,512]{1,0:T(8,128)(2,1)S(1)}, u32[]{:S(2)}, u32[]{:S(2)}) collective-permute-start(bf16[128,512]{1,0:T(8,128)(2,1)S(1)} %add_convert_fusion.11), channel_id=1, source_target_pairs={{0,8},{1,9},{2,10},{3,11},{4,12},{5,13},{6,14},{7,15},{8,0},{9,1},... | collective-permute-start | bytes 393224 | tf_op jit(solution)/shard_map/ppermute | solution.py:395
  106.0 1.4 %collective-permute-done.18 = bf16[128,1280]{1,0:T(8,128)(2,1)S(1)} collective-permute-done((bf16[128,1280]{1,0:T(8,128)(2,1)S(1)}, bf16[128,1280]{1,0:T(8,128)(2,1)S(1)}, u32[]{:S(2)}, u32[]{:S(2)}) %collective-permute-start.18) | collective-permute-done | bytes 327712 | tf_op jit(solution)/shard_map/ppermute | solution.py:395
  108.9 1.6 %collective-permute-start.25 = (bf16[256,512]{1,0:T(8,128)(2,1)S(1)}, bf16[256,512]{1,0:T(8,128)(2,1)S(1)}, u32[]{:S(2)}, u32[]{:S(2)}) collective-permute-start(bf16[256,512]{1,0:T(8,128)(2,1)S(1)} %maximum_select_fusion.5), channel_id=1, source_target_pairs={{0,8},{1,9},{2,10},{3,11},{4,12},{5,13},{6,14},{7,15},{8,0},{9,1},... | collective-permute-start | bytes 786440 | tf_op jit(solution)/shard_map/ppermute | solution.py:395
  111.5 1.4 %add_convert_fusion = bf16[1024,512]{1,0:T(8,128)(2,1)} fusion(bf16[1024,512]{1,0:T(8,128)(2,1)S(1)} %collective-permute-done.20, bf16[1024,512]{1,0:T(8,128)(2,1)S(1)} %copy-done.6, bf16[1024,512]{1,0:T(8,128)(2,1)S(1)} %copy-done.5, f32[512]{0:T(512)S(1)} %convert_element_type.227), kind=kLoop, calls=%fused_computation.4 | loop fusion | flops 3670016 | bytes 4196352 | tf_op jit(solution)/shard_map/convert_element_type | solution.py:619
  112.9 3.5 %collective-permute-done.25 = bf16[256,512]{1,0:T(8,128)(2,1)S(1)} collective-permute-done((bf16[256,512]{1,0:T(8,128)(2,1)S(1)}, bf16[256,512]{1,0:T(8,128)(2,1)S(1)}, u32[]{:S(2)}, u32[]{:S(2)}) %collective-permute-start.25) | collective-permute-done | bytes 262176 | tf_op jit(solution)/shard_map/ppermute | solution.py:395
  117.6 1.6 %unpack.1 = (f32[1,512]{1,0:T(1,128)}, f32[1,512]{1,0:T(1,128)}, f32[8,512]{1,0:T(8,128)}, f32[512,512]{1,0:T(8,128)}, f32[512,512]{1,0:T(8,128)}, /*index=5*/f3...) custom-call(s32[1]{0:T(128)} %bitcast.4.place, ...), custom_call_target="tpu_custom_call" | custom-call | flops 1000 | bytes 1000 | tf_op jit(solution)/shard_map/unpack/pallas_call | solution.py:382
  (71 shorter events, 19.0 us)
Async XLA Ops:
  2.6 13.6 %copy-start.4 = (bf16[1040,512]{1,0:T(8,128)(2,1)}, bf16[1040,512]{1,0:T(8,128)(2,1)S(1)}, u32[]{:S(2)}) copy-start(bf16[1040,512]{1,0:T(8,128)(2,1)S(1)} %fusion.3.refs_2_) | copy-start | bytes 3194884
  2.6 26.5 %collective-permute-start.2 = (bf16[1040,512]{1,0:T(8,128)(2,1)S(1)}, bf16[1040,512]{1,0:T(8,128)(2,1)S(1)}, u32[]{:S(2)}, u32[]{:S(2)}) collective-permute-start(bf16[1040,512]{1,0:T(8,128)(2,1)S(1)} %fusion.3.refs_2_), channel_id=1, source_target_pairs={{0,2},{1,3},{2,0},{3,1},{4,6},{5,7},{6,4},{7,5},{8,10},{9,11},{10,... | collective-permute-start | bytes 3194888 | tf_op jit(solution)/shard_map/ppermute | solution.py:395
  16.2 6.6 %collective-permute-start.1 = (bf16[1024,512]{1,0:T(8,128)(2,1)S(1)}, bf16[1024,512]{1,0:T(8,128)(2,1)S(1)}, u32[]{:S(2)}, u32[]{:S(2)}) collective-permute-start(bf16[1024,512]{1,0:T(8,128)(2,1)S(1)} %get-tuple-element.72.refs_1_.glow), channel_id=1, source_target_pairs={{0,1},{1,0},{2,3},{3,2},{4,5},{5,4},{6,7},{7,6},{8,9},{9,8},{10,11... | collective-permute-start | bytes 3145736 | tf_op jit(solution)/shard_map/ppermute | solution.py:395
  16.3 6.5 %collective-permute-start = (bf16[1024,512]{1,0:T(8,128)(2,1)S(1)}, bf16[1024,512]{1,0:T(8,128)(2,1)S(1)}, u32[]{:S(2)}, u32[]{:S(2)}) collective-permute-start(bf16[1024,512]{1,0:T(8,128)(2,1)S(1)} %get-tuple-element.71.refs_0_), channel_id=1, source_target_pairs={{0,1},{1,0},{2,3},{3,2},{4,5},{5,4},{6,7},{7,6},{8,9},{9,8},{10,11... | collective-permute-start | bytes 3145736 | tf_op jit(solution)/shard_map/ppermute | solution.py:395
  33.9 7.0 %copy-start.2 = (bf16[1024,512]{1,0:T(8,128)(2,1)}, bf16[1024,512]{1,0:T(8,128)(2,1)S(1)}, u32[]{:S(2)}) copy-start(bf16[1024,512]{1,0:T(8,128)(2,1)S(1)} %get-tuple-element.112) | copy-start | bytes 3145732
  33.9 8.7 %collective-permute-start.3 = (bf16[1024,512]{1,0:T(8,128)(2,1)}, bf16[1024,512]{1,0:T(8,128)(2,1)S(1)}, u32[]{:S(2)}, u32[]{:S(2)}) collective-permute-start(bf16[1024,512]{1,0:T(8,128)(2,1)} %get-tuple-element.85), channel_id=1, source_target_pairs={{0,1},{1,0},{2,3},{3,2},{4,5},{5,4},{6,7},{7,6},{8,9},{9,8},{10,11... | collective-permute-start | bytes 3145736 | tf_op jit(solution)/shard_map/ppermute | solution.py:395
  40.9 16.7 %collective-permute-start.4 = (bf16[512,512]{1,0:T(8,128)(2,1)}, bf16[512,512]{1,0:T(8,128)(2,1)}, u32[]{:S(2)}, u32[]{:S(2)}) collective-permute-start(bf16[512,512]{1,0:T(8,128)(2,1)} %get-tuple-element.96), channel_id=1, source_target_pairs={{0,2},{1,3},{2,0},{3,1},{4,6},{5,7},{6,4},{7,5},{8,10},{9,11},{10,... | collective-permute-start | bytes 1572872 | tf_op jit(solution)/shard_map/ppermute | solution.py:395
  57.6 4.4 %copy-start.1 = (bf16[256,1280]{1,0:T(8,128)(2,1)S(1)}, bf16[256,1280]{1,0:T(8,128)(2,1)}, u32[]{:S(2)}) copy-start(bf16[256,1280]{1,0:T(8,128)(2,1)} %copy-done) | copy-start | bytes 1966084
  57.6 4.4 %collective-permute-start.5 = (bf16[256,1280]{1,0:T(8,128)(2,1)}, bf16[256,1280]{1,0:T(8,128)(2,1)S(1)}, u32[]{:S(2)}, u32[]{:S(2)}) collective-permute-start(bf16[256,1280]{1,0:T(8,128)(2,1)} %get-tuple-element.97), channel_id=1, source_target_pairs={{0,1},{1,0},{2,3},{3,2},{4,5},{5,4},{6,7},{7,6},{8,9},{9,8},{10,11... | collective-permute-start | bytes 1966088 | tf_op jit(solution)/shard_map/ppermute | solution.py:395
  57.7 14.6 %collective-permute-start.7 = (bf16[512,512]{1,0:T(8,128)(2,1)}, bf16[512,512]{1,0:T(8,128)(2,1)}, u32[]{:S(2)}, u32[]{:S(2)}) collective-permute-start(bf16[512,512]{1,0:T(8,128)(2,1)} %get-tuple-element.98), channel_id=1, source_target_pairs={{0,2},{1,3},{2,0},{3,1},{4,6},{5,7},{6,4},{7,5},{8,10},{9,11},{10,... | collective-permute-start | bytes 1572872 | tf_op jit(solution)/shard_map/ppermute | solution.py:395
  60.2 8.7 %collective-permute-start.21 = (bf16[256,512]{1,0:T(8,128)(2,1)}, bf16[256,512]{1,0:T(8,128)(2,1)}, u32[]{:S(2)}, u32[]{:S(2)}) collective-permute-start(bf16[256,512]{1,0:T(8,128)(2,1)} %constant_dynamic-slice_fusion.1), channel_id=1, source_target_pairs={{0,8},{1,9},{2,10},{3,11},{4,12},{5,13},{6,14},{7,15},{8,0},{9,1},... | collective-permute-start | bytes 786440 | tf_op jit(solution)/shard_map/ppermute | solution.py:395
  62.1 18.1 %copy-start.7 = (bf16[512,512]{1,0:T(8,128)(2,1)S(1)}, bf16[512,512]{1,0:T(8,128)(2,1)}, u32[]{:S(2)}) copy-start(bf16[512,512]{1,0:T(8,128)(2,1)} %get-tuple-element.76) | copy-start | bytes 1572868
  62.1 10.1 %collective-permute-start.6 = (bf16[128,1280]{1,0:T(8,128)(2,1)S(1)}, bf16[128,1280]{1,0:T(8,128)(2,1)S(1)}, u32[]{:S(2)}, u32[]{:S(2)}) collective-permute-start(bf16[128,1280]{1,0:T(8,128)(2,1)S(1)} %get-tuple-element.129), channel_id=1, source_target_pairs={{0,4},{1,5},{2,6},{3,7},{4,0},{5,1},{6,2},{7,3},{8,12},{9,13},{10,... | collective-permute-start | bytes 983048 | tf_op jit(solution)/shard_map/ppermute | solution.py:395
  63.7 47.8 %collective-permute-start.20 = (bf16[1024,512]{1,0:T(8,128)(2,1)S(1)}, bf16[1024,512]{1,0:T(8,128)(2,1)S(1)}, u32[]{:S(2)}, u32[]{:S(2)}) collective-permute-start(bf16[1024,512]{1,0:T(8,128)(2,1)S(1)} %copy-done.3), channel_id=1, source_target_pairs={{0,1},{1,0},{2,3},{3,2},{4,5},{5,4},{6,7},{7,6},{8,9},{9,8},{10,11... | collective-permute-start | bytes 3145736 | tf_op jit(solution)/shard_map/ppermute | solution.py:395
  69.8 5.0 %collective-permute-start.22 = (bf16[128,512]{1,0:T(8,128)(2,1)S(1)}, bf16[128,512]{1,0:T(8,128)(2,1)S(1)}, u32[]{:S(2)}, u32[]{:S(2)}) collective-permute-start(bf16[128,512]{1,0:T(8,128)(2,1)S(1)} %add_convert_fusion.9), channel_id=1, source_target_pairs={{0,4},{1,5},{2,6},{3,7},{4,0},{5,1},{6,2},{7,3},{8,12},{9,13},{10,... | collective-permute-start | bytes 393224 | tf_op jit(solution)/shard_map/ppermute | solution.py:395
  72.3 6.3 %collective-permute-start.13 = (bf16[64,1280]{1,0:T(8,128)(2,1)S(1)}, bf16[64,1280]{1,0:T(8,128)(2,1)S(1)}, u32[]{:S(2)}, u32[]{:S(2)}) collective-permute-start(bf16[64,1280]{1,0:T(8,128)(2,1)S(1)} %get-tuple-element.131), channel_id=1, source_target_pairs={{0,2},{1,3},{2,0},{3,1},{4,6},{5,7},{6,4},{7,5},{8,10},{9,11},{10,... | collective-permute-start | bytes 491528 | tf_op jit(solution)/shard_map/ppermute | solution.py:395
  75.8 26.0 %collective-permute-start.23 = (bf16[128,512]{1,0:T(8,128)(2,1)S(1)}, bf16[128,512]{1,0:T(8,128)(2,1)S(1)}, u32[]{:S(2)}, u32[]{:S(2)}) collective-permute-start(bf16[128,512]{1,0:T(8,128)(2,1)S(1)} %add_convert_fusion.8), channel_id=1, source_target_pairs={{0,16},{1,17},{2,18},{3,19},{4,20},{5,21},{6,22},{7,23},{8,24},{9,... | collective-permute-start | bytes 393224 | tf_op jit(solution)/shard_map/ppermute | solution.py:395
  78.6 4.5 %collective-permute-start.14 = (bf16[32,1280]{1,0:T(8,128)(2,1)S(1)}, bf16[32,1280]{1,0:T(8,128)(2,1)S(1)}, u32[]{:S(2)}, u32[]{:S(2)}) collective-permute-start(bf16[32,1280]{1,0:T(8,128)(2,1)S(1)} %add_convert_fusion.17), channel_id=1, source_target_pairs={{0,8},{1,9},{2,10},{3,11},{4,12},{5,13},{6,14},{7,15},{8,0},{9,1},... | collective-permute-start | bytes 245768 | tf_op jit(solution)/shard_map/ppermute | solution.py:395
  83.2 5.4 %collective-permute-start.15 = (bf16[32,1280]{1,0:T(8,128)(2,1)S(1)}, bf16[32,1280]{1,0:T(8,128)(2,1)S(1)}, u32[]{:S(2)}, u32[]{:S(2)}) collective-permute-start(bf16[32,1280]{1,0:T(8,128)(2,1)S(1)} %add_convert_fusion.16), channel_id=1, source_target_pairs={{0,16},{1,17},{2,18},{3,19},{4,20},{5,21},{6,22},{7,23},{8,24},{9,... | collective-permute-start | bytes 245768 | tf_op jit(solution)/shard_map/ppermute | solution.py:395
  85.7 6.4 %collective-permute-start.8 = (bf16[256,512]{1,0:T(8,128)(2,1)S(1)}, bf16[256,512]{1,0:T(8,128)(2,1)S(1)}, u32[]{:S(2)}, u32[]{:S(2)}) collective-permute-start(bf16[256,512]{1,0:T(8,128)(2,1)S(1)} %constant_dynamic-slice_fusion), channel_id=1, source_target_pairs={{0,4},{1,5},{2,6},{3,7},{4,0},{5,1},{6,2},{7,3},{8,12},{9,13},{10,... | collective-permute-start | bytes 786440 | tf_op jit(solution)/shard_map/ppermute | solution.py:395
  88.6 6.1 %collective-permute-start.16 = (bf16[32,1280]{1,0:T(8,128)(2,1)S(1)}, bf16[32,1280]{1,0:T(8,128)(2,1)S(1)}, u32[]{:S(2)}, u32[]{:S(2)}) collective-permute-start(bf16[32,1280]{1,0:T(8,128)(2,1)S(1)} %add_convert_fusion.15), channel_id=1, source_target_pairs={{0,8},{1,9},{2,10},{3,11},{4,12},{5,13},{6,14},{7,15},{8,0},{9,1},... | collective-permute-start | bytes 245768 | tf_op jit(solution)/shard_map/ppermute | solution.py:395
  92.2 5.5 %collective-permute-start.9 = (bf16[128,512]{1,0:T(8,128)(2,1)S(1)}, bf16[128,512]{1,0:T(8,128)(2,1)S(1)}, u32[]{:S(2)}, u32[]{:S(2)}) collective-permute-start(bf16[128,512]{1,0:T(8,128)(2,1)S(1)} %add_convert_fusion.13), channel_id=1, source_target_pairs={{0,8},{1,9},{2,10},{3,11},{4,12},{5,13},{6,14},{7,15},{8,0},{9,1},... | collective-permute-start | bytes 393224 | tf_op jit(solution)/shard_map/ppermute | solution.py:395
  94.8 5.4 %collective-permute-start.17 = (bf16[64,1280]{1,0:T(8,128)(2,1)S(1)}, bf16[64,1280]{1,0:T(8,128)(2,1)S(1)}, u32[]{:S(2)}, u32[]{:S(2)}) collective-permute-start(bf16[64,1280]{1,0:T(8,128)(2,1)S(1)} %maximum_select_fusion.6), channel_id=1, source_target_pairs={{0,2},{1,3},{2,0},{3,1},{4,6},{5,7},{6,4},{7,5},{8,10},{9,11},{10,... | collective-permute-start | bytes 491528 | tf_op jit(solution)/shard_map/ppermute | solution.py:395
  97.8 6.0 %collective-permute-start.10 = (bf16[128,512]{1,0:T(8,128)(2,1)S(1)}, bf16[128,512]{1,0:T(8,128)(2,1)S(1)}, u32[]{:S(2)}, u32[]{:S(2)}) collective-permute-start(bf16[128,512]{1,0:T(8,128)(2,1)S(1)} %add_convert_fusion.12), channel_id=1, source_target_pairs={{0,16},{1,17},{2,18},{3,19},{4,20},{5,21},{6,22},{7,23},{8,24},{9,... | collective-permute-start | bytes 393224 | tf_op jit(solution)/shard_map/ppermute | solution.py:395
  100.2 11.3 %copy-start.5 = (bf16[1024,512]{1,0:T(8,128)(2,1)S(1)}, bf16[1024,512]{1,0:T(8,128)(2,1)}, u32[]{:S(2)}) copy-start(bf16[1024,512]{1,0:T(8,128)(2,1)} %get-tuple-element.88.res) | copy-start | bytes 3145732
  100.2 11.3 %copy-start.6 = (bf16[1024,512]{1,0:T(8,128)(2,1)S(1)}, bf16[1024,512]{1,0:T(8,128)(2,1)}, u32[]{:S(2)}) copy-start(bf16[1024,512]{1,0:T(8,128)(2,1)} %get-tuple-element.111) | copy-start | bytes 3145732
  100.2 7.1 %collective-permute-start.18 = (bf16[128,1280]{1,0:T(8,128)(2,1)S(1)}, bf16[128,1280]{1,0:T(8,128)(2,1)S(1)}, u32[]{:S(2)}, u32[]{:S(2)}) collective-permute-start(bf16[128,1280]{1,0:T(8,128)(2,1)S(1)} %maximum_select_fusion.3), channel_id=1, source_target_pairs={{0,4},{1,5},{2,6},{3,7},{4,0},{5,1},{6,2},{7,3},{8,12},{9,13},{10,... | collective-permute-start | bytes 983048 | tf_op jit(solution)/shard_map/ppermute | solution.py:395
  101.9 6.9 %collective-permute-start.24 = (bf16[128,512]{1,0:T(8,128)(2,1)S(1)}, bf16[128,512]{1,0:T(8,128)(2,1)S(1)}, u32[]{:S(2)}, u32[]{:S(2)}) collective-permute-start(bf16[128,512]{1,0:T(8,128)(2,1)S(1)} %add_convert_fusion.7), channel_id=1, source_target_pairs={{0,4},{1,5},{2,6},{3,7},{4,0},{5,1},{6,2},{7,3},{8,12},{9,13},{10,... | collective-permute-start | bytes 393224 | tf_op jit(solution)/shard_map/ppermute | solution.py:395
  103.8 6.6 %collective-permute-start.11 = (bf16[128,512]{1,0:T(8,128)(2,1)S(1)}, bf16[128,512]{1,0:T(8,128)(2,1)S(1)}, u32[]{:S(2)}, u32[]{:S(2)}) collective-permute-start(bf16[128,512]{1,0:T(8,128)(2,1)S(1)} %add_convert_fusion.11), channel_id=1, source_target_pairs={{0,8},{1,9},{2,10},{3,11},{4,12},{5,13},{6,14},{7,15},{8,0},{9,1},... | collective-permute-start | bytes 393224 | tf_op jit(solution)/shard_map/ppermute | solution.py:395
  107.5 10.1 %collective-permute-start.19 = (bf16[256,1280]{1,0:T(8,128)(2,1)S(1)}, bf16[256,1280]{1,0:T(8,128)(2,1)S(1)}, u32[]{:S(2)}, u32[]{:S(2)}) collective-permute-start(bf16[256,1280]{1,0:T(8,128)(2,1)S(1)} %maximum_select_fusion.mine), channel_id=1, source_target_pairs={{0,1},{1,0},{2,3},{3,2},{4,5},{5,4},{6,7},{7,6},{8,9},{9,8},{10,11... | collective-permute-start | bytes 1966088 | tf_op jit(solution)/shard_map/ppermute | solution.py:395
  108.9 7.6 %collective-permute-start.25 = (bf16[256,512]{1,0:T(8,128)(2,1)S(1)}, bf16[256,512]{1,0:T(8,128)(2,1)S(1)}, u32[]{:S(2)}, u32[]{:S(2)}) collective-permute-start(bf16[256,512]{1,0:T(8,128)(2,1)S(1)} %maximum_select_fusion.5), channel_id=1, source_target_pairs={{0,8},{1,9},{2,10},{3,11},{4,12},{5,13},{6,14},{7,15},{8,0},{9,1},... | collective-permute-start | bytes 786440 | tf_op jit(solution)/shard_map/ppermute | solution.py:395
  110.5 8.7 %collective-permute-start.12 = (bf16[256,512]{1,0:T(8,128)(2,1)S(1)}, bf16[256,512]{1,0:T(8,128)(2,1)S(1)}, u32[]{:S(2)}, u32[]{:S(2)}) collective-permute-start(bf16[256,512]{1,0:T(8,128)(2,1)S(1)} %maximum_select_fusion.4), channel_id=1, source_target_pairs={{0,4},{1,5},{2,6},{3,7},{4,0},{5,1},{6,2},{7,3},{8,12},{9,13},{10,... | collective-permute-start | bytes 786440 | tf_op jit(solution)/shard_map/ppermute | solution.py:395
  (3 other events, 9.4 us)

commit v5 on v4

--- a/solution.py
+++ b/solution.py
@@ -13,7 +13,7 @@
 epsilon = 1e-05
 AXES = ("dp", "mp")
 TILE = 128
-BIG = 256
+BIG = 512
 VMEM_LIMIT = 36 << 20
 LANES = 128
 VECTOR_ROW = 8

time: 121 us -> 120 us (level)
  transfers between devices with their start and end apart: 26 -> 26, of which waited for: 12 -> 13; matrix products, arithmetic and copies ran while one was open for 7% -> 7% of each run, Pallas kernels for 38% -> 38%
where the time goes in v5:
time: 120 us
  Pallas kernels  49.7 us (41%)
  starting transfers between devices  34.2 us (29%)
  waiting for transfers between devices  22.5 us (19%)
  other arithmetic  10.3 us (9%)
  local copies, waits for them, and re-layouts  2.3 us (2%)
    pallas_call x7, Pallas kernels, placed_call(): pl.pallas_call(kernel, out_shape=results, in_specs=[pl.BlockSpec(memory_s...  49.7 us
    ppermute x26, starting transfers between devices, swap(): return lax.ppermute(values, AXES, [(at, at ^ bit) for at in range(devices)])  34.2 us
    ppermute x26, waiting for transfers between devices, swap(): return lax.ppermute(values, AXES, [(at, at ^ bit) for at in range(devices)])  22.5 us
    convert_element_type x2, other arithmetic, sum_low(): functools.reduce(jnp.add, [part.astype(F32) for part in parts]).astype(BF16)  2.51 us
    convert_element_type x11, other arithmetic, add_low(): return (left.astype(F32) + right.astype(F32)).astype(BF16)  2.43 us
  transfers between devices with their start and end apart: 26, of which 13 were waited for; matrix products, arithmetic and copies ran while one was open for 7% of the time, Pallas kernels for 38%

profile of v5, /device:TPU:0, one launch (start us, length us, event | category | flops | bytes accessed | tf_op | source)
XLA Modules:
  0.0 119.9 jit_solution(18426683226441564731)
XLA Ops:
  2.6 3.0 %collective-permute-start.2 = (bf16[1040,512]{1,0:T(8,128)(2,1)S(1)}, bf16[1040,512]{1,0:T(8,128)(2,1)S(1)}, u32[]{:S(2)}, u32[]{:S(2)}) collective-permute-start(bf16[1040,512]{1,0:T(8,128)(2,1)S(1)} %fusion.3.refs_2_), channel_id=1, source_target_pairs={{0,2},{1,3},{2,0},{3,1},{4,6},{5,7},{6,4},{7,5},{8,10},{9,11},{10,... | collective-permute-start | bytes 3194888 | tf_op jit(solution)/shard_map/ppermute | solution.py:395
  5.6 10.5 %attend.1 = (bf16[1024,512]{1,0:T(8,128)(2,1)}, bf16[1024,512]{1,0:T(8,128)(2,1)S(1)}, bf16[1024,512]{1,0:T(8,128)(2,1)S(1)}, bf16[1024,512]{1,0:T(8,128)(2,1)},...) custom-call(s32[1,1024]{1,0:T(1,128)} %bitcast.15, ...), custom_call_target="tpu_custom_call" | custom-call | flops 1000 | bytes 1000 | tf_op jit(solution)/shard_map/attend/pallas_call | solution.py:382
  16.7 5.9 %ffn.4 = (bf16[1024,512]{1,0:T(8,128)(2,1)}, bf16[1024,512]{1,0:T(8,128)(2,1)}, bf16[512,512]{1,0:T(8,128)(2,1)}, bf16[512,512]{1,0:T(8,128)(2,1)}, f32[1,512]{1,0:T(1,128)S(1)}) custom-call(bf16[1024,512]{1,0:T(8,128)(2,1)S(1)} %get-tuple-element.71.refs_0_, bf16[1024,512]{1,0:T(8,128)(2,1)S(1)} %get-tuple-element.72.refs_1_.glow, bf16[1040,512]{1,0:T(8,128)(2,1)} %copy-done.4), custom_call_target="tpu_custom_call" | custom-call | flops 1000 | bytes 1000 | tf_op jit(solution)/shard_map/ffn/pallas_call | solution.py:382
  22.6 6.3 %ffn.5 = (bf16[1024,512]{1,0:T(8,128)(2,1)S(1)}, bf16[1024,512]{1,0:T(8,128)(2,1)S(1)}, bf16[512,512]{1,0:T(8,128)(2,1)}, bf16[512,512]{1,0:T(8,128)(2,1)}, f32[1,512]{1,0:T(1,128)S(1)}) custom-call(bf16[1024,512]{1,0:T(8,128)(2,1)S(1)} %collective-permute-done.refs_0_, bf16[1024,512]{1,0:T(8,128)(2,1)S(1)} %collective-permute-done.1.refs_1_, ...), custom_call_target="tpu_custom_call" | custom-call | flops 1000 | bytes 1000 | tf_op jit(solution)/shard_map/ffn/pallas_call | solution.py:382
  29.1 4.6 %ffn.6 = (bf16[1024,512]{1,0:T(8,128)(2,1)S(1)}, bf16[1024,512]{1,0:T(8,128)(2,1)}, bf16[512,512]{1,0:T(8,128)(2,1)}, bf16[512,512]{1,0:T(8,128)(2,1)}, f32[1,512]{1,0:T(1,128)S(1)}) custom-call(bf16[1024,512]{1,0:T(8,128)(2,1)S(1)} %collective-permute-done.refs_0_, bf16[1024,512]{1,0:T(8,128)(2,1)S(1)} %collective-permute-done.1.refs_1_, ...), custom_call_target="tpu_custom_call" | custom-call | flops 1000 | bytes 1000 | tf_op jit(solution)/shard_map/ffn/pallas_call | solution.py:382
  33.7 6.8 %ffn.7 = (bf16[1024,512]{1,0:T(8,128)(2,1)}, bf16[1024,512]{1,0:T(8,128)(2,1)S(1)}, bf16[512,512]{1,0:T(8,128)(2,1)}, bf16[512,512]{1,0:T(8,128)(2,1)}, f32[1,512]{1,0:T(1,128)S(1)}) custom-call(bf16[1024,512]{1,0:T(8,128)(2,1)S(1)} %get-tuple-element.71.refs_0_, bf16[1024,512]{1,0:T(8,128)(2,1)S(1)} %get-tuple-element.72.refs_1_.glow, ...), custom_call_target="tpu_custom_call" | custom-call | flops 1000 | bytes 1000 | tf_op jit(solution)/shard_map/ffn/pallas_call | solution.py:382
  40.6 1.7 %collective-permute-start.4 = (bf16[512,512]{1,0:T(8,128)(2,1)}, bf16[512,512]{1,0:T(8,128)(2,1)}, u32[]{:S(2)}, u32[]{:S(2)}) collective-permute-start(bf16[512,512]{1,0:T(8,128)(2,1)} %get-tuple-element.96), channel_id=1, source_target_pairs={{0,2},{1,3},{2,0},{3,1},{4,6},{5,7},{6,4},{7,5},{8,10},{9,11},{10,... | collective-permute-start | bytes 1572872 | tf_op jit(solution)/shard_map/ppermute | solution.py:395
  42.3 14.0 %back.1 = (bf16[1024,512]{1,0:T(8,128)(2,1)}, bf16[256,1280]{1,0:T(8,128)(2,1)S(1)}, bf16[256,1280]{1,0:T(8,128)(2,1)}) custom-call(s32[1]{0:T(128)} %bitcast.4.place, bf16[1024,512]{1,0:T(8,128)(2,1)S(1)} %get-tuple-element.84.second_own, bf16[1024,512]{1,0:T(8,128)(2,1)S(1)} %collective-permute-done.3.second_got, f32[1,512]{1,0:T(1,128)S(1)} %get-tuple-element.86.unit_own, ...), custom_call_target="tpu_custom_call" | custom-call | flops 1000 | bytes 1000 | tf_op jit(solution)/shard_map/back/pallas_call | solution.py:382
  57.6 1.3 %add_convert_fusion.1 = bf16[512,512]{1,0:T(8,128)(2,1)S(1)} fusion(bf16[512,512]{1,0:T(8,128)(2,1)} %collective-permute-done.4, bf16[512,512]{1,0:T(8,128)(2,1)} %get-tuple-element.125), kind=kLoop, calls=%fused_computation.7 | loop fusion | flops 1048576 | bytes 1572864 | tf_op jit(solution)/shard_map/convert_element_type | solution.py:467
  59.7 1.8 %collective-permute-start.21 = (bf16[256,512]{1,0:T(8,128)(2,1)}, bf16[256,512]{1,0:T(8,128)(2,1)}, u32[]{:S(2)}, u32[]{:S(2)}) collective-permute-start(bf16[256,512]{1,0:T(8,128)(2,1)} %constant_dynamic-slice_fusion.1), channel_id=1, source_target_pairs={{0,8},{1,9},{2,10},{3,11},{4,12},{5,13},{6,14},{7,15},{8,0},{9,1},... | collective-permute-start | bytes 786440 | tf_op jit(solution)/shard_map/ppermute | solution.py:395
  61.7 1.6 %collective-permute-start.6 = (bf16[128,1280]{1,0:T(8,128)(2,1)S(1)}, bf16[128,1280]{1,0:T(8,128)(2,1)S(1)}, u32[]{:S(2)}, u32[]{:S(2)}) collective-permute-start(bf16[128,1280]{1,0:T(8,128)(2,1)S(1)} %get-tuple-element.129), channel_id=1, source_target_pairs={{0,4},{1,5},{2,6},{3,7},{4,0},{5,1},{6,2},{7,3},{8,12},{9,13},{10,... | collective-permute-start | bytes 983048 | tf_op jit(solution)/shard_map/ppermute | solution.py:395
  63.3 5.0 %collective-permute-done.21 = bf16[256,512]{1,0:T(8,128)(2,1)} collective-permute-done((bf16[256,512]{1,0:T(8,128)(2,1)}, bf16[256,512]{1,0:T(8,128)(2,1)}, u32[]{:S(2)}, u32[]{:S(2)}) %collective-permute-start.21) | collective-permute-done | bytes 262176 | tf_op jit(solution)/shard_map/ppermute | solution.py:395
  69.3 1.7 %collective-permute-start.22 = (bf16[128,512]{1,0:T(8,128)(2,1)S(1)}, bf16[128,512]{1,0:T(8,128)(2,1)S(1)}, u32[]{:S(2)}, u32[]{:S(2)}) collective-permute-start(bf16[128,512]{1,0:T(8,128)(2,1)S(1)} %add_convert_fusion.9), channel_id=1, source_target_pairs={{0,4},{1,5},{2,6},{3,7},{4,0},{5,1},{6,2},{7,3},{8,12},{9,13},{10,... | collective-permute-start | bytes 393224 | tf_op jit(solution)/shard_map/ppermute | solution.py:395
  72.8 1.6 %collective-permute-done.22 = bf16[128,512]{1,0:T(8,128)(2,1)S(1)} collective-permute-done((bf16[128,512]{1,0:T(8,128)(2,1)S(1)}, bf16[128,512]{1,0:T(8,128)(2,1)S(1)}, u32[]{:S(2)}, u32[]{:S(2)}) %collective-permute-start.22) | collective-permute-done | bytes 131104 | tf_op jit(solution)/shard_map/ppermute | solution.py:395
  75.3 2.8 %collective-permute-start.23 = (bf16[128,512]{1,0:T(8,128)(2,1)S(1)}, bf16[128,512]{1,0:T(8,128)(2,1)S(1)}, u32[]{:S(2)}, u32[]{:S(2)}) collective-permute-start(bf16[128,512]{1,0:T(8,128)(2,1)S(1)} %add_convert_fusion.8), channel_id=1, source_target_pairs={{0,16},{1,17},{2,18},{3,19},{4,20},{5,21},{6,22},{7,23},{8,24},{9,... | collective-permute-start | bytes 393224 | tf_op jit(solution)/shard_map/ppermute | solution.py:395
  78.2 1.7 %collective-permute-start.14 = (bf16[32,1280]{1,0:T(8,128)(2,1)S(1)}, bf16[32,1280]{1,0:T(8,128)(2,1)S(1)}, u32[]{:S(2)}, u32[]{:S(2)}) collective-permute-start(bf16[32,1280]{1,0:T(8,128)(2,1)S(1)} %add_convert_fusion.17), channel_id=1, source_target_pairs={{0,8},{1,9},{2,10},{3,11},{4,12},{5,13},{6,14},{7,15},{8,0},{9,1},... | collective-permute-start | bytes 245768 | tf_op jit(solution)/shard_map/ppermute | solution.py:395
  81.0 1.7 %collective-permute-done.14 = bf16[32,1280]{1,0:T(8,128)(2,1)S(1)} collective-permute-done((bf16[32,1280]{1,0:T(8,128)(2,1)S(1)}, bf16[32,1280]{1,0:T(8,128)(2,1)S(1)}, u32[]{:S(2)}, u32[]{:S(2)}) %collective-permute-start.14) | collective-permute-done | bytes 81952 | tf_op jit(solution)/shard_map/ppermute | solution.py:395
  82.7 2.5 %collective-permute-start.15 = (bf16[32,1280]{1,0:T(8,128)(2,1)S(1)}, bf16[32,1280]{1,0:T(8,128)(2,1)S(1)}, u32[]{:S(2)}, u32[]{:S(2)}) collective-permute-start(bf16[32,1280]{1,0:T(8,128)(2,1)S(1)} %add_convert_fusion.16), channel_id=1, source_target_pairs={{0,16},{1,17},{2,18},{3,19},{4,20},{5,21},{6,22},{7,23},{8,24},{9,... | collective-permute-start | bytes 245768 | tf_op jit(solution)/shard_map/ppermute | solution.py:395
  85.2 1.6 %collective-permute-start.8 = (bf16[256,512]{1,0:T(8,128)(2,1)S(1)}, bf16[256,512]{1,0:T(8,128)(2,1)S(1)}, u32[]{:S(2)}, u32[]{:S(2)}) collective-permute-start(bf16[256,512]{1,0:T(8,128)(2,1)S(1)} %constant_dynamic-slice_fusion), channel_id=1, source_target_pairs={{0,4},{1,5},{2,6},{3,7},{4,0},{5,1},{6,2},{7,3},{8,12},{9,13},{10,... | collective-permute-start | bytes 786440 | tf_op jit(solution)/shard_map/ppermute | solution.py:395
  86.8 1.3 %collective-permute-done.15 = bf16[32,1280]{1,0:T(8,128)(2,1)S(1)} collective-permute-done((bf16[32,1280]{1,0:T(8,128)(2,1)S(1)}, bf16[32,1280]{1,0:T(8,128)(2,1)S(1)}, u32[]{:S(2)}, u32[]{:S(2)}) %collective-permute-start.15) | collective-permute-done | bytes 81952 | tf_op jit(solution)/shard_map/ppermute | solution.py:395
  88.1 2.1 %collective-permute-start.16 = (bf16[32,1280]{1,0:T(8,128)(2,1)S(1)}, bf16[32,1280]{1,0:T(8,128)(2,1)S(1)}, u32[]{:S(2)}, u32[]{:S(2)}) collective-permute-start(bf16[32,1280]{1,0:T(8,128)(2,1)S(1)} %add_convert_fusion.15), channel_id=1, source_target_pairs={{0,8},{1,9},{2,10},{3,11},{4,12},{5,13},{6,14},{7,15},{8,0},{9,1},... | collective-permute-start | bytes 245768 | tf_op jit(solution)/shard_map/ppermute | solution.py:395
  90.2 1.5 %collective-permute-done.8 = bf16[256,512]{1,0:T(8,128)(2,1)S(1)} collective-permute-done((bf16[256,512]{1,0:T(8,128)(2,1)S(1)}, bf16[256,512]{1,0:T(8,128)(2,1)S(1)}, u32[]{:S(2)}, u32[]{:S(2)}) %collective-permute-start.8) | collective-permute-done | bytes 262176 | tf_op jit(solution)/shard_map/ppermute | solution.py:395
  91.7 2.5 %collective-permute-start.9 = (bf16[128,512]{1,0:T(8,128)(2,1)S(1)}, bf16[128,512]{1,0:T(8,128)(2,1)S(1)}, u32[]{:S(2)}, u32[]{:S(2)}) collective-permute-start(bf16[128,512]{1,0:T(8,128)(2,1)S(1)} %add_convert_fusion.13), channel_id=1, source_target_pairs={{0,8},{1,9},{2,10},{3,11},{4,12},{5,13},{6,14},{7,15},{8,0},{9,1},... | collective-permute-start | bytes 393224 | tf_op jit(solution)/shard_map/ppermute | solution.py:395
  95.4 1.8 %collective-permute-done.9 = bf16[128,512]{1,0:T(8,128)(2,1)S(1)} collective-permute-done((bf16[128,512]{1,0:T(8,128)(2,1)S(1)}, bf16[128,512]{1,0:T(8,128)(2,1)S(1)}, u32[]{:S(2)}, u32[]{:S(2)}) %collective-permute-start.9) | collective-permute-done | bytes 131104 | tf_op jit(solution)/shard_map/ppermute | solution.py:395
  99.8 1.6 %collective-permute-start.18 = (bf16[128,1280]{1,0:T(8,128)(2,1)S(1)}, bf16[128,1280]{1,0:T(8,128)(2,1)S(1)}, u32[]{:S(2)}, u32[]{:S(2)}) collective-permute-start(bf16[128,1280]{1,0:T(8,128)(2,1)S(1)} %maximum_select_fusion.3), channel_id=1, source_target_pairs={{0,4},{1,5},{2,6},{3,7},{4,0},{5,1},{6,2},{7,3},{8,12},{9,13},{10,... | collective-permute-start | bytes 983048 | tf_op jit(solution)/shard_map/ppermute | solution.py:395
  102.0 1.3 %collective-permute-done.10 = bf16[128,512]{1,0:T(8,128)(2,1)S(1)} collective-permute-done((bf16[128,512]{1,0:T(8,128)(2,1)S(1)}, bf16[128,512]{1,0:T(8,128)(2,1)S(1)}, u32[]{:S(2)}, u32[]{:S(2)}) %collective-permute-start.10) | collective-permute-done | bytes 131104 | tf_op jit(solution)/shard_map/ppermute | solution.py:395
  103.4 2.1 %collective-permute-start.11 = (bf16[128,512]{1,0:T(8,128)(2,1)S(1)}, bf16[128,512]{1,0:T(8,128)(2,1)S(1)}, u32[]{:S(2)}, u32[]{:S(2)}) collective-permute-start(bf16[128,512]{1,0:T(8,128)(2,1)S(1)} %add_convert_fusion.11), channel_id=1, source_target_pairs={{0,8},{1,9},{2,10},{3,11},{4,12},{5,13},{6,14},{7,15},{8,0},{9,1},... | collective-permute-start | bytes 393224 | tf_op jit(solution)/shard_map/ppermute | solution.py:395
  105.5 1.4 %collective-permute-done.18 = bf16[128,1280]{1,0:T(8,128)(2,1)S(1)} collective-permute-done((bf16[128,1280]{1,0:T(8,128)(2,1)S(1)}, bf16[128,1280]{1,0:T(8,128)(2,1)S(1)}, u32[]{:S(2)}, u32[]{:S(2)}) %collective-permute-start.18) | collective-permute-done | bytes 327712 | tf_op jit(solution)/shard_map/ppermute | solution.py:395
  108.4 1.5 %collective-permute-start.25 = (bf16[256,512]{1,0:T(8,128)(2,1)S(1)}, bf16[256,512]{1,0:T(8,128)(2,1)S(1)}, u32[]{:S(2)}, u32[]{:S(2)}) collective-permute-start(bf16[256,512]{1,0:T(8,128)(2,1)S(1)} %maximum_select_fusion.5), channel_id=1, source_target_pairs={{0,8},{1,9},{2,10},{3,11},{4,12},{5,13},{6,14},{7,15},{8,0},{9,1},... | collective-permute-start | bytes 786440 | tf_op jit(solution)/shard_map/ppermute | solution.py:395
  111.1 1.4 %add_convert_fusion = bf16[1024,512]{1,0:T(8,128)(2,1)} fusion(bf16[1024,512]{1,0:T(8,128)(2,1)S(1)} %collective-permute-done.20, bf16[1024,512]{1,0:T(8,128)(2,1)S(1)} %copy-done.6, bf16[1024,512]{1,0:T(8,128)(2,1)S(1)} %copy-done.5, f32[512]{0:T(512)S(1)} %convert_element_type.227), kind=kLoop, calls=%fused_computation.4 | loop fusion | flops 3670016 | bytes 4196352 | tf_op jit(solution)/shard_map/convert_element_type | solution.py:619
  112.5 3.5 %collective-permute-done.25 = bf16[256,512]{1,0:T(8,128)(2,1)S(1)} collective-permute-done((bf16[256,512]{1,0:T(8,128)(2,1)S(1)}, bf16[256,512]{1,0:T(8,128)(2,1)S(1)}, u32[]{:S(2)}, u32[]{:S(2)}) %collective-permute-start.25) | collective-permute-done | bytes 262176 | tf_op jit(solution)/shard_map/ppermute | solution.py:395
  117.2 1.6 %unpack.1 = (f32[1,512]{1,0:T(1,128)}, f32[1,512]{1,0:T(1,128)}, f32[8,512]{1,0:T(8,128)}, f32[512,512]{1,0:T(8,128)}, f32[512,512]{1,0:T(8,128)}, /*index=5*/f3...) custom-call(s32[1]{0:T(128)} %bitcast.4.place, ...), custom_call_target="tpu_custom_call" | custom-call | flops 1000 | bytes 1000 | tf_op jit(solution)/shard_map/unpack/pallas_call | solution.py:382
  (71 shorter events, 19.1 us)
Async XLA Ops:
  2.6 13.5 %copy-start.4 = (bf16[1040,512]{1,0:T(8,128)(2,1)}, bf16[1040,512]{1,0:T(8,128)(2,1)S(1)}, u32[]{:S(2)}) copy-start(bf16[1040,512]{1,0:T(8,128)(2,1)S(1)} %fusion.3.refs_2_) | copy-start | bytes 3194884
  2.6 26.5 %collective-permute-start.2 = (bf16[1040,512]{1,0:T(8,128)(2,1)S(1)}, bf16[1040,512]{1,0:T(8,128)(2,1)S(1)}, u32[]{:S(2)}, u32[]{:S(2)}) collective-permute-start(bf16[1040,512]{1,0:T(8,128)(2,1)S(1)} %fusion.3.refs_2_), channel_id=1, source_target_pairs={{0,2},{1,3},{2,0},{3,1},{4,6},{5,7},{6,4},{7,5},{8,10},{9,11},{10,... | collective-permute-start | bytes 3194888 | tf_op jit(solution)/shard_map/ppermute | solution.py:395
  16.1 6.5 %collective-permute-start.1 = (bf16[1024,512]{1,0:T(8,128)(2,1)S(1)}, bf16[1024,512]{1,0:T(8,128)(2,1)S(1)}, u32[]{:S(2)}, u32[]{:S(2)}) collective-permute-start(bf16[1024,512]{1,0:T(8,128)(2,1)S(1)} %get-tuple-element.72.refs_1_.glow), channel_id=1, source_target_pairs={{0,1},{1,0},{2,3},{3,2},{4,5},{5,4},{6,7},{7,6},{8,9},{9,8},{10,11... | collective-permute-start | bytes 3145736 | tf_op jit(solution)/shard_map/ppermute | solution.py:395
  16.2 6.4 %collective-permute-start = (bf16[1024,512]{1,0:T(8,128)(2,1)S(1)}, bf16[1024,512]{1,0:T(8,128)(2,1)S(1)}, u32[]{:S(2)}, u32[]{:S(2)}) collective-permute-start(bf16[1024,512]{1,0:T(8,128)(2,1)S(1)} %get-tuple-element.71.refs_0_), channel_id=1, source_target_pairs={{0,1},{1,0},{2,3},{3,2},{4,5},{5,4},{6,7},{7,6},{8,9},{9,8},{10,11... | collective-permute-start | bytes 3145736 | tf_op jit(solution)/shard_map/ppermute | solution.py:395
  33.7 6.8 %copy-start.2 = (bf16[1024,512]{1,0:T(8,128)(2,1)}, bf16[1024,512]{1,0:T(8,128)(2,1)S(1)}, u32[]{:S(2)}) copy-start(bf16[1024,512]{1,0:T(8,128)(2,1)S(1)} %get-tuple-element.112) | copy-start | bytes 3145732
  33.7 8.6 %collective-permute-start.3 = (bf16[1024,512]{1,0:T(8,128)(2,1)}, bf16[1024,512]{1,0:T(8,128)(2,1)S(1)}, u32[]{:S(2)}, u32[]{:S(2)}) collective-permute-start(bf16[1024,512]{1,0:T(8,128)(2,1)} %get-tuple-element.85), channel_id=1, source_target_pairs={{0,1},{1,0},{2,3},{3,2},{4,5},{5,4},{6,7},{7,6},{8,9},{9,8},{10,11... | collective-permute-start | bytes 3145736 | tf_op jit(solution)/shard_map/ppermute | solution.py:395
  40.6 16.6 %collective-permute-start.4 = (bf16[512,512]{1,0:T(8,128)(2,1)}, bf16[512,512]{1,0:T(8,128)(2,1)}, u32[]{:S(2)}, u32[]{:S(2)}) collective-permute-start(bf16[512,512]{1,0:T(8,128)(2,1)} %get-tuple-element.96), channel_id=1, source_target_pairs={{0,2},{1,3},{2,0},{3,1},{4,6},{5,7},{6,4},{7,5},{8,10},{9,11},{10,... | collective-permute-start | bytes 1572872 | tf_op jit(solution)/shard_map/ppermute | solution.py:395
  57.1 4.4 %copy-start.1 = (bf16[256,1280]{1,0:T(8,128)(2,1)S(1)}, bf16[256,1280]{1,0:T(8,128)(2,1)}, u32[]{:S(2)}) copy-start(bf16[256,1280]{1,0:T(8,128)(2,1)} %copy-done) | copy-start | bytes 1966084
  57.1 4.4 %collective-permute-start.5 = (bf16[256,1280]{1,0:T(8,128)(2,1)}, bf16[256,1280]{1,0:T(8,128)(2,1)S(1)}, u32[]{:S(2)}, u32[]{:S(2)}) collective-permute-start(bf16[256,1280]{1,0:T(8,128)(2,1)} %get-tuple-element.97), channel_id=1, source_target_pairs={{0,1},{1,0},{2,3},{3,2},{4,5},{5,4},{6,7},{7,6},{8,9},{9,8},{10,11... | collective-permute-start | bytes 1966088 | tf_op jit(solution)/shard_map/ppermute | solution.py:395
  57.2 14.6 %collective-permute-start.7 = (bf16[512,512]{1,0:T(8,128)(2,1)}, bf16[512,512]{1,0:T(8,128)(2,1)}, u32[]{:S(2)}, u32[]{:S(2)}) collective-permute-start(bf16[512,512]{1,0:T(8,128)(2,1)} %get-tuple-element.98), channel_id=1, source_target_pairs={{0,2},{1,3},{2,0},{3,1},{4,6},{5,7},{6,4},{7,5},{8,10},{9,11},{10,... | collective-permute-start | bytes 1572872 | tf_op jit(solution)/shard_map/ppermute | solution.py:395
  59.7 8.7 %collective-permute-start.21 = (bf16[256,512]{1,0:T(8,128)(2,1)}, bf16[256,512]{1,0:T(8,128)(2,1)}, u32[]{:S(2)}, u32[]{:S(2)}) collective-permute-start(bf16[256,512]{1,0:T(8,128)(2,1)} %constant_dynamic-slice_fusion.1), channel_id=1, source_target_pairs={{0,8},{1,9},{2,10},{3,11},{4,12},{5,13},{6,14},{7,15},{8,0},{9,1},... | collective-permute-start | bytes 786440 | tf_op jit(solution)/shard_map/ppermute | solution.py:395
  61.7 18.2 %copy-start.7 = (bf16[512,512]{1,0:T(8,128)(2,1)S(1)}, bf16[512,512]{1,0:T(8,128)(2,1)}, u32[]{:S(2)}) copy-start(bf16[512,512]{1,0:T(8,128)(2,1)} %get-tuple-element.76) | copy-start | bytes 1572868
  61.7 10.1 %collective-permute-start.6 = (bf16[128,1280]{1,0:T(8,128)(2,1)S(1)}, bf16[128,1280]{1,0:T(8,128)(2,1)S(1)}, u32[]{:S(2)}, u32[]{:S(2)}) collective-permute-start(bf16[128,1280]{1,0:T(8,128)(2,1)S(1)} %get-tuple-element.129), channel_id=1, source_target_pairs={{0,4},{1,5},{2,6},{3,7},{4,0},{5,1},{6,2},{7,3},{8,12},{9,13},{10,... | collective-permute-start | bytes 983048 | tf_op jit(solution)/shard_map/ppermute | solution.py:395
  63.3 47.8 %collective-permute-start.20 = (bf16[1024,512]{1,0:T(8,128)(2,1)S(1)}, bf16[1024,512]{1,0:T(8,128)(2,1)S(1)}, u32[]{:S(2)}, u32[]{:S(2)}) collective-permute-start(bf16[1024,512]{1,0:T(8,128)(2,1)S(1)} %copy-done.3), channel_id=1, source_target_pairs={{0,1},{1,0},{2,3},{3,2},{4,5},{5,4},{6,7},{7,6},{8,9},{9,8},{10,11... | collective-permute-start | bytes 3145736 | tf_op jit(solution)/shard_map/ppermute | solution.py:395
  69.3 5.0 %collective-permute-start.22 = (bf16[128,512]{1,0:T(8,128)(2,1)S(1)}, bf16[128,512]{1,0:T(8,128)(2,1)S(1)}, u32[]{:S(2)}, u32[]{:S(2)}) collective-permute-start(bf16[128,512]{1,0:T(8,128)(2,1)S(1)} %add_convert_fusion.9), channel_id=1, source_target_pairs={{0,4},{1,5},{2,6},{3,7},{4,0},{5,1},{6,2},{7,3},{8,12},{9,13},{10,... | collective-permute-start | bytes 393224 | tf_op jit(solution)/shard_map/ppermute | solution.py:395
  71.9 6.3 %collective-permute-start.13 = (bf16[64,1280]{1,0:T(8,128)(2,1)S(1)}, bf16[64,1280]{1,0:T(8,128)(2,1)S(1)}, u32[]{:S(2)}, u32[]{:S(2)}) collective-permute-start(bf16[64,1280]{1,0:T(8,128)(2,1)S(1)} %get-tuple-element.131), channel_id=1, source_target_pairs={{0,2},{1,3},{2,0},{3,1},{4,6},{5,7},{6,4},{7,5},{8,10},{9,11},{10,... | collective-permute-start | bytes 491528 | tf_op jit(solution)/shard_map/ppermute | solution.py:395
  75.3 26.1 %collective-permute-start.23 = (bf16[128,512]{1,0:T(8,128)(2,1)S(1)}, bf16[128,512]{1,0:T(8,128)(2,1)S(1)}, u32[]{:S(2)}, u32[]{:S(2)}) collective-permute-start(bf16[128,512]{1,0:T(8,128)(2,1)S(1)} %add_convert_fusion.8), channel_id=1, source_target_pairs={{0,16},{1,17},{2,18},{3,19},{4,20},{5,21},{6,22},{7,23},{8,24},{9,... | collective-permute-start | bytes 393224 | tf_op jit(solution)/shard_map/ppermute | solution.py:395
  78.2 4.5 %collective-permute-start.14 = (bf16[32,1280]{1,0:T(8,128)(2,1)S(1)}, bf16[32,1280]{1,0:T(8,128)(2,1)S(1)}, u32[]{:S(2)}, u32[]{:S(2)}) collective-permute-start(bf16[32,1280]{1,0:T(8,128)(2,1)S(1)} %add_convert_fusion.17), channel_id=1, source_target_pairs={{0,8},{1,9},{2,10},{3,11},{4,12},{5,13},{6,14},{7,15},{8,0},{9,1},... | collective-permute-start | bytes 245768 | tf_op jit(solution)/shard_map/ppermute | solution.py:395
  82.7 5.4 %collective-permute-start.15 = (bf16[32,1280]{1,0:T(8,128)(2,1)S(1)}, bf16[32,1280]{1,0:T(8,128)(2,1)S(1)}, u32[]{:S(2)}, u32[]{:S(2)}) collective-permute-start(bf16[32,1280]{1,0:T(8,128)(2,1)S(1)} %add_convert_fusion.16), channel_id=1, source_target_pairs={{0,16},{1,17},{2,18},{3,19},{4,20},{5,21},{6,22},{7,23},{8,24},{9,... | collective-permute-start | bytes 245768 | tf_op jit(solution)/shard_map/ppermute | solution.py:395
  85.2 6.4 %collective-permute-start.8 = (bf16[256,512]{1,0:T(8,128)(2,1)S(1)}, bf16[256,512]{1,0:T(8,128)(2,1)S(1)}, u32[]{:S(2)}, u32[]{:S(2)}) collective-permute-start(bf16[256,512]{1,0:T(8,128)(2,1)S(1)} %constant_dynamic-slice_fusion), channel_id=1, source_target_pairs={{0,4},{1,5},{2,6},{3,7},{4,0},{5,1},{6,2},{7,3},{8,12},{9,13},{10,... | collective-permute-start | bytes 786440 | tf_op jit(solution)/shard_map/ppermute | solution.py:395
  88.1 6.1 %collective-permute-start.16 = (bf16[32,1280]{1,0:T(8,128)(2,1)S(1)}, bf16[32,1280]{1,0:T(8,128)(2,1)S(1)}, u32[]{:S(2)}, u32[]{:S(2)}) collective-permute-start(bf16[32,1280]{1,0:T(8,128)(2,1)S(1)} %add_convert_fusion.15), channel_id=1, source_target_pairs={{0,8},{1,9},{2,10},{3,11},{4,12},{5,13},{6,14},{7,15},{8,0},{9,1},... | collective-permute-start | bytes 245768 | tf_op jit(solution)/shard_map/ppermute | solution.py:395
  91.7 5.5 %collective-permute-start.9 = (bf16[128,512]{1,0:T(8,128)(2,1)S(1)}, bf16[128,512]{1,0:T(8,128)(2,1)S(1)}, u32[]{:S(2)}, u32[]{:S(2)}) collective-permute-start(bf16[128,512]{1,0:T(8,128)(2,1)S(1)} %add_convert_fusion.13), channel_id=1, source_target_pairs={{0,8},{1,9},{2,10},{3,11},{4,12},{5,13},{6,14},{7,15},{8,0},{9,1},... | collective-permute-start | bytes 393224 | tf_op jit(solution)/shard_map/ppermute | solution.py:395
  94.3 5.4 %collective-permute-start.17 = (bf16[64,1280]{1,0:T(8,128)(2,1)S(1)}, bf16[64,1280]{1,0:T(8,128)(2,1)S(1)}, u32[]{:S(2)}, u32[]{:S(2)}) collective-permute-start(bf16[64,1280]{1,0:T(8,128)(2,1)S(1)} %maximum_select_fusion.6), channel_id=1, source_target_pairs={{0,2},{1,3},{2,0},{3,1},{4,6},{5,7},{6,4},{7,5},{8,10},{9,11},{10,... | collective-permute-start | bytes 491528 | tf_op jit(solution)/shard_map/ppermute | solution.py:395
  97.3 6.0 %collective-permute-start.10 = (bf16[128,512]{1,0:T(8,128)(2,1)S(1)}, bf16[128,512]{1,0:T(8,128)(2,1)S(1)}, u32[]{:S(2)}, u32[]{:S(2)}) collective-permute-start(bf16[128,512]{1,0:T(8,128)(2,1)S(1)} %add_convert_fusion.12), channel_id=1, source_target_pairs={{0,16},{1,17},{2,18},{3,19},{4,20},{5,21},{6,22},{7,23},{8,24},{9,... | collective-permute-start | bytes 393224 | tf_op jit(solution)/shard_map/ppermute | solution.py:395
  99.8 11.3 %copy-start.5 = (bf16[1024,512]{1,0:T(8,128)(2,1)S(1)}, bf16[1024,512]{1,0:T(8,128)(2,1)}, u32[]{:S(2)}) copy-start(bf16[1024,512]{1,0:T(8,128)(2,1)} %get-tuple-element.88.res) | copy-start | bytes 3145732
  99.8 11.3 %copy-start.6 = (bf16[1024,512]{1,0:T(8,128)(2,1)S(1)}, bf16[1024,512]{1,0:T(8,128)(2,1)}, u32[]{:S(2)}) copy-start(bf16[1024,512]{1,0:T(8,128)(2,1)} %get-tuple-element.111) | copy-start | bytes 3145732
  99.8 7.1 %collective-permute-start.18 = (bf16[128,1280]{1,0:T(8,128)(2,1)S(1)}, bf16[128,1280]{1,0:T(8,128)(2,1)S(1)}, u32[]{:S(2)}, u32[]{:S(2)}) collective-permute-start(bf16[128,1280]{1,0:T(8,128)(2,1)S(1)} %maximum_select_fusion.3), channel_id=1, source_target_pairs={{0,4},{1,5},{2,6},{3,7},{4,0},{5,1},{6,2},{7,3},{8,12},{9,13},{10,... | collective-permute-start | bytes 983048 | tf_op jit(solution)/shard_map/ppermute | solution.py:395
  101.4 6.9 %collective-permute-start.24 = (bf16[128,512]{1,0:T(8,128)(2,1)S(1)}, bf16[128,512]{1,0:T(8,128)(2,1)S(1)}, u32[]{:S(2)}, u32[]{:S(2)}) collective-permute-start(bf16[128,512]{1,0:T(8,128)(2,1)S(1)} %add_convert_fusion.7), channel_id=1, source_target_pairs={{0,4},{1,5},{2,6},{3,7},{4,0},{5,1},{6,2},{7,3},{8,12},{9,13},{10,... | collective-permute-start | bytes 393224 | tf_op jit(solution)/shard_map/ppermute | solution.py:395
  103.4 6.6 %collective-permute-start.11 = (bf16[128,512]{1,0:T(8,128)(2,1)S(1)}, bf16[128,512]{1,0:T(8,128)(2,1)S(1)}, u32[]{:S(2)}, u32[]{:S(2)}) collective-permute-start(bf16[128,512]{1,0:T(8,128)(2,1)S(1)} %add_convert_fusion.11), channel_id=1, source_target_pairs={{0,8},{1,9},{2,10},{3,11},{4,12},{5,13},{6,14},{7,15},{8,0},{9,1},... | collective-permute-start | bytes 393224 | tf_op jit(solution)/shard_map/ppermute | solution.py:395
  107.1 10.1 %collective-permute-start.19 = (bf16[256,1280]{1,0:T(8,128)(2,1)S(1)}, bf16[256,1280]{1,0:T(8,128)(2,1)S(1)}, u32[]{:S(2)}, u32[]{:S(2)}) collective-permute-start(bf16[256,1280]{1,0:T(8,128)(2,1)S(1)} %maximum_select_fusion.mine), channel_id=1, source_target_pairs={{0,1},{1,0},{2,3},{3,2},{4,5},{5,4},{6,7},{7,6},{8,9},{9,8},{10,11... | collective-permute-start | bytes 1966088 | tf_op jit(solution)/shard_map/ppermute | solution.py:395
  108.4 7.6 %collective-permute-start.25 = (bf16[256,512]{1,0:T(8,128)(2,1)S(1)}, bf16[256,512]{1,0:T(8,128)(2,1)S(1)}, u32[]{:S(2)}, u32[]{:S(2)}) collective-permute-start(bf16[256,512]{1,0:T(8,128)(2,1)S(1)} %maximum_select_fusion.5), channel_id=1, source_target_pairs={{0,8},{1,9},{2,10},{3,11},{4,12},{5,13},{6,14},{7,15},{8,0},{9,1},... | collective-permute-start | bytes 786440 | tf_op jit(solution)/shard_map/ppermute | solution.py:395
  110.0 8.8 %collective-permute-start.12 = (bf16[256,512]{1,0:T(8,128)(2,1)S(1)}, bf16[256,512]{1,0:T(8,128)(2,1)S(1)}, u32[]{:S(2)}, u32[]{:S(2)}) collective-permute-start(bf16[256,512]{1,0:T(8,128)(2,1)S(1)} %maximum_select_fusion.4), channel_id=1, source_target_pairs={{0,4},{1,5},{2,6},{3,7},{4,0},{5,1},{6,2},{7,3},{8,12},{9,13},{10,... | collective-permute-start | bytes 786440 | tf_op jit(solution)/shard_map/ppermute | solution.py:395
  (3 other events, 9.5 us)

commit v6 on v5

--- a/solution.py
+++ b/solution.py
@@ -260,8 +260,10 @@
         bias_sum += row_sum(outer)
         grad = outer + norm_back(second, gain_two, hat, inverse)
         grad_res[span, :] = grad
-        grad_mixed[span, :] = dot_nt(grad.astype(BF16), wo[...])
-    packed[:, width : 2 * width] = dot_tn(mixed[...], grad_res[...].astype(BF16)).astype(BF16)
+        low_grad = grad.astype(BF16)
+        low1[span, :] = low_grad
+        grad_mixed[span, :] = dot_nt(low_grad, wo[...])
+    packed[:, width : 2 * width] = dot_tn(mixed[...], low1[...]).astype(BF16)
     key_sum[...] = jnp.zeros_like(key_sum)
     value_sum[...] = jnp.zeros_like(value_sum)
     for tile in range(tiles):

time: 120 us -> 120 us (level)
  no operation moved by 1% of the time
where the time goes in v6:
time: 120 us
  Pallas kernels  49.7 us (41%)
  starting transfers between devices  34.2 us (29%)
  waiting for transfers between devices  22.5 us (19%)
  other arithmetic  10.3 us (9%)
  local copies, waits for them, and re-layouts  2.3 us (2%)
    pallas_call x7, Pallas kernels, placed_call(): pl.pallas_call(kernel, out_shape=results, in_specs=[pl.BlockSpec(memory_s...  49.7 us
    ppermute x26, starting transfers between devices, swap(): return lax.ppermute(values, AXES, [(at, at ^ bit) for at in range(devices)])  34.2 us
    ppermute x26, waiting for transfers between devices, swap(): return lax.ppermute(values, AXES, [(at, at ^ bit) for at in range(devices)])  22.5 us
    convert_element_type x2, other arithmetic, sum_low(): functools.reduce(jnp.add, [part.astype(F32) for part in parts]).astype(BF16)  2.51 us
    convert_element_type x11, other arithmetic, add_low(): return (left.astype(F32) + right.astype(F32)).astype(BF16)  2.43 us
  transfers between devices with their start and end apart: 26, of which 13 were waited for; matrix products, arithmetic and copies ran while one was open for 7% of the time, Pallas kernels for 38%

profile of v6, /device:TPU:0, one launch (start us, length us, event | category | flops | bytes accessed | tf_op | source)
XLA Modules:
  0.0 119.9 jit_solution(18426683226441564731)
XLA Ops:
  2.6 3.0 %collective-permute-start.2 = (bf16[1040,512]{1,0:T(8,128)(2,1)S(1)}, bf16[1040,512]{1,0:T(8,128)(2,1)S(1)}, u32[]{:S(2)}, u32[]{:S(2)}) collective-permute-start(bf16[1040,512]{1,0:T(8,128)(2,1)S(1)} %fusion.3.refs_2_), channel_id=1, source_target_pairs={{0,2},{1,3},{2,0},{3,1},{4,6},{5,7},{6,4},{7,5},{8,10},{9,11},{10,... | collective-permute-start | bytes 3194888 | tf_op jit(solution)/shard_map/ppermute | solution.py:397
  5.6 10.5 %attend.1 = (bf16[1024,512]{1,0:T(8,128)(2,1)}, bf16[1024,512]{1,0:T(8,128)(2,1)S(1)}, bf16[1024,512]{1,0:T(8,128)(2,1)S(1)}, bf16[1024,512]{1,0:T(8,128)(2,1)},...) custom-call(s32[1,1024]{1,0:T(1,128)} %bitcast.15, ...), custom_call_target="tpu_custom_call" | custom-call | flops 1000 | bytes 1000 | tf_op jit(solution)/shard_map/attend/pallas_call | solution.py:384
  16.7 5.9 %ffn.4 = (bf16[1024,512]{1,0:T(8,128)(2,1)}, bf16[1024,512]{1,0:T(8,128)(2,1)}, bf16[512,512]{1,0:T(8,128)(2,1)}, bf16[512,512]{1,0:T(8,128)(2,1)}, f32[1,512]{1,0:T(1,128)S(1)}) custom-call(bf16[1024,512]{1,0:T(8,128)(2,1)S(1)} %get-tuple-element.71.refs_0_, bf16[1024,512]{1,0:T(8,128)(2,1)S(1)} %get-tuple-element.72.refs_1_.glow, bf16[1040,512]{1,0:T(8,128)(2,1)} %copy-done.4), custom_call_target="tpu_custom_call" | custom-call | flops 1000 | bytes 1000 | tf_op jit(solution)/shard_map/ffn/pallas_call | solution.py:384
  22.6 6.3 %ffn.5 = (bf16[1024,512]{1,0:T(8,128)(2,1)S(1)}, bf16[1024,512]{1,0:T(8,128)(2,1)S(1)}, bf16[512,512]{1,0:T(8,128)(2,1)}, bf16[512,512]{1,0:T(8,128)(2,1)}, f32[1,512]{1,0:T(1,128)S(1)}) custom-call(bf16[1024,512]{1,0:T(8,128)(2,1)S(1)} %collective-permute-done.refs_0_, bf16[1024,512]{1,0:T(8,128)(2,1)S(1)} %collective-permute-done.1.refs_1_, ...), custom_call_target="tpu_custom_call" | custom-call | flops 1000 | bytes 1000 | tf_op jit(solution)/shard_map/ffn/pallas_call | solution.py:384
  29.1 4.6 %ffn.6 = (bf16[1024,512]{1,0:T(8,128)(2,1)S(1)}, bf16[1024,512]{1,0:T(8,128)(2,1)}, bf16[512,512]{1,0:T(8,128)(2,1)}, bf16[512,512]{1,0:T(8,128)(2,1)}, f32[1,512]{1,0:T(1,128)S(1)}) custom-call(bf16[1024,512]{1,0:T(8,128)(2,1)S(1)} %collective-permute-done.refs_0_, bf16[1024,512]{1,0:T(8,128)(2,1)S(1)} %collective-permute-done.1.refs_1_, ...), custom_call_target="tpu_custom_call" | custom-call | flops 1000 | bytes 1000 | tf_op jit(solution)/shard_map/ffn/pallas_call | solution.py:384
  33.7 6.8 %ffn.7 = (bf16[1024,512]{1,0:T(8,128)(2,1)}, bf16[1024,512]{1,0:T(8,128)(2,1)S(1)}, bf16[512,512]{1,0:T(8,128)(2,1)}, bf16[512,512]{1,0:T(8,128)(2,1)}, f32[1,512]{1,0:T(1,128)S(1)}) custom-call(bf16[1024,512]{1,0:T(8,128)(2,1)S(1)} %get-tuple-element.71.refs_0_, bf16[1024,512]{1,0:T(8,128)(2,1)S(1)} %get-tuple-element.72.refs_1_.glow, ...), custom_call_target="tpu_custom_call" | custom-call | flops 1000 | bytes 1000 | tf_op jit(solution)/shard_map/ffn/pallas_call | solution.py:384
  40.6 1.7 %collective-permute-start.4 = (bf16[512,512]{1,0:T(8,128)(2,1)}, bf16[512,512]{1,0:T(8,128)(2,1)}, u32[]{:S(2)}, u32[]{:S(2)}) collective-permute-start(bf16[512,512]{1,0:T(8,128)(2,1)} %get-tuple-element.96), channel_id=1, source_target_pairs={{0,2},{1,3},{2,0},{3,1},{4,6},{5,7},{6,4},{7,5},{8,10},{9,11},{10,... | collective-permute-start | bytes 1572872 | tf_op jit(solution)/shard_map/ppermute | solution.py:397
  42.3 14.0 %back.1 = (bf16[1024,512]{1,0:T(8,128)(2,1)}, bf16[256,1280]{1,0:T(8,128)(2,1)S(1)}, bf16[256,1280]{1,0:T(8,128)(2,1)}) custom-call(s32[1]{0:T(128)} %bitcast.4.place, bf16[1024,512]{1,0:T(8,128)(2,1)S(1)} %get-tuple-element.84.second_own, bf16[1024,512]{1,0:T(8,128)(2,1)S(1)} %collective-permute-done.3.second_got, f32[1,512]{1,0:T(1,128)S(1)} %get-tuple-element.86.unit_own, ...), custom_call_target="tpu_custom_call" | custom-call | flops 1000 | bytes 1000 | tf_op jit(solution)/shard_map/back/pallas_call | solution.py:384
  57.6 1.3 %add_convert_fusion.1 = bf16[512,512]{1,0:T(8,128)(2,1)S(1)} fusion(bf16[512,512]{1,0:T(8,128)(2,1)} %collective-permute-done.4, bf16[512,512]{1,0:T(8,128)(2,1)} %get-tuple-element.125), kind=kLoop, calls=%fused_computation.7 | loop fusion | flops 1048576 | bytes 1572864 | tf_op jit(solution)/shard_map/convert_element_type | solution.py:469
  59.7 1.8 %collective-permute-start.21 = (bf16[256,512]{1,0:T(8,128)(2,1)}, bf16[256,512]{1,0:T(8,128)(2,1)}, u32[]{:S(2)}, u32[]{:S(2)}) collective-permute-start(bf16[256,512]{1,0:T(8,128)(2,1)} %constant_dynamic-slice_fusion.1), channel_id=1, source_target_pairs={{0,8},{1,9},{2,10},{3,11},{4,12},{5,13},{6,14},{7,15},{8,0},{9,1},... | collective-permute-start | bytes 786440 | tf_op jit(solution)/shard_map/ppermute | solution.py:397
  61.7 1.6 %collective-permute-start.6 = (bf16[128,1280]{1,0:T(8,128)(2,1)S(1)}, bf16[128,1280]{1,0:T(8,128)(2,1)S(1)}, u32[]{:S(2)}, u32[]{:S(2)}) collective-permute-start(bf16[128,1280]{1,0:T(8,128)(2,1)S(1)} %get-tuple-element.129), channel_id=1, source_target_pairs={{0,4},{1,5},{2,6},{3,7},{4,0},{5,1},{6,2},{7,3},{8,12},{9,13},{10,... | collective-permute-start | bytes 983048 | tf_op jit(solution)/shard_map/ppermute | solution.py:397
  63.3 5.0 %collective-permute-done.21 = bf16[256,512]{1,0:T(8,128)(2,1)} collective-permute-done((bf16[256,512]{1,0:T(8,128)(2,1)}, bf16[256,512]{1,0:T(8,128)(2,1)}, u32[]{:S(2)}, u32[]{:S(2)}) %collective-permute-start.21) | collective-permute-done | bytes 262176 | tf_op jit(solution)/shard_map/ppermute | solution.py:397
  69.3 1.7 %collective-permute-start.22 = (bf16[128,512]{1,0:T(8,128)(2,1)S(1)}, bf16[128,512]{1,0:T(8,128)(2,1)S(1)}, u32[]{:S(2)}, u32[]{:S(2)}) collective-permute-start(bf16[128,512]{1,0:T(8,128)(2,1)S(1)} %add_convert_fusion.9), channel_id=1, source_target_pairs={{0,4},{1,5},{2,6},{3,7},{4,0},{5,1},{6,2},{7,3},{8,12},{9,13},{10,... | collective-permute-start | bytes 393224 | tf_op jit(solution)/shard_map/ppermute | solution.py:397
  72.8 1.6 %collective-permute-done.22 = bf16[128,512]{1,0:T(8,128)(2,1)S(1)} collective-permute-done((bf16[128,512]{1,0:T(8,128)(2,1)S(1)}, bf16[128,512]{1,0:T(8,128)(2,1)S(1)}, u32[]{:S(2)}, u32[]{:S(2)}) %collective-permute-start.22) | collective-permute-done | bytes 131104 | tf_op jit(solution)/shard_map/ppermute | solution.py:397
  75.3 2.8 %collective-permute-start.23 = (bf16[128,512]{1,0:T(8,128)(2,1)S(1)}, bf16[128,512]{1,0:T(8,128)(2,1)S(1)}, u32[]{:S(2)}, u32[]{:S(2)}) collective-permute-start(bf16[128,512]{1,0:T(8,128)(2,1)S(1)} %add_convert_fusion.8), channel_id=1, source_target_pairs={{0,16},{1,17},{2,18},{3,19},{4,20},{5,21},{6,22},{7,23},{8,24},{9,... | collective-permute-start | bytes 393224 | tf_op jit(solution)/shard_map/ppermute | solution.py:397
  78.2 1.7 %collective-permute-start.14 = (bf16[32,1280]{1,0:T(8,128)(2,1)S(1)}, bf16[32,1280]{1,0:T(8,128)(2,1)S(1)}, u32[]{:S(2)}, u32[]{:S(2)}) collective-permute-start(bf16[32,1280]{1,0:T(8,128)(2,1)S(1)} %add_convert_fusion.17), channel_id=1, source_target_pairs={{0,8},{1,9},{2,10},{3,11},{4,12},{5,13},{6,14},{7,15},{8,0},{9,1},... | collective-permute-start | bytes 245768 | tf_op jit(solution)/shard_map/ppermute | solution.py:397
  81.0 1.7 %collective-permute-done.14 = bf16[32,1280]{1,0:T(8,128)(2,1)S(1)} collective-permute-done((bf16[32,1280]{1,0:T(8,128)(2,1)S(1)}, bf16[32,1280]{1,0:T(8,128)(2,1)S(1)}, u32[]{:S(2)}, u32[]{:S(2)}) %collective-permute-start.14) | collective-permute-done | bytes 81952 | tf_op jit(solution)/shard_map/ppermute | solution.py:397
  82.7 2.5 %collective-permute-start.15 = (bf16[32,1280]{1,0:T(8,128)(2,1)S(1)}, bf16[32,1280]{1,0:T(8,128)(2,1)S(1)}, u32[]{:S(2)}, u32[]{:S(2)}) collective-permute-start(bf16[32,1280]{1,0:T(8,128)(2,1)S(1)} %add_convert_fusion.16), channel_id=1, source_target_pairs={{0,16},{1,17},{2,18},{3,19},{4,20},{5,21},{6,22},{7,23},{8,24},{9,... | collective-permute-start | bytes 245768 | tf_op jit(solution)/shard_map/ppermute | solution.py:397
  85.2 1.6 %collective-permute-start.8 = (bf16[256,512]{1,0:T(8,128)(2,1)S(1)}, bf16[256,512]{1,0:T(8,128)(2,1)S(1)}, u32[]{:S(2)}, u32[]{:S(2)}) collective-permute-start(bf16[256,512]{1,0:T(8,128)(2,1)S(1)} %constant_dynamic-slice_fusion), channel_id=1, source_target_pairs={{0,4},{1,5},{2,6},{3,7},{4,0},{5,1},{6,2},{7,3},{8,12},{9,13},{10,... | collective-permute-start | bytes 786440 | tf_op jit(solution)/shard_map/ppermute | solution.py:397
  86.8 1.3 %collective-permute-done.15 = bf16[32,1280]{1,0:T(8,128)(2,1)S(1)} collective-permute-done((bf16[32,1280]{1,0:T(8,128)(2,1)S(1)}, bf16[32,1280]{1,0:T(8,128)(2,1)S(1)}, u32[]{:S(2)}, u32[]{:S(2)}) %collective-permute-start.15) | collective-permute-done | bytes 81952 | tf_op jit(solution)/shard_map/ppermute | solution.py:397
  88.1 2.1 %collective-permute-start.16 = (bf16[32,1280]{1,0:T(8,128)(2,1)S(1)}, bf16[32,1280]{1,0:T(8,128)(2,1)S(1)}, u32[]{:S(2)}, u32[]{:S(2)}) collective-permute-start(bf16[32,1280]{1,0:T(8,128)(2,1)S(1)} %add_convert_fusion.15), channel_id=1, source_target_pairs={{0,8},{1,9},{2,10},{3,11},{4,12},{5,13},{6,14},{7,15},{8,0},{9,1},... | collective-permute-start | bytes 245768 | tf_op jit(solution)/shard_map/ppermute | solution.py:397
  90.2 1.5 %collective-permute-done.8 = bf16[256,512]{1,0:T(8,128)(2,1)S(1)} collective-permute-done((bf16[256,512]{1,0:T(8,128)(2,1)S(1)}, bf16[256,512]{1,0:T(8,128)(2,1)S(1)}, u32[]{:S(2)}, u32[]{:S(2)}) %collective-permute-start.8) | collective-permute-done | bytes 262176 | tf_op jit(solution)/shard_map/ppermute | solution.py:397
  91.7 2.5 %collective-permute-start.9 = (bf16[128,512]{1,0:T(8,128)(2,1)S(1)}, bf16[128,512]{1,0:T(8,128)(2,1)S(1)}, u32[]{:S(2)}, u32[]{:S(2)}) collective-permute-start(bf16[128,512]{1,0:T(8,128)(2,1)S(1)} %add_convert_fusion.13), channel_id=1, source_target_pairs={{0,8},{1,9},{2,10},{3,11},{4,12},{5,13},{6,14},{7,15},{8,0},{9,1},... | collective-permute-start | bytes 393224 | tf_op jit(solution)/shard_map/ppermute | solution.py:397
  95.4 1.8 %collective-permute-done.9 = bf16[128,512]{1,0:T(8,128)(2,1)S(1)} collective-permute-done((bf16[128,512]{1,0:T(8,128)(2,1)S(1)}, bf16[128,512]{1,0:T(8,128)(2,1)S(1)}, u32[]{:S(2)}, u32[]{:S(2)}) %collective-permute-start.9) | collective-permute-done | bytes 131104 | tf_op jit(solution)/shard_map/ppermute | solution.py:397
  99.8 1.6 %collective-permute-start.18 = (bf16[128,1280]{1,0:T(8,128)(2,1)S(1)}, bf16[128,1280]{1,0:T(8,128)(2,1)S(1)}, u32[]{:S(2)}, u32[]{:S(2)}) collective-permute-start(bf16[128,1280]{1,0:T(8,128)(2,1)S(1)} %maximum_select_fusion.3), channel_id=1, source_target_pairs={{0,4},{1,5},{2,6},{3,7},{4,0},{5,1},{6,2},{7,3},{8,12},{9,13},{10,... | collective-permute-start | bytes 983048 | tf_op jit(solution)/shard_map/ppermute | solution.py:397
  102.0 1.3 %collective-permute-done.10 = bf16[128,512]{1,0:T(8,128)(2,1)S(1)} collective-permute-done((bf16[128,512]{1,0:T(8,128)(2,1)S(1)}, bf16[128,512]{1,0:T(8,128)(2,1)S(1)}, u32[]{:S(2)}, u32[]{:S(2)}) %collective-permute-start.10) | collective-permute-done | bytes 131104 | tf_op jit(solution)/shard_map/ppermute | solution.py:397
  103.4 2.1 %collective-permute-start.11 = (bf16[128,512]{1,0:T(8,128)(2,1)S(1)}, bf16[128,512]{1,0:T(8,128)(2,1)S(1)}, u32[]{:S(2)}, u32[]{:S(2)}) collective-permute-start(bf16[128,512]{1,0:T(8,128)(2,1)S(1)} %add_convert_fusion.11), channel_id=1, source_target_pairs={{0,8},{1,9},{2,10},{3,11},{4,12},{5,13},{6,14},{7,15},{8,0},{9,1},... | collective-permute-start | bytes 393224 | tf_op jit(solution)/shard_map/ppermute | solution.py:397
  105.5 1.4 %collective-permute-done.18 = bf16[128,1280]{1,0:T(8,128)(2,1)S(1)} collective-permute-done((bf16[128,1280]{1,0:T(8,128)(2,1)S(1)}, bf16[128,1280]{1,0:T(8,128)(2,1)S(1)}, u32[]{:S(2)}, u32[]{:S(2)}) %collective-permute-start.18) | collective-permute-done | bytes 327712 | tf_op jit(solution)/shard_map/ppermute | solution.py:397
  108.4 1.5 %collective-permute-start.25 = (bf16[256,512]{1,0:T(8,128)(2,1)S(1)}, bf16[256,512]{1,0:T(8,128)(2,1)S(1)}, u32[]{:S(2)}, u32[]{:S(2)}) collective-permute-start(bf16[256,512]{1,0:T(8,128)(2,1)S(1)} %maximum_select_fusion.5), channel_id=1, source_target_pairs={{0,8},{1,9},{2,10},{3,11},{4,12},{5,13},{6,14},{7,15},{8,0},{9,1},... | collective-permute-start | bytes 786440 | tf_op jit(solution)/shard_map/ppermute | solution.py:397
  111.1 1.4 %add_convert_fusion = bf16[1024,512]{1,0:T(8,128)(2,1)} fusion(bf16[1024,512]{1,0:T(8,128)(2,1)S(1)} %collective-permute-done.20, bf16[1024,512]{1,0:T(8,128)(2,1)S(1)} %copy-done.6, bf16[1024,512]{1,0:T(8,128)(2,1)S(1)} %copy-done.5, f32[512]{0:T(512)S(1)} %convert_element_type.227), kind=kLoop, calls=%fused_computation.4 | loop fusion | flops 3670016 | bytes 4196352 | tf_op jit(solution)/shard_map/convert_element_type | solution.py:621
  112.5 3.5 %collective-permute-done.25 = bf16[256,512]{1,0:T(8,128)(2,1)S(1)} collective-permute-done((bf16[256,512]{1,0:T(8,128)(2,1)S(1)}, bf16[256,512]{1,0:T(8,128)(2,1)S(1)}, u32[]{:S(2)}, u32[]{:S(2)}) %collective-permute-start.25) | collective-permute-done | bytes 262176 | tf_op jit(solution)/shard_map/ppermute | solution.py:397
  117.2 1.6 %unpack.1 = (f32[1,512]{1,0:T(1,128)}, f32[1,512]{1,0:T(1,128)}, f32[8,512]{1,0:T(8,128)}, f32[512,512]{1,0:T(8,128)}, f32[512,512]{1,0:T(8,128)}, /*index=5*/f3...) custom-call(s32[1]{0:T(128)} %bitcast.4.place, ...), custom_call_target="tpu_custom_call" | custom-call | flops 1000 | bytes 1000 | tf_op jit(solution)/shard_map/unpack/pallas_call | solution.py:384
  (71 shorter events, 19.1 us)
Async XLA Ops:
  2.6 13.5 %copy-start.4 = (bf16[1040,512]{1,0:T(8,128)(2,1)}, bf16[1040,512]{1,0:T(8,128)(2,1)S(1)}, u32[]{:S(2)}) copy-start(bf16[1040,512]{1,0:T(8,128)(2,1)S(1)} %fusion.3.refs_2_) | copy-start | bytes 3194884
  2.6 26.5 %collective-permute-start.2 = (bf16[1040,512]{1,0:T(8,128)(2,1)S(1)}, bf16[1040,512]{1,0:T(8,128)(2,1)S(1)}, u32[]{:S(2)}, u32[]{:S(2)}) collective-permute-start(bf16[1040,512]{1,0:T(8,128)(2,1)S(1)} %fusion.3.refs_2_), channel_id=1, source_target_pairs={{0,2},{1,3},{2,0},{3,1},{4,6},{5,7},{6,4},{7,5},{8,10},{9,11},{10,... | collective-permute-start | bytes 3194888 | tf_op jit(solution)/shard_map/ppermute | solution.py:397
  16.1 6.5 %collective-permute-start.1 = (bf16[1024,512]{1,0:T(8,128)(2,1)S(1)}, bf16[1024,512]{1,0:T(8,128)(2,1)S(1)}, u32[]{:S(2)}, u32[]{:S(2)}) collective-permute-start(bf16[1024,512]{1,0:T(8,128)(2,1)S(1)} %get-tuple-element.72.refs_1_.glow), channel_id=1, source_target_pairs={{0,1},{1,0},{2,3},{3,2},{4,5},{5,4},{6,7},{7,6},{8,9},{9,8},{10,11... | collective-permute-start | bytes 3145736 | tf_op jit(solution)/shard_map/ppermute | solution.py:397
  16.2 6.4 %collective-permute-start = (bf16[1024,512]{1,0:T(8,128)(2,1)S(1)}, bf16[1024,512]{1,0:T(8,128)(2,1)S(1)}, u32[]{:S(2)}, u32[]{:S(2)}) collective-permute-start(bf16[1024,512]{1,0:T(8,128)(2,1)S(1)} %get-tuple-element.71.refs_0_), channel_id=1, source_target_pairs={{0,1},{1,0},{2,3},{3,2},{4,5},{5,4},{6,7},{7,6},{8,9},{9,8},{10,11... | collective-permute-start | bytes 3145736 | tf_op jit(solution)/shard_map/ppermute | solution.py:397
  33.7 6.8 %copy-start.2 = (bf16[1024,512]{1,0:T(8,128)(2,1)}, bf16[1024,512]{1,0:T(8,128)(2,1)S(1)}, u32[]{:S(2)}) copy-start(bf16[1024,512]{1,0:T(8,128)(2,1)S(1)} %get-tuple-element.112) | copy-start | bytes 3145732
  33.7 8.6 %collective-permute-start.3 = (bf16[1024,512]{1,0:T(8,128)(2,1)}, bf16[1024,512]{1,0:T(8,128)(2,1)S(1)}, u32[]{:S(2)}, u32[]{:S(2)}) collective-permute-start(bf16[1024,512]{1,0:T(8,128)(2,1)} %get-tuple-element.85), channel_id=1, source_target_pairs={{0,1},{1,0},{2,3},{3,2},{4,5},{5,4},{6,7},{7,6},{8,9},{9,8},{10,11... | collective-permute-start | bytes 3145736 | tf_op jit(solution)/shard_map/ppermute | solution.py:397
  40.6 16.6 %collective-permute-start.4 = (bf16[512,512]{1,0:T(8,128)(2,1)}, bf16[512,512]{1,0:T(8,128)(2,1)}, u32[]{:S(2)}, u32[]{:S(2)}) collective-permute-start(bf16[512,512]{1,0:T(8,128)(2,1)} %get-tuple-element.96), channel_id=1, source_target_pairs={{0,2},{1,3},{2,0},{3,1},{4,6},{5,7},{6,4},{7,5},{8,10},{9,11},{10,... | collective-permute-start | bytes 1572872 | tf_op jit(solution)/shard_map/ppermute | solution.py:397
  57.1 4.4 %copy-start.1 = (bf16[256,1280]{1,0:T(8,128)(2,1)S(1)}, bf16[256,1280]{1,0:T(8,128)(2,1)}, u32[]{:S(2)}) copy-start(bf16[256,1280]{1,0:T(8,128)(2,1)} %copy-done) | copy-start | bytes 1966084
  57.1 4.4 %collective-permute-start.5 = (bf16[256,1280]{1,0:T(8,128)(2,1)}, bf16[256,1280]{1,0:T(8,128)(2,1)S(1)}, u32[]{:S(2)}, u32[]{:S(2)}) collective-permute-start(bf16[256,1280]{1,0:T(8,128)(2,1)} %get-tuple-element.97), channel_id=1, source_target_pairs={{0,1},{1,0},{2,3},{3,2},{4,5},{5,4},{6,7},{7,6},{8,9},{9,8},{10,11... | collective-permute-start | bytes 1966088 | tf_op jit(solution)/shard_map/ppermute | solution.py:397
  57.2 14.6 %collective-permute-start.7 = (bf16[512,512]{1,0:T(8,128)(2,1)}, bf16[512,512]{1,0:T(8,128)(2,1)}, u32[]{:S(2)}, u32[]{:S(2)}) collective-permute-start(bf16[512,512]{1,0:T(8,128)(2,1)} %get-tuple-element.98), channel_id=1, source_target_pairs={{0,2},{1,3},{2,0},{3,1},{4,6},{5,7},{6,4},{7,5},{8,10},{9,11},{10,... | collective-permute-start | bytes 1572872 | tf_op jit(solution)/shard_map/ppermute | solution.py:397
  59.7 8.7 %collective-permute-start.21 = (bf16[256,512]{1,0:T(8,128)(2,1)}, bf16[256,512]{1,0:T(8,128)(2,1)}, u32[]{:S(2)}, u32[]{:S(2)}) collective-permute-start(bf16[256,512]{1,0:T(8,128)(2,1)} %constant_dynamic-slice_fusion.1), channel_id=1, source_target_pairs={{0,8},{1,9},{2,10},{3,11},{4,12},{5,13},{6,14},{7,15},{8,0},{9,1},... | collective-permute-start | bytes 786440 | tf_op jit(solution)/shard_map/ppermute | solution.py:397
  61.7 18.2 %copy-start.7 = (bf16[512,512]{1,0:T(8,128)(2,1)S(1)}, bf16[512,512]{1,0:T(8,128)(2,1)}, u32[]{:S(2)}) copy-start(bf16[512,512]{1,0:T(8,128)(2,1)} %get-tuple-element.76) | copy-start | bytes 1572868
  61.7 10.1 %collective-permute-start.6 = (bf16[128,1280]{1,0:T(8,128)(2,1)S(1)}, bf16[128,1280]{1,0:T(8,128)(2,1)S(1)}, u32[]{:S(2)}, u32[]{:S(2)}) collective-permute-start(bf16[128,1280]{1,0:T(8,128)(2,1)S(1)} %get-tuple-element.129), channel_id=1, source_target_pairs={{0,4},{1,5},{2,6},{3,7},{4,0},{5,1},{6,2},{7,3},{8,12},{9,13},{10,... | collective-permute-start | bytes 983048 | tf_op jit(solution)/shard_map/ppermute | solution.py:397
  63.3 47.8 %collective-permute-start.20 = (bf16[1024,512]{1,0:T(8,128)(2,1)S(1)}, bf16[1024,512]{1,0:T(8,128)(2,1)S(1)}, u32[]{:S(2)}, u32[]{:S(2)}) collective-permute-start(bf16[1024,512]{1,0:T(8,128)(2,1)S(1)} %copy-done.3), channel_id=1, source_target_pairs={{0,1},{1,0},{2,3},{3,2},{4,5},{5,4},{6,7},{7,6},{8,9},{9,8},{10,11... | collective-permute-start | bytes 3145736 | tf_op jit(solution)/shard_map/ppermute | solution.py:397
  69.3 5.0 %collective-permute-start.22 = (bf16[128,512]{1,0:T(8,128)(2,1)S(1)}, bf16[128,512]{1,0:T(8,128)(2,1)S(1)}, u32[]{:S(2)}, u32[]{:S(2)}) collective-permute-start(bf16[128,512]{1,0:T(8,128)(2,1)S(1)} %add_convert_fusion.9), channel_id=1, source_target_pairs={{0,4},{1,5},{2,6},{3,7},{4,0},{5,1},{6,2},{7,3},{8,12},{9,13},{10,... | collective-permute-start | bytes 393224 | tf_op jit(solution)/shard_map/ppermute | solution.py:397
  71.9 6.3 %collective-permute-start.13 = (bf16[64,1280]{1,0:T(8,128)(2,1)S(1)}, bf16[64,1280]{1,0:T(8,128)(2,1)S(1)}, u32[]{:S(2)}, u32[]{:S(2)}) collective-permute-start(bf16[64,1280]{1,0:T(8,128)(2,1)S(1)} %get-tuple-element.131), channel_id=1, source_target_pairs={{0,2},{1,3},{2,0},{3,1},{4,6},{5,7},{6,4},{7,5},{8,10},{9,11},{10,... | collective-permute-start | bytes 491528 | tf_op jit(solution)/shard_map/ppermute | solution.py:397
  75.3 26.1 %collective-permute-start.23 = (bf16[128,512]{1,0:T(8,128)(2,1)S(1)}, bf16[128,512]{1,0:T(8,128)(2,1)S(1)}, u32[]{:S(2)}, u32[]{:S(2)}) collective-permute-start(bf16[128,512]{1,0:T(8,128)(2,1)S(1)} %add_convert_fusion.8), channel_id=1, source_target_pairs={{0,16},{1,17},{2,18},{3,19},{4,20},{5,21},{6,22},{7,23},{8,24},{9,... | collective-permute-start | bytes 393224 | tf_op jit(solution)/shard_map/ppermute | solution.py:397
  78.2 4.5 %collective-permute-start.14 = (bf16[32,1280]{1,0:T(8,128)(2,1)S(1)}, bf16[32,1280]{1,0:T(8,128)(2,1)S(1)}, u32[]{:S(2)}, u32[]{:S(2)}) collective-permute-start(bf16[32,1280]{1,0:T(8,128)(2,1)S(1)} %add_convert_fusion.17), channel_id=1, source_target_pairs={{0,8},{1,9},{2,10},{3,11},{4,12},{5,13},{6,14},{7,15},{8,0},{9,1},... | collective-permute-start | bytes 245768 | tf_op jit(solution)/shard_map/ppermute | solution.py:397
  82.7 5.4 %collective-permute-start.15 = (bf16[32,1280]{1,0:T(8,128)(2,1)S(1)}, bf16[32,1280]{1,0:T(8,128)(2,1)S(1)}, u32[]{:S(2)}, u32[]{:S(2)}) collective-permute-start(bf16[32,1280]{1,0:T(8,128)(2,1)S(1)} %add_convert_fusion.16), channel_id=1, source_target_pairs={{0,16},{1,17},{2,18},{3,19},{4,20},{5,21},{6,22},{7,23},{8,24},{9,... | collective-permute-start | bytes 245768 | tf_op jit(solution)/shard_map/ppermute | solution.py:397
  85.2 6.4 %collective-permute-start.8 = (bf16[256,512]{1,0:T(8,128)(2,1)S(1)}, bf16[256,512]{1,0:T(8,128)(2,1)S(1)}, u32[]{:S(2)}, u32[]{:S(2)}) collective-permute-start(bf16[256,512]{1,0:T(8,128)(2,1)S(1)} %constant_dynamic-slice_fusion), channel_id=1, source_target_pairs={{0,4},{1,5},{2,6},{3,7},{4,0},{5,1},{6,2},{7,3},{8,12},{9,13},{10,... | collective-permute-start | bytes 786440 | tf_op jit(solution)/shard_map/ppermute | solution.py:397
  88.1 6.1 %collective-permute-start.16 = (bf16[32,1280]{1,0:T(8,128)(2,1)S(1)}, bf16[32,1280]{1,0:T(8,128)(2,1)S(1)}, u32[]{:S(2)}, u32[]{:S(2)}) collective-permute-start(bf16[32,1280]{1,0:T(8,128)(2,1)S(1)} %add_convert_fusion.15), channel_id=1, source_target_pairs={{0,8},{1,9},{2,10},{3,11},{4,12},{5,13},{6,14},{7,15},{8,0},{9,1},... | collective-permute-start | bytes 245768 | tf_op jit(solution)/shard_map/ppermute | solution.py:397
  91.7 5.5 %collective-permute-start.9 = (bf16[128,512]{1,0:T(8,128)(2,1)S(1)}, bf16[128,512]{1,0:T(8,128)(2,1)S(1)}, u32[]{:S(2)}, u32[]{:S(2)}) collective-permute-start(bf16[128,512]{1,0:T(8,128)(2,1)S(1)} %add_convert_fusion.13), channel_id=1, source_target_pairs={{0,8},{1,9},{2,10},{3,11},{4,12},{5,13},{6,14},{7,15},{8,0},{9,1},... | collective-permute-start | bytes 393224 | tf_op jit(solution)/shard_map/ppermute | solution.py:397
  94.3 5.4 %collective-permute-start.17 = (bf16[64,1280]{1,0:T(8,128)(2,1)S(1)}, bf16[64,1280]{1,0:T(8,128)(2,1)S(1)}, u32[]{:S(2)}, u32[]{:S(2)}) collective-permute-start(bf16[64,1280]{1,0:T(8,128)(2,1)S(1)} %maximum_select_fusion.6), channel_id=1, source_target_pairs={{0,2},{1,3},{2,0},{3,1},{4,6},{5,7},{6,4},{7,5},{8,10},{9,11},{10,... | collective-permute-start | bytes 491528 | tf_op jit(solution)/shard_map/ppermute | solution.py:397
  97.3 6.0 %collective-permute-start.10 = (bf16[128,512]{1,0:T(8,128)(2,1)S(1)}, bf16[128,512]{1,0:T(8,128)(2,1)S(1)}, u32[]{:S(2)}, u32[]{:S(2)}) collective-permute-start(bf16[128,512]{1,0:T(8,128)(2,1)S(1)} %add_convert_fusion.12), channel_id=1, source_target_pairs={{0,16},{1,17},{2,18},{3,19},{4,20},{5,21},{6,22},{7,23},{8,24},{9,... | collective-permute-start | bytes 393224 | tf_op jit(solution)/shard_map/ppermute | solution.py:397
  99.8 11.3 %copy-start.5 = (bf16[1024,512]{1,0:T(8,128)(2,1)S(1)}, bf16[1024,512]{1,0:T(8,128)(2,1)}, u32[]{:S(2)}) copy-start(bf16[1024,512]{1,0:T(8,128)(2,1)} %get-tuple-element.88.res) | copy-start | bytes 3145732
  99.8 11.3 %copy-start.6 = (bf16[1024,512]{1,0:T(8,128)(2,1)S(1)}, bf16[1024,512]{1,0:T(8,128)(2,1)}, u32[]{:S(2)}) copy-start(bf16[1024,512]{1,0:T(8,128)(2,1)} %get-tuple-element.111) | copy-start | bytes 3145732
  99.8 7.1 %collective-permute-start.18 = (bf16[128,1280]{1,0:T(8,128)(2,1)S(1)}, bf16[128,1280]{1,0:T(8,128)(2,1)S(1)}, u32[]{:S(2)}, u32[]{:S(2)}) collective-permute-start(bf16[128,1280]{1,0:T(8,128)(2,1)S(1)} %maximum_select_fusion.3), channel_id=1, source_target_pairs={{0,4},{1,5},{2,6},{3,7},{4,0},{5,1},{6,2},{7,3},{8,12},{9,13},{10,... | collective-permute-start | bytes 983048 | tf_op jit(solution)/shard_map/ppermute | solution.py:397
  101.4 6.9 %collective-permute-start.24 = (bf16[128,512]{1,0:T(8,128)(2,1)S(1)}, bf16[128,512]{1,0:T(8,128)(2,1)S(1)}, u32[]{:S(2)}, u32[]{:S(2)}) collective-permute-start(bf16[128,512]{1,0:T(8,128)(2,1)S(1)} %add_convert_fusion.7), channel_id=1, source_target_pairs={{0,4},{1,5},{2,6},{3,7},{4,0},{5,1},{6,2},{7,3},{8,12},{9,13},{10,... | collective-permute-start | bytes 393224 | tf_op jit(solution)/shard_map/ppermute | solution.py:397
  103.4 6.6 %collective-permute-start.11 = (bf16[128,512]{1,0:T(8,128)(2,1)S(1)}, bf16[128,512]{1,0:T(8,128)(2,1)S(1)}, u32[]{:S(2)}, u32[]{:S(2)}) collective-permute-start(bf16[128,512]{1,0:T(8,128)(2,1)S(1)} %add_convert_fusion.11), channel_id=1, source_target_pairs={{0,8},{1,9},{2,10},{3,11},{4,12},{5,13},{6,14},{7,15},{8,0},{9,1},... | collective-permute-start | bytes 393224 | tf_op jit(solution)/shard_map/ppermute | solution.py:397
  107.1 10.1 %collective-permute-start.19 = (bf16[256,1280]{1,0:T(8,128)(2,1)S(1)}, bf16[256,1280]{1,0:T(8,128)(2,1)S(1)}, u32[]{:S(2)}, u32[]{:S(2)}) collective-permute-start(bf16[256,1280]{1,0:T(8,128)(2,1)S(1)} %maximum_select_fusion.mine), channel_id=1, source_target_pairs={{0,1},{1,0},{2,3},{3,2},{4,5},{5,4},{6,7},{7,6},{8,9},{9,8},{10,11... | collective-permute-start | bytes 1966088 | tf_op jit(solution)/shard_map/ppermute | solution.py:397
  108.4 7.6 %collective-permute-start.25 = (bf16[256,512]{1,0:T(8,128)(2,1)S(1)}, bf16[256,512]{1,0:T(8,128)(2,1)S(1)}, u32[]{:S(2)}, u32[]{:S(2)}) collective-permute-start(bf16[256,512]{1,0:T(8,128)(2,1)S(1)} %maximum_select_fusion.5), channel_id=1, source_target_pairs={{0,8},{1,9},{2,10},{3,11},{4,12},{5,13},{6,14},{7,15},{8,0},{9,1},... | collective-permute-start | bytes 786440 | tf_op jit(solution)/shard_map/ppermute | solution.py:397
  110.0 8.8 %collective-permute-start.12 = (bf16[256,512]{1,0:T(8,128)(2,1)S(1)}, bf16[256,512]{1,0:T(8,128)(2,1)S(1)}, u32[]{:S(2)}, u32[]{:S(2)}) collective-permute-start(bf16[256,512]{1,0:T(8,128)(2,1)S(1)} %maximum_select_fusion.4), channel_id=1, source_target_pairs={{0,4},{1,5},{2,6},{3,7},{4,0},{5,1},{6,2},{7,3},{8,12},{9,13},{10,... | collective-permute-start | bytes 786440 | tf_op jit(solution)/shard_map/ppermute | solution.py:397
  (3 other events, 9.5 us)
